TPU v7x, 256 devices: a whole 4x4x8 slice. The times are simulated.
256 devices in a mesh: inst: 32 (over x, z_hi, core), head: 8 (over z_lo, y).
Axes of the slice: x: 4, y: 4, z: 8 (z_hi: 4, z_lo: 2; z = z_hi * 2 + z_lo), core: 2. Of those that a mesh axis runs over, the one named last changes fastest.
Arguments:
- latent_cache: bfloat16 [256, 1024, 576], P('inst', 'head'), may hold values from -6 to 6
- cache_lengths: int32 [256], P('inst'), may hold values from 1 to 1024, as said below
- partner: int32 [32], replicated, may hold values from 0 to 31, as said below
- queries: bfloat16 [4, 256, 128, 576], P(None, 'inst', 'head'), may hold values from -240 to 240
- step_rows: bfloat16 [4, 256, 576], P(None, 'inst'), may hold values from -6 to 6
- arrivals: bfloat16 [65536, 576], P(('inst', 'head')), may hold values from -6 to 6
- arrival_routes: int32 [65536, 1], P(('inst', 'head')), may hold values from 0 to 31; in each aligned block of 256 rows (0 to 255, 256 to 511, ...) at most 16 rows name the same one
- arrival_owners: int32 [65536], P(('inst', 'head')), may hold values from 0 to 3
- new_queries: bfloat16 [4, 128, 128, 576], P(None, 'inst', 'head'), may hold values from -240 to 240
- new_step_rows: bfloat16 [4, 128, 576], P(None, 'inst'), may hold values from -6 to 6
- value_up: bfloat16 [128, 512, 128], P('head'), may hold values from -0.25 to 0.25
Outputs:
- resident_out: bfloat16 [4, 256, 16384], P(None, 'inst', 'head')
- arrival_out: bfloat16 [4, 128, 16384], P(None, 'inst', 'head')
Inputs may be any that keep to these rules, and one draw needn't show every extreme that they name: `cache_lengths`: every resident request has 1 to 1024 valid positions; some has exactly 1024, some exactly 1. partner is a perfect matching: partner[partner[i]] = i and partner[i] != i. `arrival_routes`: among the rows of one device, no instance is named by more than 16 rows.
All inputs are finite; a program needn't handle non-finite values.
Results may differ from a plain program's by a relative error of at most 0.012.
Values may be sent and summed in bfloat16 or wider, within the bound.
No kernel may reach another device: no remote copies, remote signals or barrier semaphores. Data moves between devices by JAX's collectives and lax.ppermute only.
A program may use at most 128 MiB of HBM per device.

v0:
```python
import jax
import jax.numpy as jnp
from jax import lax
from jax.sharding import PartitionSpec as P

LATENT_WIDTH = 512
KR = 64
VD = 128
MIG = 1
KD = 576


def weights_from(first, first_keep, second, second_keep):
    first = jnp.where(first_keep, first, -1e30)
    second = jnp.where(second_keep, second, -1e30)
    peak = jnp.maximum(jnp.max(first, -1, keepdims=True), jnp.max(second, -1, keepdims=True))
    first_w = jnp.where(first_keep, jnp.exp(first - peak), 0.0)
    second_w = jnp.where(second_keep, jnp.exp(second - peak), 0.0)
    total = jnp.sum(first_w, -1, keepdims=True) + jnp.sum(second_w, -1, keepdims=True)
    return (first_w.astype(jnp.bfloat16), second_w.astype(jnp.bfloat16), total)


def finish(latent_rows, value_up, steps, count, heads):
    latent_rows = latent_rows.reshape(count, steps, heads, LATENT_WIDTH)
    out = jnp.einsum("rshc,hcv->srhv", latent_rows, value_up, preferred_element_type=jnp.float32)
    return out.astype(jnp.bfloat16).reshape(steps, count, heads * VD)


def tail_mask(steps, heads):
    query_step = jnp.arange(steps * heads) // heads
    return jnp.arange(steps)[None, None, :] <= query_step[None, :, None]


def bucket(rows, target, owner, destinations, capacity):
    onehot = (target[:, None] == jnp.arange(destinations, dtype=jnp.int32)[None, :]).astype(
        jnp.int32
    )
    ranking = jnp.sum(jnp.cumsum(onehot, 0) * onehot, 1) - 1
    packed = (
        jnp.zeros((destinations, capacity, rows.shape[1]), rows.dtype).at[target, ranking].set(rows)
    )
    labels = jnp.full((destinations, capacity), -1, jnp.int32).at[target, ranking].set(owner)
    return (packed, labels)


def partner_picker(target_inst, dim, carry, piece):
    result = []
    for total, block in zip(carry, piece):
        moved = jnp.moveaxis(block, dim, 0)
        blocks = moved.shape[0] // MIG
        source = jnp.arange(blocks)
        shaped = moved.reshape((blocks, MIG) + moved.shape[1:])
        matched = (source == target_inst).reshape((blocks,) + (1,) * (shaped.ndim - 1))
        chosen = jnp.sum(jnp.where(matched, shaped, jnp.zeros_like(shaped)), 0)
        result.append(jnp.moveaxis(chosen, 0, dim).astype(total.dtype))
    return tuple(result)


def attend_resident(complete_cache, lens_now, queries, step_rows, value_up):
    score_scale = (VD + KR) ** (-0.5)
    steps, count, heads = (queries.shape[0], queries.shape[1], queries.shape[2])
    query_tile = jnp.transpose(queries, (1, 0, 2, 3)).reshape(count, steps * heads, KD)
    trailing_keys = jnp.transpose(step_rows, (1, 0, 2))
    primary_part = (
        jnp.einsum("ano,amo->anm", query_tile, complete_cache, preferred_element_type=jnp.float32)
        * score_scale
    )
    tail_part = (
        jnp.einsum("ano,amo->anm", query_tile, trailing_keys, preferred_element_type=jnp.float32)
        * score_scale
    )
    keep_main = jnp.arange(complete_cache.shape[1])[None, None, :] < lens_now[:, None, None]
    primary_weights, tail_weights, total = weights_from(
        primary_part, keep_main, tail_part, tail_mask(steps, heads)
    )
    latent_rows = jnp.einsum(
        "wax,wxe->wae",
        primary_weights,
        complete_cache[..., :LATENT_WIDTH],
        preferred_element_type=jnp.float32,
    )
    latent_rows = latent_rows + jnp.einsum(
        "wax,wxe->wae",
        tail_weights,
        trailing_keys[..., :LATENT_WIDTH],
        preferred_element_type=jnp.float32,
    )
    latent_rows = (latent_rows / total).astype(jnp.bfloat16)
    return finish(latent_rows, value_up, steps, count, heads)


def local(
    latent_cache,
    cache_lengths,
    partner,
    queries,
    step_rows,
    arrivals,
    arrival_routes,
    arrival_owners,
    new_queries,
    new_step_rows,
    value_up,
):
    n_inst = lax.axis_size("inst")
    n_head = lax.axis_size("head")
    target_inst = partner[lax.axis_index("inst")]
    score_scale = (VD + KR) ** (-0.5)
    steps, heads = (queries.shape[0], queries.shape[2])
    start_carry = (jnp.zeros_like(latent_cache[:MIG]), jnp.zeros((MIG,), jnp.int32))
    moved_rows, moved_lens = partner_picker(
        target_inst,
        0,
        start_carry,
        (
            lax.all_gather(latent_cache[:MIG], "inst", axis=0, tiled=True),
            lax.all_gather(cache_lengths[:MIG], "inst", axis=0, tiled=True),
        ),
    )
    local_cache = jnp.concatenate([moved_rows, latent_cache[MIG:]], 0)
    lens_now = jnp.concatenate([moved_lens, cache_lengths[MIG:]], 0)
    complete_cache = lax.all_gather(local_cache, "head", axis=1, tiled=True)
    local_out = attend_resident(complete_cache, lens_now, queries, step_rows, value_up)
    capacity = 2 * arrivals.shape[0] // n_inst
    group_rows, group_routes, group_owners = (
        lax.all_gather(arrivals, "head", axis=0, tiled=True),
        lax.all_gather(arrival_routes, "head", axis=0, tiled=True),
        lax.all_gather(arrival_owners, "head", axis=0, tiled=True),
    )
    packed, labels = bucket(group_rows, group_routes[:, 0], group_owners, n_inst, capacity * n_head)
    landed_rows, landed_labels = (
        lax.all_to_all(packed, "inst", split_axis=0, concat_axis=0, tiled=True),
        lax.all_to_all(labels, "inst", split_axis=0, concat_axis=0, tiled=True),
    )
    slot_row_index = landed_rows.reshape(-1, KD)
    slot_owner = landed_labels.reshape(-1)
    new_count = new_queries.shape[1]
    fresh_block = jnp.transpose(new_queries, (1, 0, 2, 3)).reshape(new_count, steps * heads, KD)
    fresh_tail = jnp.transpose(new_step_rows, (1, 0, 2))
    arrived_main = (
        jnp.einsum("uzf,yf->uzy", fresh_block, slot_row_index, preferred_element_type=jnp.float32)
        * score_scale
    )
    arrived_tail = (
        jnp.einsum("ano,amo->anm", fresh_block, fresh_tail, preferred_element_type=jnp.float32)
        * score_scale
    )
    keep_arrived = (
        slot_owner[None, None, :] == jnp.arange(new_count, dtype=jnp.int32)[:, None, None]
    )
    arrival_weights, fresh_tail_weights, arrived_total = weights_from(
        arrived_main, keep_arrived, arrived_tail, tail_mask(steps, heads)
    )
    new_latent = jnp.einsum(
        "nmt,tw->nmw",
        arrival_weights,
        slot_row_index[:, :LATENT_WIDTH],
        preferred_element_type=jnp.float32,
    )
    new_latent = new_latent + jnp.einsum(
        "wax,wxe->wae",
        fresh_tail_weights,
        fresh_tail[..., :LATENT_WIDTH],
        preferred_element_type=jnp.float32,
    )
    new_latent = (new_latent / arrived_total).astype(jnp.bfloat16)
    arrival_out = finish(new_latent, value_up, steps, new_count, heads)
    return (local_out, arrival_out)


def solution(mesh):
    in_specs = (
        P("inst", "head", None),
        P("inst"),
        P(),
        P(None, "inst", "head", None),
        P(None, "inst", None),
        P(("inst", "head"), None),
        P(("inst", "head"), None),
        P(("inst", "head")),
        P(None, "inst", "head", None),
        P(None, "inst", None),
        P("head", None, None),
    )
    out_specs = (P(None, "inst", "head"), P(None, "inst", "head"))
    return jax.shard_map(local, mesh=mesh, in_specs=in_specs, out_specs=out_specs, check_vma=False)
```

profile of v0, /device:TPU:6, one launch (start us, length us, event | category | flops | bytes accessed | tf_op | source)
XLA Modules:
  0.0 386.1 jit_solution(909926072881002720)
XLA Ops:
  7.2 1.7 slice.32
  9.1 0.7 all-gather.9.cloned.1.call-update
  9.8 1.2 dynamic_slice.3
  11.0 0.6 iota_compare_fusion.5
  11.7 64.3 %all-gather.5.cloned.1.call-done = bf16[32,128,576]{1,2,0:T(8,128)(2,1)} async-done(((bf16[1,128,576]{1,2,0:T(8,128)(2,1)}), bf16[32,128,576]{1,2,0:T(8,128)(2,1)}) %all-gather.5.cloned.1.call-update) | async-done | bytes 4718608 | tf_op jit(solution)/shard_map/all_gather | solution.py:116
  76.0 3.5 select_reduce_fusion
  79.5 1.1 pad_maximum_fusion
  80.7 16.7 %all_gather.21 = s32[2048,1]{0,1:T(1,128)S(1)} all-gather(s32[256,1]{0,1:T(1,128)S(1)} %copy-done.5), channel_id=1, replica_groups=mesh['inst'=32,'head'=8] {'head'}, dimensions={0}, use_global_device_ids=true | all-gather | bytes 9216 | tf_op jit(solution)/shard_map/all_gather | solution.py:127
  97.4 9.1 %reduce-window.6 = s32[32,16,128]{2,1,0:T(8,128)S(1)} reduce-window(s32[32,16,128]{2,1,0:T(8,128)S(1)} %fusion.50, s32[]{:T(128)} %constant.24.clone.1), window={size=1x1x128 pad=0_0x0_0x127_0}, to_apply=%region_6.7 | reduce-window | flops 8323072 | bytes 524292 | tf_op jit(solution)/shard_map/reduce-window
  106.5 0.1 slice.42
  106.6 0.2 copy.51
  106.9 0.2 reduce-window.9
  107.0 15.5 %all-gather = s32[8,1,256]{2,1,0:T(1,128)S(1)} all-gather(s32[1,1,256]{2,1,0:T(1,128)S(1)} %bitcast.125), channel_id=1, replica_groups=mesh['inst'=32,'head'=8] {'head'}, dimensions={0}, use_global_device_ids=true | all-gather | bytes 9216 | tf_op jit(solution)/shard_map/all_gather | solution.py:128
  122.6 0.1 broadcast_add_fusion
  122.7 0.1 fusion.48
  122.9 0.1 multiply_reduce_fusion
  123.0 0.1 and_reduce_fusion
  123.1 8.6 %scatter_custom_fusion = s32[4096]{0:T(1024)} fusion(s32[2048]{0:T(1024)S(1)} %broadcast_select_fusion, s32[2048]{0:T(1024)S(1)} %bitcast.124, s32[]{:T(128)} %constant.54.clone.1), kind=kCustom, calls=%fused_computation.75 | custom fusion | bytes 16388
  131.7 7.7 %all-to-all-start = ((s32[32,1,128]{2,1,0:T(1,128)}), s32[32,1,128]{2,1,0:T(1,128)S(1)}, u32[]{:S(2)}, u32[]{:S(2)}) async-start(s32[32,1,128]{2,1,0:T(1,128)} %bitcast.22), calls=%async_computation | async-start | bytes 32768 | tf_op jit(solution)/shard_map/all_to_all | solution.py:133
  139.5 4.4 %copy.40 = bf16[2048,576]{1,0:T(8,128)(2,1)} copy(bf16[2048,576]{0,1:T(8,128)(2,1)} %all-gather.9.cloned.1.call-done) | data formatting | bytes 4718592 | tf_op jit(solution)/shard_map/all_gather | solution.py:126
  143.9 13.4 %scatter_custom_fusion.1 = bf16[4096,576]{1,0:T(8,128)(2,1)} fusion(s32[2048]{0:T(1024)S(1)} %broadcast_select_fusion, bf16[2048,576]{1,0:T(8,128)(2,1)} %copy.40, bf16[]{:T(256)} %constant.47.clone.1), kind=kCustom, calls=%fused_computation.14 | custom fusion | bytes 4719104
  157.3 7.7 %copy.41 = bf16[32,128,576]{1,2,0:T(8,128)(2,1)} copy(bf16[32,128,576]{2,1,0:T(8,128)(2,1)} %bitcast.106) | data formatting | bytes 9437184 | tf_op jit(solution)/shard_map/scatter | solution.py:40
  165.0 10.0 %all-to-all-start.1 = ((bf16[32,128,576]{1,2,0:T(8,128)(2,1)}), bf16[32,128,576]{1,2,0:T(8,128)(2,1)}, u32[]{:S(2)}, u32[]{:S(2)}) async-start(bf16[32,128,576]{1,2,0:T(8,128)(2,1)} %copy.41), calls=%async_computation.1 | async-start | bytes 9437184 | tf_op jit(solution)/shard_map/all_to_all | solution.py:132
  175.0 0.1 slice.31
  175.1 1.2 copy.33
  176.3 0.6 dynamic-slice
  176.9 0.7 slice_dynamic-update-slice_fusion
  177.7 160.9 %all-reduce = s32[32]{0:T(128)S(1)} all-reduce(s32[32]{0:T(128)S(1)} %slice_dynamic-update-slice_fusion), channel_id=1, replica_groups=mesh['inst'=32,'head'=8] {'inst'}, use_global_device_ids=true, to_apply=%add | all-reduce | flops 32 | bytes 256
  338.6 1.3 select_reduce_fusion.1
  339.9 0.7 pad_add_fusion.1
  340.6 0.1 iota_compare_fusion.3
  340.7 0.2 fusion.75
  340.9 0.3 fusion.73
  341.3 7.5 %copy.42 = bf16[32,128,576]{1,0,2:T(8,128)(2,1)} copy(bf16[32,128,576]{1,2,0:T(8,128)(2,1)} %all-to-all-done.1) | data formatting | bytes 9437184 | tf_op jit(solution)/shard_map/all_to_all | solution.py:132
  348.8 8.2 %reshape.220 = bf16[4096,576,1]{0,1,2:T(8,128)(2,1)} reshape(bf16[32,128,576]{1,0,2:T(8,128)(2,1)} %copy.42) | data formatting | bytes 9437184 | tf_op jit(solution)/shard_map/reshape | solution.py:135
  357.0 4.6 %fusion.74 = (f32[4,64]{1,0:T(4,128)S(1)}, f32[4,64,4096]{2,1,0:T(8,128)S(1)}) fusion(bf16[4096,576,1]{0,1,2:T(8,128)(2,1)} %reshape.220, bf16[4,64,576]{2,1,0:T(8,128)(2,1)S(1)} %bitcast.110, pred[4,4096]{1,0:T(4,128)(4,1)S(1)} %iota_compare_fusion.2), kind=kOutput, calls=%fused_computation.105 | convolution fusion | flops 1211105024 | bytes 9225216 | tf_op jit(solution)/shard_map/uzf,yf->uzy/dot_general | solution.py:141
  361.6 1.0 fusion.5
  362.6 3.0 copy_bitcast_fusion
  365.7 1.3 fusion.4
  367.0 0.3 fusion.24
  367.3 0.5 fusion.34
  367.8 0.6 reshape.190
  368.5 5.8 %bitcast_reduce_fusion = (f32[8,64]{1,0:T(8,128)S(1)}, f32[8,1024,64]{1,2,0:T(8,128)S(1)}) fusion(pred[8,1024]{1,0:T(8,128)(4,1)S(1)} %iota_compare_fusion.3, bf16[8,64,576]{2,1,0:T(8,128)(2,1)S(1)} %bitcast.108, bf16[8,1024,576]{1,2,0:T(8,128)(2,1)} %all-gather.7.cloned.1.call-done), kind=kOutput, calls=%fused_computation.21 | convolution fusion | flops 605552128 | bytes 12134400 | tf_op jit(solution)/shard_map/ano,amo->anm/dot_general | solution.py:65
  374.3 0.7 fusion.19
  375.1 2.9 fusion
  378.0 0.4 fusion.22
  378.3 0.5 fusion.28
  378.9 0.7 copy.71
  (51 shorter events, 0.5 us)
Async XLA Ops:
  7.2 360.1 %copy-start = (bf16[16,512,128]{2,1,0:T(8,128)(2,1)S(1)}, bf16[16,512,128]{2,1,0:T(8,128)(2,1)}, u32[]{:S(2)}) copy-start(bf16[16,512,128]{2,1,0:T(8,128)(2,1)} %param.21) | copy-start | bytes 6291460
  7.2 72.3 %slice-start = ((bf16[8,128,576]{1,2,0:T(8,128)(2,1)}), bf16[7,128,576]{1,2,0:T(8,128)(2,1)S(1)}, s32[]{:S(2)}) async-start(bf16[8,128,576]{1,2,0:T(8,128)(2,1)} %param.11), calls=%async_computation.5 | async-start | bytes 2064384 | tf_op jit(solution)/shard_map/slice | solution.py:120
  7.2 68.8 %all-gather.5.cloned.1.call-start = ((), (), s32[]{:S(2)}) async-start(), calls=%async_computation.2 | async-start | bytes 4866048 | tf_op jit(solution)/shard_map/all_gather | solution.py:116
  9.0 130.5 %all-gather.9.cloned.1.call-start = ((), (), s32[]{:S(2)}) async-start(), calls=%async_computation.4 | async-start | bytes 2654208 | tf_op jit(solution)/shard_map/all_gather | solution.py:126
  9.8 358.7 %all-gather.7.cloned.1.call-start = ((), (), s32[]{:S(2)}) async-start(), calls=%async_computation.3 | async-start | bytes 10616832 | tf_op jit(solution)/shard_map/all_gather | solution.py:122
  11.7 69.0 %copy-start.5 = (s32[256,1]{0,1:T(1,128)S(1)}, s32[256,1]{0,1:T(1,128)}, u32[]{:S(2)}) copy-start(s32[256,1]{0,1:T(1,128)} %param.17) | copy-start | bytes 3076
  11.7 95.3 %copy-start.6 = (s32[256]{0:T(256)S(1)}, s32[256]{0:T(256)}, u32[]{:S(2)}) copy-start(s32[256]{0:T(256)} %param.18) | copy-start | bytes 3076
  79.5 43.4 %copy-start.8 = (s32[2]{0:T(128)S(1)}, s32[2]{0:T(128)}, u32[]{:S(2)}) copy-start(s32[2]{0:T(128)} %constant.63) | copy-start | bytes 28
  79.5 43.5 %copy-start.7 = (s32[2]{0:T(128)S(1)}, s32[2]{0:T(128)}, u32[]{:S(2)}) copy-start(s32[2]{0:T(128)} %constant.66) | copy-start | bytes 28
  131.7 33.2 %all-to-all-start = ((s32[32,1,128]{2,1,0:T(1,128)}), s32[32,1,128]{2,1,0:T(1,128)S(1)}, u32[]{:S(2)}, u32[]{:S(2)}) async-start(s32[32,1,128]{2,1,0:T(1,128)} %bitcast.22), calls=%async_computation | async-start | bytes 32768 | tf_op jit(solution)/shard_map/all_to_all | solution.py:133
  164.9 10.0 %copy-start.2 = (bf16[4,4,16,576]{3,2,1,0:T(8,128)(2,1)S(1)}, bf16[4,4,16,576]{3,2,1,0:T(8,128)(2,1)}, u32[]{:S(2)}) copy-start(bf16[4,4,16,576]{3,2,1,0:T(8,128)(2,1)} %param.19) | copy-start | bytes 884740
  164.9 10.1 %copy-start.3 = (bf16[4,4,576]{2,1,0:T(4,128)(2,1)S(1)}, bf16[4,4,576]{2,1,0:T(4,128)(2,1)}, u32[]{:S(2)}) copy-start(bf16[4,4,576]{2,1,0:T(4,128)(2,1)} %param.20) | copy-start | bytes 55300
  164.9 10.1 %copy-start.9 = (s32[8]{0:T(128)S(1)}, s32[8]{0:T(128)}, u32[]{:S(2)}) copy-start(s32[8]{0:T(128)} %param.12) | copy-start | bytes 100
  164.9 11.4 %copy-start.4 = (bf16[4,8,576]{2,1,0:T(8,128)(2,1)S(1)}, bf16[4,8,576]{2,1,0:T(8,128)(2,1)}, u32[]{:S(2)}) copy-start(bf16[4,8,576]{2,1,0:T(8,128)(2,1)} %param.15) | copy-start | bytes 110596
  164.9 11.4 %copy-start.10 = (u32[256]{0:T(256)S(1)}, u32[256]{0:T(256)}, u32[]{:S(2)}) copy-start(u32[256]{0:T(256)} %constant.80) | copy-start | bytes 3076
  165.0 176.3 %all-to-all-start.1 = ((bf16[32,128,576]{1,2,0:T(8,128)(2,1)}), bf16[32,128,576]{1,2,0:T(8,128)(2,1)}, u32[]{:S(2)}, u32[]{:S(2)}) async-start(bf16[32,128,576]{1,2,0:T(8,128)(2,1)} %copy.41), calls=%async_computation.1 | async-start | bytes 9437184 | tf_op jit(solution)/shard_map/all_to_all | solution.py:132
  368.5 6.6 %copy-start.1 = (bf16[8,1024,576]{1,2,0:T(8,128)(2,1)S(1)}, bf16[8,1024,576]{1,2,0:T(8,128)(2,1)}, u32[]{:S(2)}) copy-start(bf16[8,1024,576]{1,2,0:T(8,128)(2,1)} %all-gather.7.cloned.1.call-done) | copy-start | bytes 28311556
Sparse Core Ops, SparseCore 0:
  10.6 65.3 all-gather.4
  77.7 46.9 all-gather.8
  126.4 210.4 all-gather.6
where the time goes:
time: 390 us; the launch traced here: 386 us
  blocking collectives  193 us (49%)
  waiting for transfers between devices  65 us (17%)
  local copies, waits for them, and re-layouts  60.2 us (15%)
  other arithmetic  19 us (5%)
  starting transfers between devices  17.8 us (5%)
  matrix products  16.8 us (4%)
  between operations  14.2 us (4%)
    unnamed x1, blocking collectives  161 us
    all_gather x1, waiting for transfers between devices, local(): lax.all_gather(latent_cache[:MIG], 'inst', axis=0, tiled=True)  64.3 us
    unnamed x31, local copies, waits for them, and re-layouts  24.6 us
    all_gather x1, blocking collectives, local(): lax.all_gather(arrival_routes, 'head', axis=0, tiled=True)  16.7 us
    all_gather x1, blocking collectives, local(): lax.all_gather(arrival_owners, 'head', axis=0, tiled=True)  15.5 us
    reshape x2, local copies, waits for them, and re-layouts, local(): slot_row_index = landed_rows.reshape(-1, KD)  11.2 us
    all_to_all x1, starting transfers between devices, local(): lax.all_to_all(packed, 'inst', split_axis=0, concat_axis=0, tiled=True)  9.97 us
    another operation x3, other arithmetic  9.4 us
  transfers between devices with their start and end apart: 5, of which 1 were waited for; matrix products, arithmetic and copies ran while one was open for 22% of the time, Pallas kernels for 0%

commit v1 on v0

v1 whole, which is shorter than its diff:
```python
import jax
import jax.numpy as jnp
from jax import lax
from jax.experimental import pallas as pl
from jax.experimental.pallas import tpu as pltpu
from jax.sharding import PartitionSpec as P

LATENT = 512
KR = 64
VD = 128
KD = 576
KX = 640
LANES = 128
CAP = 16
N_INST = 32
N_HEAD = 8
N_Y = 4
PIECE = 32
PIECES = 18
ROWS_SENT = 80
SENT = ROWS_SENT + PIECE
SCALE = (VD + KR) ** (-0.5)
BIG = 1e30
BF = jnp.bfloat16
F32 = jnp.float32
VMEM_LIMIT = 48 * 1024 * 1024

NT = (((1,), (1,)), ((), ()))


def params(**kw):
    return pltpu.CompilerParams(vmem_limit_bytes=VMEM_LIMIT, **kw)


def vmem():
    return pl.BlockSpec(memory_space=pltpu.VMEM)


def smem():
    return pl.BlockSpec(memory_space=pltpu.SMEM)


def pack_kernel(routes, owners, rows, cache, lens, out):
    n = rows.shape[1]
    route = routes[...]
    hot = (lax.broadcasted_iota(jnp.int32, (N_INST, n), 0) == route).astype(F32)
    upper = (
        lax.broadcasted_iota(jnp.int32, (n, n), 0) <= lax.broadcasted_iota(jnp.int32, (n, n), 1)
    ).astype(BF)
    count = jnp.dot(hot.astype(BF), upper, preferred_element_type=F32)
    rank = jnp.sum(count * hot, 0, keepdims=True) - 1.0
    slot = route * CAP + rank.astype(jnp.int32)
    place = (lax.broadcasted_iota(jnp.int32, (N_INST * CAP, n), 0) == slot).astype(BF)
    owned = (lax.broadcasted_iota(jnp.int32, (KX - KD, n), 0) == owners[...]).astype(BF)
    main = lax.dot_general(place, rows[...], NT, preferred_element_type=F32)
    mark = lax.dot_general(place, owned, NT, preferred_element_type=F32)
    mark = (mark - 1.0) * BIG
    for t in range(4):
        block = main[:, t * LANES : (t + 1) * LANES].astype(BF)
        out[:, t * CAP : (t + 1) * CAP, :] = block.reshape(N_INST, CAP, LANES)
    block = jnp.concatenate([main[:, LATENT:], mark], 1).astype(BF)
    out[:, 4 * CAP : 5 * CAP, :] = block.reshape(N_INST, CAP, LANES)
    for j in range(PIECES):
        out[j, ROWS_SENT:, :] = cache[0, j * PIECE : (j + 1) * PIECE, :]
    for j in range(PIECES, N_INST):
        out[j, ROWS_SENT:, :] = jnp.zeros((PIECE, LANES), BF)
    length = lens[0]
    col = lax.broadcasted_iota(jnp.int32, (PIECE, LANES), 1)
    high = (length // 32).astype(F32)
    low = (length % 32).astype(F32)
    out[PIECES, ROWS_SENT:, :] = jnp.where(col == 0, high, low).astype(BF)


def pack(routes, owners, rows, cache, lens):
    return pl.pallas_call(
        pack_kernel,
        out_shape=jax.ShapeDtypeStruct((N_INST, SENT, LANES), BF),
        in_specs=[vmem(), vmem(), vmem(), pl.BlockSpec((1, KD, LANES), lambda i: (0, 0, 0)), smem()],
        out_specs=pl.BlockSpec((N_INST, SENT, LANES), lambda i: (0, 0, 0)),
        grid=(1,),
        compiler_params=params(),
    )(routes, owners, rows, cache, lens)


def forward_kernel(partner, landed, out, rows):
    for d in range(N_INST):
        out[d] = landed[partner[d], ROWS_SENT:, :]
    rows[...] = landed[:, :ROWS_SENT, :]


def forward(partner, landed):
    return pl.pallas_call(
        forward_kernel,
        out_shape=(
            jax.ShapeDtypeStruct((N_INST, PIECE, LANES), BF),
            jax.ShapeDtypeStruct((N_INST, ROWS_SENT, LANES), BF),
        ),
        in_specs=[smem(), vmem()],
        out_specs=(vmem(), vmem()),
        compiler_params=params(),
    )(partner, landed)


def resident_kernel(info, *refs):
    queries = refs[:N_HEAD]
    keys, tail, out, scores = refs[N_HEAD:]
    me, length = info[0], info[1]
    chunks = keys.shape[0]
    rows = queries[0].shape[0]
    heads = rows // 4
    for b in range(N_HEAD):
        q = queries[b][...]
        for c in range(chunks):
            scores[:, c * LANES : (c + 1) * LANES] = jnp.dot(q, keys[c], preferred_element_type=F32)
        width = chunks * LANES
        last = lax.dot_general(q, tail[...], NT, preferred_element_type=F32)
        tcol = lax.broadcasted_iota(jnp.int32, last.shape, 1)
        step = lax.broadcasted_iota(jnp.int32, last.shape, 0) // heads
        last = jnp.where(tcol <= step, last * SCALE, -BIG)
        col = lax.broadcasted_iota(jnp.int32, (rows, width), 1)
        main = jnp.where(col < length, scores[...] * SCALE, -BIG)
        peak = jnp.maximum(jnp.max(main, -1, keepdims=True), jnp.max(last, -1, keepdims=True))
        main = jnp.exp(main - peak)
        last = jnp.exp(last - peak)
        total = jnp.sum(main, -1, keepdims=True) + jnp.sum(last, -1, keepdims=True)
        acc = jnp.dot(last.astype(BF), tail[:, :LATENT], preferred_element_type=F32)
        main = main.astype(BF)
        for c in range(chunks):
            acc = acc + lax.dot_general(
                main[:, c * LANES : (c + 1) * LANES],
                keys[c, :LATENT, :],
                NT,
                preferred_element_type=F32,
            )
        out[me ^ b] = (acc / total).astype(BF)


def resident(info, queries, keys, tail):
    rows = queries[0].shape[0]
    return pl.pallas_call(
        resident_kernel,
        out_shape=jax.ShapeDtypeStruct((N_HEAD, rows, LATENT), BF),
        in_specs=[smem()] + [vmem()] * (N_HEAD + 2),
        out_specs=vmem(),
        scratch_shapes=[pltpu.VMEM((rows, keys.shape[0] * LANES), F32)],
        compiler_params=params(),
    )(info, *queries, keys, tail)


def arrival_kernel(info, near, far, r0, r1, r2, r3, tail, out_near, stat_near, out_far, keys):
    count = N_INST * CAP
    for i, r in enumerate((r0, r1, r2, r3)):
        for t in range(KX // LANES):
            keys[i * count : (i + 1) * count, t * LANES : (t + 1) * LANES] = r[
                :, t * CAP : (t + 1) * CAP, :
            ].reshape(count, LANES)
    use_tail = info[2]
    rows = near.shape[0]
    tile = 128
    for source in range(2):
        stats = []
        for part in range(rows // tile):
            q = (near, far)[source][part * tile : (part + 1) * tile, :]
            main = lax.dot_general(q, keys[...], NT, preferred_element_type=F32) * SCALE
            last = lax.dot_general(q, tail[...], NT, preferred_element_type=F32) * SCALE
            tstep = lax.broadcasted_iota(jnp.int32, last.shape, 1) // 4
            step = (lax.broadcasted_iota(jnp.int32, last.shape, 0) % 16) // 4
            last = jnp.where(jnp.logical_and(tstep <= step, use_tail > 0), last, -BIG)
            peak = jnp.maximum(jnp.max(main, -1, keepdims=True), jnp.max(last, -1, keepdims=True))
            main = jnp.exp(main - peak)
            last = jnp.exp(last - peak)
            total = jnp.sum(main, -1, keepdims=True) + jnp.sum(last, -1, keepdims=True)
            acc = jnp.dot(main.astype(BF), keys[:, :LATENT], preferred_element_type=F32)
            acc = acc + jnp.dot(last.astype(BF), tail[:, :LATENT], preferred_element_type=F32)
            value = (acc / total).astype(BF)
            lse = peak + jnp.log(total)
            stats.append(jnp.transpose(jnp.broadcast_to(lse, (tile, LANES))))
            if source == 0:
                out_near[part * tile : (part + 1) * tile, :] = value
            else:
                out_far[part * tile : (part + 1) * tile, :] = value
        stat = jnp.concatenate(stats, 1)[:CAP]
        if source == 0:
            stat_near[...] = stat
        else:
            high = stat.astype(BF).astype(F32)
            middle = (stat - high).astype(BF).astype(F32)
            low = stat - high - middle
            row = lax.broadcasted_iota(jnp.int32, stat.shape, 0)
            split = jnp.where(row == 0, high, jnp.where(row == 1, middle, jnp.where(row == 2, low, 0.0)))
            out_far[rows:, :rows] = split.astype(BF)
            out_far[rows:, rows:] = jnp.zeros((CAP, LATENT - rows), BF)


def arrival(info, near, far, rows, tail):
    n = near.shape[0]
    return pl.pallas_call(
        arrival_kernel,
        out_shape=(
            jax.ShapeDtypeStruct((n, LATENT), BF),
            jax.ShapeDtypeStruct((CAP, n), F32),
            jax.ShapeDtypeStruct((n + CAP, LATENT), BF),
        ),
        in_specs=[smem()] + [vmem()] * 7,
        out_specs=(vmem(),) * 3,
        scratch_shapes=[pltpu.VMEM((4 * N_INST * CAP, KX), BF)],
        compiler_params=params(),
    )(info, near, far, *rows, tail)


def combine_kernel(near, stat_near, far, value_up, out):
    n = near.shape[0]
    split = far[n:, :n].astype(F32)
    stat_far = split[0:1] + split[1:2] + split[2:3]
    mine = stat_near[0:1, :]
    top = jnp.maximum(mine, stat_far)
    a, b = jnp.exp(mine - top), jnp.exp(stat_far - top)
    share = a / (a + b)
    share = jnp.transpose(jnp.broadcast_to(share, (LANES, n)))[:, :1]
    value = near[...].astype(F32) * share + far[:n, :].astype(F32) * (1.0 - share)
    value = value.astype(BF)
    for h in range(value_up.shape[0]):
        out[:, h * VD : (h + 1) * VD] = jnp.dot(
            value[h * 16 : (h + 1) * 16], value_up[h], preferred_element_type=F32
        ).astype(BF)


def combine(near, stat_near, far, value_up):
    heads = value_up.shape[0]
    return pl.pallas_call(
        combine_kernel,
        out_shape=jax.ShapeDtypeStruct((16, heads * VD), BF),
        in_specs=[vmem()] * 4,
        out_specs=vmem(),
        compiler_params=params(),
    )(near, stat_near, far, value_up)


def xor_pairs(d):
    return [(h, h ^ d) for h in range(N_HEAD)]


def local(
    latent_cache,
    cache_lengths,
    partner,
    queries,
    step_rows,
    arrivals,
    arrival_routes,
    arrival_owners,
    new_queries,
    new_step_rows,
    value_up,
):
    me = lax.axis_index("head")
    steps, count, heads = queries.shape[0], queries.shape[1], queries.shape[2]
    new_count = new_queries.shape[1]

    cache_t = jnp.transpose(latent_cache, (0, 2, 1))
    sent = pack(
        arrival_routes.reshape(1, -1),
        arrival_owners.reshape(1, -1),
        jnp.transpose(arrivals),
        cache_t,
        cache_lengths,
    )

    hot = jnp.eye(new_count, KX - KD, dtype=BF)
    near = jnp.concatenate(
        [new_queries, jnp.broadcast_to(hot[None, :, None, :], (steps, new_count, heads, KX - KD))], -1
    )
    near = jnp.transpose(near, (2, 0, 1, 3)).reshape(heads * steps * new_count, KX)
    far = lax.ppermute(near, "head", xor_pairs(N_Y))

    q_all = jnp.transpose(queries, (1, 0, 2, 3)).reshape(count, steps * heads, KD)
    q_blocks = []
    for d in range(N_HEAD):
        block = lax.dynamic_index_in_dim(q_all, me ^ d, 0, keepdims=False)
        q_blocks.append(block if d == 0 else lax.ppermute(block, "head", xor_pairs(d)))

    landed = lax.all_to_all(sent, "inst", split_axis=0, concat_axis=0, tiled=True)
    pieces, rows = forward(partner, landed)
    row_blocks = [rows] + [lax.ppermute(rows, "head", xor_pairs(d)) for d in (1, 3, 2)]
    moved = lax.all_to_all(pieces, "inst", split_axis=0, concat_axis=0, tiled=True)
    moved_cache = moved[:PIECES].reshape(1, KD, LANES)
    tag = moved[PIECES, 0, :2].astype(F32)
    moved_len = (tag[0] * 32.0 + tag[1]).astype(jnp.int32)

    full = jnp.concatenate([moved_cache, cache_t[1:]], 0)
    keys = lax.all_to_all(full, "head", split_axis=0, concat_axis=0, tiled=True)
    own_len = lax.dynamic_index_in_dim(cache_lengths, me, 0, keepdims=False)
    length = jnp.where(me == 0, moved_len, own_len)
    info = jnp.stack([me, length, (me < N_Y).astype(jnp.int32)]).astype(jnp.int32)
    tail = lax.dynamic_index_in_dim(step_rows, me, 1, keepdims=False)
    tail = jnp.pad(tail, ((0, LANES - steps), (0, 0)))
    lat = resident(info, q_blocks, keys, tail)
    lat = lax.all_to_all(lat, "head", split_axis=0, concat_axis=0, tiled=True)
    lat = lat.reshape(count, steps, heads, LATENT)
    local_out = jnp.einsum("rshc,hcv->srhv", lat, value_up, preferred_element_type=F32)
    local_out = local_out.astype(BF).reshape(steps, count, heads * VD)

    mark = jnp.where(jnp.arange(KX - KD)[None, :] == jnp.arange(new_count)[:, None], 0.0, -BIG).astype(BF)
    mark = jnp.broadcast_to(mark[None], (steps, new_count, KX - KD))
    new_tail = jnp.concatenate([new_step_rows, mark], -1).reshape(steps * new_count, KX)
    blank = jnp.full((LANES - steps * new_count, KX), 0.0, BF)
    new_tail = jnp.concatenate([new_tail, blank], 0)
    use_tail = jnp.stack([me, length, (me < N_Y).astype(jnp.int32)]).astype(jnp.int32)
    out_near, stat_near, out_far = arrival(use_tail, near, far, row_blocks, new_tail)
    got = lax.ppermute(out_far, "head", xor_pairs(N_Y))
    arrival_out = combine(out_near, stat_near, got, value_up).reshape(steps, new_count, heads * VD)
    return (local_out, arrival_out)


def solution(mesh):
    in_specs = (
        P("inst", "head", None),
        P("inst"),
        P(),
        P(None, "inst", "head", None),
        P(None, "inst", None),
        P(("inst", "head"), None),
        P(("inst", "head"), None),
        P(("inst", "head")),
        P(None, "inst", "head", None),
        P(None, "inst", None),
        P("head", None, None),
    )
    out_specs = (P(None, "inst", "head"), P(None, "inst", "head"))
    return jax.shard_map(local, mesh=mesh, in_specs=in_specs, out_specs=out_specs, check_vma=False)
```

time: 390 us -> 149 us (0.38)
  blocking collectives: 193 us -> 36.6 us
  local copies, waits for them, and re-layouts: 60.2 us -> 9.09 us
  waiting for transfers between devices: 65 us -> 43.7 us
  Pallas kernels: 0 us -> 19.2 us
  other arithmetic: 19 us -> 1.4 us
  starting transfers between devices: 17.8 us -> 33.1 us
  matrix products: 16.8 us -> 1.62 us
  between operations: 14.2 us -> 2.74 us
    unnamed x1 -> x0, blocking collectives: 161 us -> none
    all_gather x3 -> x0, waiting for transfers between devices: 64.3 us -> none  [the longest x1 64.3 us: local(): lax.all_gather(latent_cache[:MIG], 'inst', axis=0, tiled=True)]
    all_to_all x0 -> x1, blocking collectives: none -> 36.6 us  [local(): lax.all_to_all(sent, 'inst', split_axis=0, concat_axis=0, tiled=True)]
    ppermute x0 -> x12, waiting for transfers between devices: none -> 32.8 us  [the longest x1 10.5 us: local(): far = lax.ppermute(near, 'head', xor_pairs(N_Y))]
    all_gather x2 -> x0, blocking collectives: 32.2 us -> none  [the longest x1 16.7 us: local(): lax.all_gather(arrival_routes, 'head', axis=0, tiled=True)]
    pallas_call x0 -> x5, Pallas kernels: none -> 19.2 us  [the longest x1 8.49 us: resident(): pl.pallas_call(resident_kernel, out_shape=jax.ShapeDtypeStruct((N_HEAD, r...]
    unnamed x31 -> x26, local copies, waits for them, and re-layouts: 24.6 us -> 5.45 us
    ppermute x0 -> x12, starting transfers between devices: none -> 18.3 us  [the longest x7 11.4 us: local(): lax.ppermute(block, 'head', xor_pairs(d))]
  transfers between devices with their start and end apart: 5 -> 15, of which waited for: 1 -> 7; matrix products, arithmetic and copies ran while one was open for 22% -> 3% of each run, Pallas kernels for 0% -> 11%
where the time goes in v1:
time: 149 us; the launch traced here: 147 us
  waiting for transfers between devices  43.7 us (29%)
  blocking collectives  36.6 us (25%)
  starting transfers between devices  33.1 us (22%)
  Pallas kernels  19.2 us (13%)
  local copies, waits for them, and re-layouts  9.09 us (6%)
  between operations  2.74 us (2%)
  matrix products  1.62 us (1%)
    all_to_all x1, blocking collectives, local(): lax.all_to_all(sent, 'inst', split_axis=0, concat_axis=0, tiled=True)  36.6 us
    ppermute x7, starting transfers between devices, local(): lax.ppermute(block, 'head', xor_pairs(d))  11.4 us
    all_to_all x1, waiting for transfers between devices, local(): lax.all_to_all(pieces, 'inst', split_axis=0, concat_axis=0, tiled=True)  10.9 us
    ppermute x1, waiting for transfers between devices, local(): far = lax.ppermute(near, 'head', xor_pairs(N_Y))  10.5 us
    ppermute x7, waiting for transfers between devices, local(): lax.ppermute(block, 'head', xor_pairs(d))  9.66 us
    pallas_call x1, Pallas kernels, resident(): pl.pallas_call(resident_kernel, out_shape=jax.ShapeDtypeStruct((N_HEAD, r...  8.49 us
    pallas_call x1, Pallas kernels, arrival(): pl.pallas_call(arrival_kernel, out_shape=(jax.ShapeDtypeStruct((n, LATENT...  7.69 us
    ppermute x3, waiting for transfers between devices, local(): lax.ppermute(rows, 'head', xor_pairs(d))  6.4 us
  transfers between devices with their start and end apart: 15, of which 7 were waited for; matrix products, arithmetic and copies ran while one was open for 3% of the time, Pallas kernels for 11%

profile of v1, /device:TPU:6, one launch (start us, length us, event | category | flops | bytes accessed | tf_op | source)
XLA Modules:
  0.0 147.5 jit_solution(17442486451958383552)
XLA Ops:
  0.6 0.0 copy-start
  0.6 0.0 copy-start.2
  0.7 1.3 copy-done.2
  1.9 1.0 copy-done.4
  2.9 0.7 copy-done.5
  3.6 0.7 copy-done.6
  4.3 0.7 copy-done.8
  4.9 1.2 shard_map.122
  6.1 0.0 copy-start.7
  6.1 36.6 %all_to_all.20.landed = bf16[32,112,128]{2,1,0:T(8,128)(2,1)S(1)} all-to-all(bf16[32,112,128]{2,1,0:T(8,128)(2,1)S(1)} %shard_map.122), channel_id=1, replica_groups=mesh['inst'=32,'head'=8] {'inst'}, dimensions={0} | all-to-all | bytes 1835008 | tf_op jit(solution)/shard_map/all_to_all | solution.py:282
  42.8 1.3 shard_map.123
  44.1 6.0 %all-to-all-start.1 = ((bf16[32,32,128]{2,1,0:T(8,128)(2,1)}), bf16[32,32,128]{2,1,0:T(8,128)(2,1)S(1)}, u32[]{:S(2)}, u32[]{:S(2)}) async-start(bf16[32,32,128]{2,1,0:T(8,128)(2,1)} %get-tuple-element.7), calls=%async_computation.1 | async-start | bytes 524288 | tf_op jit(solution)/shard_map/all_to_all | solution.py:285
  50.0 0.1 slice.24
  50.1 10.9 %all-to-all-done.1 = bf16[32,32,128]{2,1,0:T(8,128)(2,1)S(1)} async-done(((bf16[32,32,128]{2,1,0:T(8,128)(2,1)}), bf16[32,32,128]{2,1,0:T(8,128)(2,1)S(1)}, u32[]{:S(2)}, u32[]{:S(2)}) %all-to-all-start.1) | async-done | bytes 262176 | tf_op jit(solution)/shard_map/all_to_all | solution.py:285
  61.1 1.1 pad_maximum_fusion
  62.2 4.5 %all-to-all-start.2 = ((bf16[8,576,128]{2,1,0:T(8,128)(2,1)}), bf16[8,576,128]{2,1,0:T(8,128)(2,1)S(1)}, u32[]{:S(2)}, u32[]{:S(2)}) async-start(bf16[8,576,128]{2,1,0:T(8,128)(2,1)} %pad_maximum_fusion), calls=%async_computation.2 | async-start | bytes 2359296 | tf_op jit(solution)/shard_map/all_to_all | solution.py:291
  66.7 1.2 copy.15
  67.9 0.7 dynamic-slice_bitcast_fusion
  68.6 2.0 %collective-permute-start = (bf16[64,576]{1,0:T(8,128)(2,1)}, bf16[64,576]{1,0:T(8,128)(2,1)S(1)}, u32[]{:S(2)}, u32[]{:S(2)}) collective-permute-start(bf16[64,576]{1,0:T(8,128)(2,1)} %get-tuple-element.18), channel_id=1, source_target_pairs={{0,1},{1,0},{2,3},{3,2},{4,5},{5,4},{6,7},{7,6},{8,9},{9,8},{10,11... | collective-permute-start | bytes 221192 | tf_op jit(solution)/shard_map/ppermute | solution.py:280
  70.6 2.7 %collective-permute-start.1 = (bf16[64,576]{1,0:T(8,128)(2,1)S(1)}, bf16[64,576]{1,0:T(8,128)(2,1)S(1)}, u32[]{:S(2)}, u32[]{:S(2)}) collective-permute-start(bf16[64,576]{1,0:T(8,128)(2,1)S(1)} %get-tuple-element.17), channel_id=1, source_target_pairs={{0,2},{1,3},{2,0},{3,1},{4,6},{5,7},{6,4},{7,5},{8,10},{9,11},{10,... | collective-permute-start | bytes 221192 | tf_op jit(solution)/shard_map/ppermute | solution.py:280
  73.3 2.0 %collective-permute-start.3 = (bf16[64,576]{1,0:T(8,128)(2,1)S(1)}, bf16[64,576]{1,0:T(8,128)(2,1)S(1)}, u32[]{:S(2)}, u32[]{:S(2)}) collective-permute-start(bf16[64,576]{1,0:T(8,128)(2,1)S(1)} %get-tuple-element.15), channel_id=1, source_target_pairs={{0,4},{1,5},{2,6},{3,7},{4,0},{5,1},{6,2},{7,3},{8,12},{9,13},{10,... | collective-permute-start | bytes 221192 | tf_op jit(solution)/shard_map/ppermute | solution.py:280
  75.3 0.3 collective-permute-start.4
  75.6 0.6 dynamic_slice.33
  76.3 0.6 fusion.10
  78.7 6.1 %collective-permute-done.refs_1_ = bf16[64,576]{1,0:T(8,128)(2,1)S(1)} collective-permute-done((bf16[64,576]{1,0:T(8,128)(2,1)}, bf16[64,576]{1,0:T(8,128)(2,1)S(1)}, u32[]{:S(2)}, u32[]{:S(2)}) %collective-permute-start) | collective-permute-done | bytes 73760 | tf_op jit(solution)/shard_map/ppermute | solution.py:280
  84.8 3.3 %collective-permute-start.5 = (bf16[64,576]{1,0:T(8,128)(2,1)S(1)}, bf16[64,576]{1,0:T(8,128)(2,1)S(1)}, u32[]{:S(2)}, u32[]{:S(2)}) collective-permute-start(bf16[64,576]{1,0:T(8,128)(2,1)S(1)} %get-tuple-element.13), channel_id=1, source_target_pairs={{0,6},{1,7},{2,4},{3,5},{4,2},{5,3},{6,0},{7,1},{8,14},{9,15},{10,... | collective-permute-start | bytes 221192 | tf_op jit(solution)/shard_map/ppermute | solution.py:280
  88.1 2.3 %collective-permute-done.1.refs_2_ = bf16[64,576]{1,0:T(8,128)(2,1)S(1)} collective-permute-done((bf16[64,576]{1,0:T(8,128)(2,1)S(1)}, bf16[64,576]{1,0:T(8,128)(2,1)S(1)}, u32[]{:S(2)}, u32[]{:S(2)}) %collective-permute-start.1) | collective-permute-done | bytes 73760 | tf_op jit(solution)/shard_map/ppermute | solution.py:280
  90.4 1.2 collective-permute-start.6
  91.6 2.9 %collective-permute-start.9 = (bf16[32,80,128]{2,1,0:T(8,128)(2,1)S(1)}, bf16[32,80,128]{2,1,0:T(8,128)(2,1)}, u32[]{:S(2)}, u32[]{:S(2)}) collective-permute-start(bf16[32,80,128]{2,1,0:T(8,128)(2,1)S(1)} %get-tuple-element.8.r0), channel_id=1, source_target_pairs={{0,3},{1,2},{2,1},{3,0},{4,7},{5,6},{6,5},{7,4},{8,11},{9,10},{10,... | collective-permute-start | bytes 1966088 | tf_op jit(solution)/shard_map/ppermute | solution.py:284
  94.5 1.2 collective-permute-start.10
  95.7 0.1 pad_add_fusion.info
  95.7 1.3 collective-permute-done.6.refs_7_
  97.0 8.5 %shard_map.124 = bf16[8,64,512]{2,1,0:T(8,128)(2,1)} custom-call(s32[3]{0:T(128)S(1)} %pad_add_fusion.info, bf16[64,576]{1,0:T(8,128)(2,1)S(1)} %get-tuple-element.19.refs_0_, bf16[64,576]{1,0:T(8,128)(2,1)S(1)} %collective-permute-done.refs_1_, bf16[64,576]{1,0:T(8,128)(2,1)S(1)} %collective-permute-done.1.refs_2_, ...), custom_call_target="tpu_custom_call" | custom-call | tf_op jit(solution)/shard_map/pallas_call | solution.py:140
  105.5 4.3 %all-to-all-start.3 = ((bf16[8,64,512]{2,1,0:T(8,128)(2,1)}), bf16[8,64,512]{2,1,0:T(8,128)(2,1)}, u32[]{:S(2)}, u32[]{:S(2)}) async-start(bf16[8,64,512]{2,1,0:T(8,128)(2,1)} %shard_map.124), calls=%async_computation.3 | async-start | bytes 1048576 | tf_op jit(solution)/shard_map/all_to_all | solution.py:298
  109.9 0.1 maximum_bitcast_fusion
  110.0 0.1 copy.18
  110.1 0.1 reshape.70.near
  110.2 2.0 %collective-permute-start.7 = (bf16[256,640]{1,0:T(8,128)(2,1)S(1)}, bf16[256,640]{1,0:T(8,128)(2,1)S(1)}, u32[]{:S(2)}, u32[]{:S(2)}) collective-permute-start(bf16[256,640]{1,0:T(8,128)(2,1)S(1)} %reshape.70.near), channel_id=1, source_target_pairs={{0,4},{1,5},{2,6},{3,7},{4,0},{5,1},{6,2},{7,3},{8,12},{9,13},{10,... | collective-permute-start | bytes 983048 | tf_op jit(solution)/shard_map/ppermute | solution.py:274
  112.2 0.1 pad_maximum_fusion.1
  112.3 10.5 %collective-permute-done.7.far = bf16[256,640]{1,0:T(8,128)(2,1)S(1)} collective-permute-done((bf16[256,640]{1,0:T(8,128)(2,1)S(1)}, bf16[256,640]{1,0:T(8,128)(2,1)S(1)}, u32[]{:S(2)}, u32[]{:S(2)}) %collective-permute-start.7) | collective-permute-done | bytes 327712 | tf_op jit(solution)/shard_map/ppermute | solution.py:274
  122.8 6.4 %collective-permute-done.9.r2 = bf16[32,80,128]{2,1,0:T(8,128)(2,1)} collective-permute-done((bf16[32,80,128]{2,1,0:T(8,128)(2,1)S(1)}, bf16[32,80,128]{2,1,0:T(8,128)(2,1)}, u32[]{:S(2)}, u32[]{:S(2)}) %collective-permute-start.9) | collective-permute-done | bytes 655392 | tf_op jit(solution)/shard_map/ppermute | solution.py:284
  129.2 7.7 %shard_map.125 = (bf16[256,512]{1,0:T(8,128)(2,1)S(1)}, f32[16,256]{1,0:T(8,128)S(1)}, bf16[272,512]{1,0:T(8,128)(2,1)S(1)}) custom-call(s32[3]{0:T(128)S(1)} %pad_add_fusion.info, bf16[256,640]{1,0:T(8,128)(2,1)S(1)} %reshape.70.near, bf16[256,640]{1,0:T(8,128)(2,1)S(1)} %collective-permute-done.7.far, bf16[32,80,128]{2,1,0:T(8,128)(2,1)S(1)} %get-tuple-element.8.r0, ...), custom_call_target="tpu_custom_call" | custom-call | tf_op jit(solution)/shard_map/pallas_call | solution.py:197
  136.9 0.8 collective-permute-start.11
  137.8 6.2 %collective-permute-done.11.far = bf16[272,512]{1,0:T(8,128)(2,1)S(1)} collective-permute-done((bf16[272,512]{1,0:T(8,128)(2,1)S(1)}, bf16[272,512]{1,0:T(8,128)(2,1)S(1)}, u32[]{:S(2)}, u32[]{:S(2)}) %collective-permute-start.11) | collective-permute-done | bytes 278560 | tf_op jit(solution)/shard_map/ppermute | solution.py:310
  144.0 0.6 shard_map.126
  144.5 0.7 reshape.72
  145.2 1.6 %fusion.5 = bf16[16,4,1,8,128]{4,3,2,1,0:T(8,128)(2,1)S(1)} fusion(bf16[16,512,128]{2,1,0:T(8,128)(2,1)S(1)} %copy-done.1, bf16[8,4,16,512]{3,2,1,0:T(8,128)(2,1)} %bitcast.21), kind=kOutput, calls=%fused_computation.4 | convolution fusion | flops 67174400 | bytes 2752512 | tf_op jit(solution)/shard_map/rshc,hcv->srhv/dot_general | solution.py:300
  146.8 0.7 copy.26
  (37 shorter events, 0.2 us)
Async XLA Ops:
  0.6 75.6 %copy-start = (bf16[4,8,576]{2,1,0:T(8,128)(2,1)S(1)}, bf16[4,8,576]{2,1,0:T(8,128)(2,1)}, u32[]{:S(2)}) copy-start(bf16[4,8,576]{2,1,0:T(8,128)(2,1)} %param.15) | copy-start | bytes 110596
  0.6 1.3 copy-start.2
  1.9 1.0 copy-start.4
  2.9 0.7 copy-start.5
  3.6 0.7 copy-start.6
  4.2 0.7 copy-start.8
  6.1 36.7 %copy-start.7 = (s32[32]{0:T(128)S(1)}, s32[32]{0:T(128)}, u32[]{:S(2)}) copy-start(s32[32]{0:T(128)} %partner.1) | copy-start | bytes 388
  42.8 7.3 %copy-start.3 = (bf16[8,128,576]{1,2,0:T(8,128)(2,1)S(1)}, bf16[8,128,576]{1,2,0:T(8,128)(2,1)}, u32[]{:S(2)}) copy-start(bf16[8,128,576]{1,2,0:T(8,128)(2,1)} %param.11) | copy-start | bytes 3538948
  44.1 17.0 %all-to-all-start.1 = ((bf16[32,32,128]{2,1,0:T(8,128)(2,1)}), bf16[32,32,128]{2,1,0:T(8,128)(2,1)S(1)}, u32[]{:S(2)}, u32[]{:S(2)}) async-start(bf16[32,32,128]{2,1,0:T(8,128)(2,1)} %get-tuple-element.7), calls=%async_computation.1 | async-start | bytes 524288 | tf_op jit(solution)/shard_map/all_to_all | solution.py:285
  62.2 34.8 %all-to-all-start.2 = ((bf16[8,576,128]{2,1,0:T(8,128)(2,1)}), bf16[8,576,128]{2,1,0:T(8,128)(2,1)S(1)}, u32[]{:S(2)}, u32[]{:S(2)}) async-start(bf16[8,576,128]{2,1,0:T(8,128)(2,1)} %pad_maximum_fusion), calls=%async_computation.2 | async-start | bytes 2359296 | tf_op jit(solution)/shard_map/all_to_all | solution.py:291
  66.7 8.9 %copy-start.9 = (s32[8]{0:T(128)S(1)}, s32[8]{0:T(128)}, u32[]{:S(2)}) copy-start(s32[8]{0:T(128)} %lens.1) | copy-start | bytes 100
  68.6 16.2 %collective-permute-start = (bf16[64,576]{1,0:T(8,128)(2,1)}, bf16[64,576]{1,0:T(8,128)(2,1)S(1)}, u32[]{:S(2)}, u32[]{:S(2)}) collective-permute-start(bf16[64,576]{1,0:T(8,128)(2,1)} %get-tuple-element.18), channel_id=1, source_target_pairs={{0,1},{1,0},{2,3},{3,2},{4,5},{5,4},{6,7},{7,6},{8,9},{9,8},{10,11... | collective-permute-start | bytes 221192 | tf_op jit(solution)/shard_map/ppermute | solution.py:280
  70.6 19.7 %collective-permute-start.1 = (bf16[64,576]{1,0:T(8,128)(2,1)S(1)}, bf16[64,576]{1,0:T(8,128)(2,1)S(1)}, u32[]{:S(2)}, u32[]{:S(2)}) collective-permute-start(bf16[64,576]{1,0:T(8,128)(2,1)S(1)} %get-tuple-element.17), channel_id=1, source_target_pairs={{0,2},{1,3},{2,0},{3,1},{4,6},{5,7},{6,4},{7,5},{8,10},{9,11},{10,... | collective-permute-start | bytes 221192 | tf_op jit(solution)/shard_map/ppermute | solution.py:280
  73.3 18.3 %collective-permute-start.2 = (bf16[64,576]{1,0:T(8,128)(2,1)S(1)}, bf16[64,576]{1,0:T(8,128)(2,1)S(1)}, u32[]{:S(2)}, u32[]{:S(2)}) collective-permute-start(bf16[64,576]{1,0:T(8,128)(2,1)S(1)} %get-tuple-element.16), channel_id=1, source_target_pairs={{0,3},{1,2},{2,1},{3,0},{4,7},{5,6},{6,5},{7,4},{8,11},{9,10},{10,... | collective-permute-start | bytes 221192 | tf_op jit(solution)/shard_map/ppermute | solution.py:280
  73.3 18.3 %collective-permute-start.3 = (bf16[64,576]{1,0:T(8,128)(2,1)S(1)}, bf16[64,576]{1,0:T(8,128)(2,1)S(1)}, u32[]{:S(2)}, u32[]{:S(2)}) collective-permute-start(bf16[64,576]{1,0:T(8,128)(2,1)S(1)} %get-tuple-element.15), channel_id=1, source_target_pairs={{0,4},{1,5},{2,6},{3,7},{4,0},{5,1},{6,2},{7,3},{8,12},{9,13},{10,... | collective-permute-start | bytes 221192 | tf_op jit(solution)/shard_map/ppermute | solution.py:280
  75.3 19.1 %collective-permute-start.4 = (bf16[64,576]{1,0:T(8,128)(2,1)S(1)}, bf16[64,576]{1,0:T(8,128)(2,1)S(1)}, u32[]{:S(2)}, u32[]{:S(2)}) collective-permute-start(bf16[64,576]{1,0:T(8,128)(2,1)S(1)} %get-tuple-element.14), channel_id=1, source_target_pairs={{0,5},{1,4},{2,7},{3,6},{4,1},{5,0},{6,3},{7,2},{8,13},{9,12},{10,... | collective-permute-start | bytes 221192 | tf_op jit(solution)/shard_map/ppermute | solution.py:280
  84.8 10.9 %collective-permute-start.5 = (bf16[64,576]{1,0:T(8,128)(2,1)S(1)}, bf16[64,576]{1,0:T(8,128)(2,1)S(1)}, u32[]{:S(2)}, u32[]{:S(2)}) collective-permute-start(bf16[64,576]{1,0:T(8,128)(2,1)S(1)} %get-tuple-element.13), channel_id=1, source_target_pairs={{0,6},{1,7},{2,4},{3,5},{4,2},{5,3},{6,0},{7,1},{8,14},{9,15},{10,... | collective-permute-start | bytes 221192 | tf_op jit(solution)/shard_map/ppermute | solution.py:280
  90.4 6.7 %collective-permute-start.6 = (bf16[64,576]{1,0:T(8,128)(2,1)S(1)}, bf16[64,576]{1,0:T(8,128)(2,1)S(1)}, u32[]{:S(2)}, u32[]{:S(2)}) collective-permute-start(bf16[64,576]{1,0:T(8,128)(2,1)S(1)} %get-tuple-element.12), channel_id=1, source_target_pairs={{0,7},{1,6},{2,5},{3,4},{4,3},{5,2},{6,1},{7,0},{8,15},{9,14},{10,... | collective-permute-start | bytes 221192 | tf_op jit(solution)/shard_map/ppermute | solution.py:280
  91.6 31.3 %collective-permute-start.8 = (bf16[32,80,128]{2,1,0:T(8,128)(2,1)S(1)}, bf16[32,80,128]{2,1,0:T(8,128)(2,1)}, u32[]{:S(2)}, u32[]{:S(2)}) collective-permute-start(bf16[32,80,128]{2,1,0:T(8,128)(2,1)S(1)} %get-tuple-element.8.r0), channel_id=1, source_target_pairs={{0,1},{1,0},{2,3},{3,2},{4,5},{5,4},{6,7},{7,6},{8,9},{9,8},{10,11... | collective-permute-start | bytes 1966088 | tf_op jit(solution)/shard_map/ppermute | solution.py:284
  91.6 37.7 %collective-permute-start.9 = (bf16[32,80,128]{2,1,0:T(8,128)(2,1)S(1)}, bf16[32,80,128]{2,1,0:T(8,128)(2,1)}, u32[]{:S(2)}, u32[]{:S(2)}) collective-permute-start(bf16[32,80,128]{2,1,0:T(8,128)(2,1)S(1)} %get-tuple-element.8.r0), channel_id=1, source_target_pairs={{0,3},{1,2},{2,1},{3,0},{4,7},{5,6},{6,5},{7,4},{8,11},{9,10},{10,... | collective-permute-start | bytes 1966088 | tf_op jit(solution)/shard_map/ppermute | solution.py:284
  94.5 34.8 %collective-permute-start.10 = (bf16[32,80,128]{2,1,0:T(8,128)(2,1)S(1)}, bf16[32,80,128]{2,1,0:T(8,128)(2,1)}, u32[]{:S(2)}, u32[]{:S(2)}) collective-permute-start(bf16[32,80,128]{2,1,0:T(8,128)(2,1)S(1)} %get-tuple-element.8.r0), channel_id=1, source_target_pairs={{0,2},{1,3},{2,0},{3,1},{4,6},{5,7},{6,4},{7,5},{8,10},{9,11},{10,... | collective-permute-start | bytes 1966088 | tf_op jit(solution)/shard_map/ppermute | solution.py:284
  105.5 4.3 %copy-start.10 = (bf16[4,4,16,576]{3,2,1,0:T(8,128)(2,1)S(1)}, bf16[4,4,16,576]{3,2,1,0:T(8,128)(2,1)}, u32[]{:S(2)}) copy-start(bf16[4,4,16,576]{3,2,1,0:T(8,128)(2,1)} %param.19) | copy-start | bytes 884740
  105.5 39.7 %all-to-all-start.3 = ((bf16[8,64,512]{2,1,0:T(8,128)(2,1)}), bf16[8,64,512]{2,1,0:T(8,128)(2,1)}, u32[]{:S(2)}, u32[]{:S(2)}) async-start(bf16[8,64,512]{2,1,0:T(8,128)(2,1)} %shard_map.124), calls=%async_computation.3 | async-start | bytes 1048576 | tf_op jit(solution)/shard_map/all_to_all | solution.py:298
  109.8 2.4 %copy-start.11 = (bf16[4,4,576]{2,1,0:T(4,128)(2,1)S(1)}, bf16[4,4,576]{2,1,0:T(4,128)(2,1)}, u32[]{:S(2)}) copy-start(bf16[4,4,576]{2,1,0:T(4,128)(2,1)} %param.20) | copy-start | bytes 55300
  110.2 12.7 %collective-permute-start.7 = (bf16[256,640]{1,0:T(8,128)(2,1)S(1)}, bf16[256,640]{1,0:T(8,128)(2,1)S(1)}, u32[]{:S(2)}, u32[]{:S(2)}) collective-permute-start(bf16[256,640]{1,0:T(8,128)(2,1)S(1)} %reshape.70.near), channel_id=1, source_target_pairs={{0,4},{1,5},{2,6},{3,7},{4,0},{5,1},{6,2},{7,3},{8,12},{9,13},{10,... | collective-permute-start | bytes 983048 | tf_op jit(solution)/shard_map/ppermute | solution.py:274
  112.3 31.7 %copy-start.1 = (bf16[16,512,128]{2,1,0:T(8,128)(2,1)S(1)}, bf16[16,512,128]{2,1,0:T(8,128)(2,1)}, u32[]{:S(2)}) copy-start(bf16[16,512,128]{2,1,0:T(8,128)(2,1)} %value_up.1) | copy-start | bytes 6291460
  136.9 7.0 %collective-permute-start.11 = (bf16[272,512]{1,0:T(8,128)(2,1)S(1)}, bf16[272,512]{1,0:T(8,128)(2,1)S(1)}, u32[]{:S(2)}, u32[]{:S(2)}) collective-permute-start(bf16[272,512]{1,0:T(8,128)(2,1)S(1)} %get-tuple-element.11), channel_id=1, source_target_pairs={{0,4},{1,5},{2,6},{3,7},{4,0},{5,1},{6,2},{7,3},{8,12},{9,13},{10,... | collective-permute-start | bytes 835592 | tf_op jit(solution)/shard_map/ppermute | solution.py:310

commit v2 on v1

--- a/solution.py
+++ b/solution.py
@@ -15,32 +15,36 @@
 N_INST = 32
 N_HEAD = 8
 N_Y = 4
-PIECE = 32
-PIECES = 18
+PIECE = 24
+PIECES = 24
 ROWS_SENT = 80
 SENT = ROWS_SENT + PIECE
 SCALE = (VD + KR) ** (-0.5)
 BIG = 1e30
 BF = jnp.bfloat16
 F32 = jnp.float32
-VMEM_LIMIT = 48 * 1024 * 1024
+VMEM_LIMIT = 60 * 1024 * 1024
 
 NT = (((1,), (1,)), ((), ()))
 
 
-def params(**kw):
-    return pltpu.CompilerParams(vmem_limit_bytes=VMEM_LIMIT, **kw)
+def params(limit=32 * 1024 * 1024):
+    return pltpu.CompilerParams(vmem_limit_bytes=limit)
 
 
 def vmem():
     return pl.BlockSpec(memory_space=pltpu.VMEM)
 
 
+def whole(x):
+    return pl.BlockSpec(x.shape, lambda i: (0,) * len(x.shape))
+
+
 def smem():
     return pl.BlockSpec(memory_space=pltpu.SMEM)
 
 
-def pack_kernel(routes, owners, rows, cache, lens, out):
+def pack_kernel(lens, routes, owners, rows, cache, out):
     n = rows.shape[1]
     route = routes[...]
     hot = (lax.broadcasted_iota(jnp.int32, (N_INST, n), 0) == route).astype(F32)
@@ -72,14 +76,48 @@
 
 
 def pack(routes, owners, rows, cache, lens):
+    shape = jax.ShapeDtypeStruct((N_INST, SENT, LANES), BF)
+    first = pl.BlockSpec((1, KD, LANES), lambda i: (0, 0, 0))
     return pl.pallas_call(
         pack_kernel,
-        out_shape=jax.ShapeDtypeStruct((N_INST, SENT, LANES), BF),
-        in_specs=[vmem(), vmem(), vmem(), pl.BlockSpec((1, KD, LANES), lambda i: (0, 0, 0)), smem()],
-        out_specs=pl.BlockSpec((N_INST, SENT, LANES), lambda i: (0, 0, 0)),
+        out_shape=shape,
+        in_specs=[smem(), whole(routes), whole(owners), whole(rows), first],
+        out_specs=whole(shape),
         grid=(1,),
+        compiler_params=params(VMEM_LIMIT),
+    )(lens, routes, owners, rows, cache)
+
+
+def copy_kernel(x, out):
+    out[...] = x[...]
+
+
+def copied(x):
+    block = pl.BlockSpec((1,) + x.shape[1:], lambda i: (i, 0, 0))
+    return pl.pallas_call(
+        copy_kernel,
+        out_shape=jax.ShapeDtypeStruct(x.shape, x.dtype),
+        in_specs=[block],
+        out_specs=block,
+        grid=(x.shape[0],),
         compiler_params=params(),
-    )(routes, owners, rows, cache, lens)
+    )(x)
+
+
+def settle_kernel(moved, _, out):
+    out[0] = moved[...]
+
+
+def settle(moved, cache):
+    return pl.pallas_call(
+        settle_kernel,
+        out_shape=jax.ShapeDtypeStruct(cache.shape, BF),
+        in_specs=[pl.BlockSpec((KD, LANES), lambda i: (0, 0)), pl.BlockSpec(memory_space=pl.ANY)],
+        out_specs=pl.BlockSpec((1, KD, LANES), lambda i: (0, 0, 0)),
+        grid=(1,),
+        input_output_aliases={1: 0},
+        compiler_params=params(),
+    )(moved, cache)
 
 
 def forward_kernel(partner, landed, out, rows):
@@ -89,74 +127,96 @@
 
 
 def forward(partner, landed):
+    shapes = (
+        jax.ShapeDtypeStruct((N_INST, PIECE, LANES), BF),
+        jax.ShapeDtypeStruct((N_INST, ROWS_SENT, LANES), BF),
+    )
     return pl.pallas_call(
         forward_kernel,
-        out_shape=(
-            jax.ShapeDtypeStruct((N_INST, PIECE, LANES), BF),
-            jax.ShapeDtypeStruct((N_INST, ROWS_SENT, LANES), BF),
-        ),
+        out_shape=shapes,
         in_specs=[smem(), vmem()],
-        out_specs=(vmem(), vmem()),
+        out_specs=(vmem(),) * 2,
         compiler_params=params(),
     )(partner, landed)
 
 
 def resident_kernel(info, *refs):
-    queries = refs[:N_HEAD]
-    keys, tail, out, scores = refs[N_HEAD:]
+    across = refs[:N_Y]
+    beyond, chunked, tail, tag, out, query, keys, weights, totals = refs[N_Y:]
     me, length = info[0], info[1]
-    chunks = keys.shape[0]
-    rows = queries[0].shape[0]
+    side = me // N_Y
+    chunks = chunked.shape[0]
+    rows = beyond.shape[1]
     heads = rows // 4
-    for b in range(N_HEAD):
-        q = queries[b][...]
-        for c in range(chunks):
-            scores[:, c * LANES : (c + 1) * LANES] = jnp.dot(q, keys[c], preferred_element_type=F32)
-        width = chunks * LANES
+    width = chunks * LANES
+    for d in range(N_Y):
+        query[d * rows : (d + 1) * rows, :] = across[d][side]
+        query[(N_Y + d) * rows : (N_Y + d + 1) * rows, :] = beyond[d]
+    for c in range(chunks):
+        keys[:, c * LANES : (c + 1) * LANES] = chunked[c]
+    moved = tag[...].astype(F32)
+    moved = (moved[0:1, 0:1] * 32.0 + moved[0:1, 1:2]).astype(jnp.int32)
+    length = jnp.where(me == 0, moved, length)
+    valid = lax.broadcasted_iota(jnp.int32, (1, width), 1) < length
+    tile = 128
+    for part in range(N_HEAD * rows // tile):
+        span = slice(part * tile, (part + 1) * tile)
+        q = query[span, :]
+        main = jnp.dot(q, keys[...], preferred_element_type=F32)
         last = lax.dot_general(q, tail[...], NT, preferred_element_type=F32)
         tcol = lax.broadcasted_iota(jnp.int32, last.shape, 1)
-        step = lax.broadcasted_iota(jnp.int32, last.shape, 0) // heads
+        step = lax.broadcasted_iota(jnp.int32, last.shape, 0) % rows // heads
         last = jnp.where(tcol <= step, last * SCALE, -BIG)
-        col = lax.broadcasted_iota(jnp.int32, (rows, width), 1)
-        main = jnp.where(col < length, scores[...] * SCALE, -BIG)
+        main = jnp.where(valid, main * SCALE, -BIG)
         peak = jnp.maximum(jnp.max(main, -1, keepdims=True), jnp.max(last, -1, keepdims=True))
         main = jnp.exp(main - peak)
         last = jnp.exp(last - peak)
-        total = jnp.sum(main, -1, keepdims=True) + jnp.sum(last, -1, keepdims=True)
-        acc = jnp.dot(last.astype(BF), tail[:, :LATENT], preferred_element_type=F32)
-        main = main.astype(BF)
-        for c in range(chunks):
-            acc = acc + lax.dot_general(
-                main[:, c * LANES : (c + 1) * LANES],
-                keys[c, :LATENT, :],
-                NT,
-                preferred_element_type=F32,
-            )
-        out[me ^ b] = (acc / total).astype(BF)
-
-
-def resident(info, queries, keys, tail):
-    rows = queries[0].shape[0]
+        totals[span, :] = jnp.broadcast_to(
+            jnp.sum(main, -1, keepdims=True) + jnp.sum(last, -1, keepdims=True), (tile, LANES)
+        )
+        weights[span, :width] = main.astype(BF)
+        weights[span, width:] = last.astype(BF)
+    acc = lax.dot_general(weights[:, :width], keys[:LATENT, :], NT, preferred_element_type=F32)
+    acc = acc + jnp.dot(weights[:, width:], tail[:, :LATENT], preferred_element_type=F32)
+    for b in range(N_HEAD):
+        span = slice(b * rows, (b + 1) * rows)
+        out[me ^ b] = (acc[span] / totals[span, :1]).astype(BF)
+
+
+def resident(info, across, beyond, keys, tail, tag):
+    rows = beyond.shape[1]
+    count = N_HEAD * rows
+    width = keys.shape[0] * LANES
+    shape = jax.ShapeDtypeStruct((N_HEAD, rows, LATENT), BF)
+    inputs = (*across, beyond, keys, tail, tag)
     return pl.pallas_call(
         resident_kernel,
-        out_shape=jax.ShapeDtypeStruct((N_HEAD, rows, LATENT), BF),
-        in_specs=[smem()] + [vmem()] * (N_HEAD + 2),
-        out_specs=vmem(),
-        scratch_shapes=[pltpu.VMEM((rows, keys.shape[0] * LANES), F32)],
-        compiler_params=params(),
-    )(info, *queries, keys, tail)
-
-
-def arrival_kernel(info, near, far, r0, r1, r2, r3, tail, out_near, stat_near, out_far, keys):
-    count = N_INST * CAP
-    for i, r in enumerate((r0, r1, r2, r3)):
+        out_shape=shape,
+        in_specs=[smem()] + [whole(x) for x in inputs],
+        out_specs=whole(shape),
+        grid=(1,),
+        scratch_shapes=[
+            pltpu.VMEM((count, KD), BF),
+            pltpu.VMEM((KD, width), BF),
+            pltpu.VMEM((count, width + LANES), BF),
+            pltpu.VMEM((count, LANES), F32),
+        ],
+        compiler_params=params(VMEM_LIMIT),
+    )(info, *inputs)
+
+
+def arrival_kernel(info, near, far, r0, r1, r2, r3, r4, tail, out_near, stat_near, out_far, keys):
+    start = 0
+    for r in (r0, r1, r2, r3, r4):
+        count = r.shape[0] * CAP
         for t in range(KX // LANES):
-            keys[i * count : (i + 1) * count, t * LANES : (t + 1) * LANES] = r[
+            keys[start : start + count, t * LANES : (t + 1) * LANES] = r[
                 :, t * CAP : (t + 1) * CAP, :
             ].reshape(count, LANES)
+        start = start + count
     use_tail = info[2]
     rows = near.shape[0]
-    tile = 128
+    tile = 256
     for source in range(2):
         stats = []
         for part in range(rows // tile):
@@ -194,18 +254,20 @@
 
 def arrival(info, near, far, rows, tail):
     n = near.shape[0]
+    shapes = (
+        jax.ShapeDtypeStruct((n, LATENT), BF),
+        jax.ShapeDtypeStruct((CAP, n), F32),
+        jax.ShapeDtypeStruct((n + CAP, LATENT), BF),
+    )
+    inputs = (near, far, *rows, tail)
     return pl.pallas_call(
         arrival_kernel,
-        out_shape=(
-            jax.ShapeDtypeStruct((n, LATENT), BF),
-            jax.ShapeDtypeStruct((CAP, n), F32),
-            jax.ShapeDtypeStruct((n + CAP, LATENT), BF),
-        ),
-        in_specs=[smem()] + [vmem()] * 7,
+        out_shape=shapes,
+        in_specs=[smem()] + [vmem()] * len(inputs),
         out_specs=(vmem(),) * 3,
         scratch_shapes=[pltpu.VMEM((4 * N_INST * CAP, KX), BF)],
         compiler_params=params(),
-    )(info, near, far, *rows, tail)
+    )(info, *inputs)
 
 
 def combine_kernel(near, stat_near, far, value_up, out):
@@ -238,6 +300,16 @@
 
 def xor_pairs(d):
     return [(h, h ^ d) for h in range(N_HEAD)]
+
+
+def spread(blocks, y, side):
+    paired = blocks.reshape((2, N_Y) + blocks.shape[1:])
+    across = []
+    for d in range(N_Y):
+        block = lax.dynamic_index_in_dim(paired, y ^ d, 1, keepdims=False)
+        across.append(block if d == 0 else lax.ppermute(block, "head", xor_pairs(d)))
+    beyond = jnp.stack([lax.dynamic_index_in_dim(b, 1 - side, 0, keepdims=False) for b in across])
+    return across, lax.ppermute(beyond, "head", xor_pairs(N_Y))
 
 
 def local(
@@ -271,43 +343,45 @@
         [new_queries, jnp.broadcast_to(hot[None, :, None, :], (steps, new_count, heads, KX - KD))], -1
     )
     near = jnp.transpose(near, (2, 0, 1, 3)).reshape(heads * steps * new_count, KX)
-    far = lax.ppermute(near, "head", xor_pairs(N_Y))
-
+    y, side = me % N_Y, me // N_Y
     q_all = jnp.transpose(queries, (1, 0, 2, 3)).reshape(count, steps * heads, KD)
-    q_blocks = []
-    for d in range(N_HEAD):
-        block = lax.dynamic_index_in_dim(q_all, me ^ d, 0, keepdims=False)
-        q_blocks.append(block if d == 0 else lax.ppermute(block, "head", xor_pairs(d)))
+    across, beyond = spread(q_all, y, side)
 
     landed = lax.all_to_all(sent, "inst", split_axis=0, concat_axis=0, tiled=True)
-    pieces, rows = forward(partner, landed)
-    row_blocks = [rows] + [lax.ppermute(rows, "head", xor_pairs(d)) for d in (1, 3, 2)]
-    moved = lax.all_to_all(pieces, "inst", split_axis=0, concat_axis=0, tiled=True)
-    moved_cache = moved[:PIECES].reshape(1, KD, LANES)
-    tag = moved[PIECES, 0, :2].astype(F32)
-    moved_len = (tag[0] * 32.0 + tag[1]).astype(jnp.int32)
-
-    full = jnp.concatenate([moved_cache, cache_t[1:]], 0)
-    keys = lax.all_to_all(full, "head", split_axis=0, concat_axis=0, tiled=True)
+    full = copied(cache_t)
     own_len = lax.dynamic_index_in_dim(cache_lengths, me, 0, keepdims=False)
-    length = jnp.where(me == 0, moved_len, own_len)
-    info = jnp.stack([me, length, (me < N_Y).astype(jnp.int32)]).astype(jnp.int32)
+    info = jnp.stack([me, own_len, (me < N_Y).astype(jnp.int32)]).astype(jnp.int32)
     tail = lax.dynamic_index_in_dim(step_rows, me, 1, keepdims=False)
     tail = jnp.pad(tail, ((0, LANES - steps), (0, 0)))
-    lat = resident(info, q_blocks, keys, tail)
-    lat = lax.all_to_all(lat, "head", split_axis=0, concat_axis=0, tiled=True)
-    lat = lat.reshape(count, steps, heads, LATENT)
-    local_out = jnp.einsum("rshc,hcv->srhv", lat, value_up, preferred_element_type=F32)
-    local_out = local_out.astype(BF).reshape(steps, count, heads * VD)
-
     mark = jnp.where(jnp.arange(KX - KD)[None, :] == jnp.arange(new_count)[:, None], 0.0, -BIG).astype(BF)
     mark = jnp.broadcast_to(mark[None], (steps, new_count, KX - KD))
     new_tail = jnp.concatenate([new_step_rows, mark], -1).reshape(steps * new_count, KX)
     blank = jnp.full((LANES - steps * new_count, KX), 0.0, BF)
     new_tail = jnp.concatenate([new_tail, blank], 0)
-    use_tail = jnp.stack([me, length, (me < N_Y).astype(jnp.int32)]).astype(jnp.int32)
-    out_near, stat_near, out_far = arrival(use_tail, near, far, row_blocks, new_tail)
+    landed, full, info, tail, new_tail, near, *across = lax.optimization_barrier(
+        (landed, full, info, tail, new_tail, near, *across)
+    )
+    pieces, rows = forward(partner, landed)
+    far = lax.ppermute(near, "head", xor_pairs(N_Y))
+    half = N_INST // 2
+    r1, r3 = (lax.ppermute(rows, "head", xor_pairs(d)) for d in (1, 3))
+    moved = lax.all_to_all(pieces, "inst", split_axis=0, concat_axis=0, tiled=True)
+    full = settle(moved.reshape(-1, LANES), full)
+    r1, r3 = lax.optimization_barrier((r1, r3))
+    f1 = lax.ppermute(r3[:half], "head", xor_pairs(1))
+    f3 = lax.ppermute(r1[half:], "head", xor_pairs(3))
+    full, f1, f3, far, beyond = lax.optimization_barrier((full, f1, f3, far, beyond))
+    keys = lax.all_to_all(full, "head", split_axis=0, concat_axis=0, tiled=True)
+    row_blocks = (rows, r1, r3, f1, f3)
+    out_near, stat_near, out_far = arrival(info, near, far, row_blocks, new_tail)
     got = lax.ppermute(out_far, "head", xor_pairs(N_Y))
+    keys, out_far = lax.optimization_barrier((keys, out_far))
+    lat = resident(info, across, beyond, keys, tail, moved[PIECES])
+    lat = lax.all_to_all(lat, "head", split_axis=0, concat_axis=0, tiled=True)
+    lat = lat.reshape(count, steps, heads, LATENT)
+    local_out = jnp.einsum("rshc,hcv->srhv", lat, value_up, preferred_element_type=F32)
+    local_out = local_out.astype(BF).reshape(steps, count, heads * VD)
+
     arrival_out = combine(out_near, stat_near, got, value_up).reshape(steps, new_count, heads * VD)
     return (local_out, arrival_out)
 

time: 149 us -> 120 us (0.81)
  blocking collectives: 36.6 us -> 0 us
  starting transfers between devices: 33.1 us -> 39.1 us
  local copies, waits for them, and re-layouts: 9.09 us -> 14.3 us
  other arithmetic: 1.4 us -> 4.9 us
  waiting for transfers between devices: 43.7 us -> 40.8 us
  between operations: 2.74 us -> 0.89 us
    all_to_all x1 -> x0, blocking collectives: 36.6 us -> none  [local(): lax.all_to_all(sent, 'inst', split_axis=0, concat_axis=0, tiled=True)]
    all_to_all x0 -> x1, starting transfers between devices: none -> 11.6 us  [local(): lax.all_to_all(sent, 'inst', split_axis=0, concat_axis=0, tiled=True)]
    all_to_all x1, waiting for transfers between devices: 10.9 us -> 0.01 us  [local(): lax.all_to_all(pieces, 'inst', split_axis=0, concat_axis=0, tiled=True)]
    ppermute x1, waiting for transfers between devices: 10.5 us -> 0.01 us  [local(): far = lax.ppermute(near, 'head', xor_pairs(N_Y))]
    all_to_all x0 -> x1, waiting for transfers between devices: none -> 8.14 us  [local(): lax.all_to_all(sent, 'inst', split_axis=0, concat_axis=0, tiled=True)]
    all_to_all x1, waiting for transfers between devices: 0.01 us -> 7.44 us  [local(): keys = lax.all_to_all(full, 'head', split_axis=0, concat_axis=0, tiled=True)]
    ppermute x10 -> x8, starting transfers between devices: 15.5 us -> 9.58 us  [the longest x3 4.09 us: spread(): lax.ppermute(block, 'head', xor_pairs(d))]
    ppermute x1, waiting for transfers between devices: 6.19 us -> 12.1 us  [local(): got = lax.ppermute(out_far, 'head', xor_pairs(N_Y))]
  transfers between devices with their start and end apart: 15 -> 14, of which waited for: 7 -> 6; matrix products, arithmetic and copies ran while one was open for 3% -> 14% of each run, Pallas kernels for 11% -> 8%
where the time goes in v2:
time: 120 us; the launch traced here: 118 us
  waiting for transfers between devices  40.8 us (34%)
  starting transfers between devices  39.1 us (33%)
  Pallas kernels  18 us (15%)
  local copies, waits for them, and re-layouts  14.3 us (12%)
  other arithmetic  4.9 us (4%)
    ppermute x1, waiting for transfers between devices, local(): got = lax.ppermute(out_far, 'head', xor_pairs(N_Y))  12.1 us
    all_to_all x1, starting transfers between devices, local(): lax.all_to_all(sent, 'inst', split_axis=0, concat_axis=0, tiled=True)  11.6 us
    all_to_all x1, waiting for transfers between devices, local(): lax.all_to_all(sent, 'inst', split_axis=0, concat_axis=0, tiled=True)  8.14 us
    ppermute x1, waiting for transfers between devices, spread(): return (across, lax.ppermute(beyond, 'head', xor_pairs(N_Y)))  8.13 us
    all_to_all x1, waiting for transfers between devices, local(): keys = lax.all_to_all(full, 'head', split_axis=0, concat_axis=0, tiled=True)  7.44 us
    all_to_all x1, starting transfers between devices, local(): lax.all_to_all(pieces, 'inst', split_axis=0, concat_axis=0, tiled=True)  6.41 us
    pallas_call x1, Pallas kernels, arrival(): pl.pallas_call(arrival_kernel, out_shape=shapes, in_specs=[smem()] + [vme...  5.22 us
    ppermute x2, waiting for transfers between devices, local(): r1, r3 = (lax.ppermute(rows, 'head', xor_pairs(d)) for d in (1, 3))  4.94 us
  transfers between devices with their start and end apart: 14, of which 6 were waited for; matrix products, arithmetic and copies ran while one was open for 14% of the time, Pallas kernels for 8%

profile of v2, /device:TPU:6, one launch (start us, length us, event | category | flops | bytes accessed | tf_op | source)
XLA Modules:
  0.0 118.5 jit_solution(11303463296163035047)
XLA Ops:
  0.7 2.7 %shard_map.122 = bf16[32,104,128]{2,1,0:T(8,128)(2,1)} custom-call(s32[8]{0:T(128)} %lens.1, s32[1,256]{1,0:T(1,128)} %bitcast.52, s32[1,256]{1,0:T(1,128)} %bitcast.53, bf16[576,256]{1,0:T(8,128)(2,1)} %bitcast.49, bf16[8,576,128]{2,1,0:T(8,128)(2,1)} %bitcast.43), custom_call_target="tpu_custom_call" | custom-call | tf_op jit(solution)/shard_map/pallas_call | solution.py:81
  3.3 11.6 %all-to-all-start = ((bf16[32,104,128]{2,1,0:T(8,128)(2,1)}), bf16[32,104,128]{2,1,0:T(8,128)(2,1)S(1)}, u32[]{:S(2)}, u32[]{:S(2)}) async-start(bf16[32,104,128]{2,1,0:T(8,128)(2,1)} %shard_map.122), calls=%async_computation | async-start | bytes 1703936 | tf_op jit(solution)/shard_map/all_to_all | solution.py:350
  15.1 0.9 dynamic-slice_bitcast_fusion
  16.0 3.0 %collective-permute-start.2 = (bf16[2,64,576]{2,1,0:T(8,128)(2,1)}, bf16[2,64,576]{2,1,0:T(8,128)(2,1)S(1)}, u32[]{:S(2)}, u32[]{:S(2)}) collective-permute-start(bf16[2,64,576]{2,1,0:T(8,128)(2,1)} %get-tuple-element.48), channel_id=1, source_target_pairs={{0,3},{1,2},{2,1},{3,0},{4,7},{5,6},{6,5},{7,4},{8,11},{9,10},{10,... | collective-permute-start | bytes 442376 | tf_op jit(solution)/shard_map/ppermute | solution.py:310
  19.0 0.6 collective-permute-start.1
  19.6 0.5 collective-permute-start
  20.1 1.4 %pad_maximum_fusion.1 = bf16[4,4,640]{2,1,0:T(4,128)(2,1)} fusion(bf16[4,4,64]{2,1,0:T(4,128)(2,1)S(1)} %broadcast_in_dim.14, bf16[4,4,576]{2,1,0:T(4,128)(2,1)} %param.20), kind=kLoop, calls=%fused_computation.13 | loop fusion | flops 40960 | bytes 40960 | tf_op jit(solution)/shard_map/concatenate | solution.py:358
  21.5 1.1 maximum_bitcast_fusion
  22.6 0.6 constant_dynamic-slice_fusion.3
  23.2 0.5 dynamic_slice.36
  23.8 2.8 %shard_map.123._ = bf16[8,576,128]{2,1,0:T(8,128)(2,1)} custom-call(bf16[8,576,128]{2,1,0:T(8,128)(2,1)S(1)} %bitcast.44), custom_call_target="tpu_custom_call" | custom-call | tf_op jit(solution)/shard_map/pallas_call | solution.py:97
  26.5 0.7 copy.28
  27.2 0.7 reshape.53
  28.0 0.7 pad.5.refs_6_
  28.9 0.6 pad_add_fusion.info
  29.6 8.1 %all-to-all-done.landed = bf16[32,104,128]{2,1,0:T(8,128)(2,1)S(1)} async-done(((bf16[32,104,128]{2,1,0:T(8,128)(2,1)}), bf16[32,104,128]{2,1,0:T(8,128)(2,1)S(1)}, u32[]{:S(2)}, u32[]{:S(2)}) %all-to-all-start) | async-done | bytes 852000 | tf_op jit(solution)/shard_map/all_to_all | solution.py:350
  37.7 1.3 %shard_map.124 = (bf16[32,24,128]{2,1,0:T(8,128)(2,1)}, bf16[32,80,128]{2,1,0:T(8,128)(2,1)S(1)}) custom-call(s32[32]{0:T(128)S(1)} %copy-done.8, bf16[32,104,128]{2,1,0:T(8,128)(2,1)S(1)} %all-to-all-done.landed), custom_call_target="tpu_custom_call" | custom-call | tf_op jit(solution)/shard_map/pallas_call | solution.py:134
  39.0 3.0 %collective-permute-start.4 = (bf16[32,80,128]{2,1,0:T(8,128)(2,1)S(1)}, bf16[32,80,128]{2,1,0:T(8,128)(2,1)S(1)}, u32[]{:S(2)}, u32[]{:S(2)}) collective-permute-start(bf16[32,80,128]{2,1,0:T(8,128)(2,1)S(1)} %get-tuple-element.33.r0), channel_id=1, source_target_pairs={{0,3},{1,2},{2,1},{3,0},{4,7},{5,6},{6,5},{7,4},{8,11},{9,10},{10,... | collective-permute-start | bytes 1966088 | tf_op jit(solution)/shard_map/ppermute | solution.py:367
  42.1 0.6 dynamic-slice_bitcast_fusion.4
  42.8 0.6 constant_dynamic-slice_fusion
  43.4 1.5 %constant_dynamic-slice_fusion.1 = bf16[1,64,576]{2,1,0:T(8,128)(2,1)} fusion(bf16[2,64,576]{2,1,0:T(8,128)(2,1)} %copy-done.13, s32[]{:T(128)S(6)} %select_n.57), kind=kLoop, calls=%fused_computation.17 | loop fusion | bytes 147460 | tf_op jit(solution)/shard_map/jit(dynamic_index_in_dim)/dynamic_slice | solution.py:311
  44.9 1.5 %constant_dynamic-slice_fusion.2 = bf16[1,64,576]{2,1,0:T(8,128)(2,1)} fusion(bf16[2,64,576]{2,1,0:T(8,128)(2,1)} %copy-done.14, s32[]{:T(128)S(6)} %select_n.57), kind=kLoop, calls=%fused_computation.18 | loop fusion | bytes 147460 | tf_op jit(solution)/shard_map/jit(dynamic_index_in_dim)/dynamic_slice | solution.py:311
  46.5 1.4 %collective-permute-start.7 = (bf16[256,640]{1,0:T(8,128)(2,1)S(1)}, bf16[256,640]{1,0:T(8,128)(2,1)S(1)}, u32[]{:S(2)}, u32[]{:S(2)}) collective-permute-start(bf16[256,640]{1,0:T(8,128)(2,1)S(1)} %reshape.54.near), channel_id=1, source_target_pairs={{0,4},{1,5},{2,6},{3,7},{4,0},{5,1},{6,2},{7,3},{8,12},{9,13},{10,... | collective-permute-start | bytes 983048 | tf_op jit(solution)/shard_map/ppermute | solution.py:365
  47.8 6.4 %all-to-all-start.1 = ((bf16[32,24,128]{2,1,0:T(8,128)(2,1)}), bf16[32,24,128]{2,1,0:T(8,128)(2,1)S(1)}, u32[]{:S(2)}, u32[]{:S(2)}) async-start(bf16[32,24,128]{2,1,0:T(8,128)(2,1)} %get-tuple-element.31), calls=%async_computation.1 | async-start | bytes 393216 | tf_op jit(solution)/shard_map/all_to_all | solution.py:368
  54.3 3.5 %collective-permute-done.4.r2 = bf16[32,80,128]{2,1,0:T(8,128)(2,1)S(1)} collective-permute-done((bf16[32,80,128]{2,1,0:T(8,128)(2,1)S(1)}, bf16[32,80,128]{2,1,0:T(8,128)(2,1)S(1)}, u32[]{:S(2)}, u32[]{:S(2)}) %collective-permute-start.4) | collective-permute-done | bytes 655392 | tf_op jit(solution)/shard_map/ppermute | solution.py:367
  57.7 1.5 %collective-permute-done.3.r1 = bf16[32,80,128]{2,1,0:T(8,128)(2,1)S(1)} collective-permute-done((bf16[32,80,128]{2,1,0:T(8,128)(2,1)S(1)}, bf16[32,80,128]{2,1,0:T(8,128)(2,1)S(1)}, u32[]{:S(2)}, u32[]{:S(2)}) %collective-permute-start.3) | collective-permute-done | bytes 655392 | tf_op jit(solution)/shard_map/ppermute | solution.py:367
  59.2 0.8 slice.9
  60.0 0.8 slice.10
  60.7 1.5 %collective-permute-start.6 = (bf16[16,80,128]{2,1,0:T(8,128)(2,1)}, bf16[16,80,128]{2,1,0:T(8,128)(2,1)S(1)}, u32[]{:S(2)}, u32[]{:S(2)}) collective-permute-start(bf16[16,80,128]{2,1,0:T(8,128)(2,1)} %slice.10), channel_id=1, source_target_pairs={{0,3},{1,2},{2,1},{3,0},{4,7},{5,6},{6,5},{7,4},{8,11},{9,10},{10,... | collective-permute-start | bytes 983048 | tf_op jit(solution)/shard_map/ppermute | solution.py:372
  62.2 1.8 %pad_maximum_fusion = bf16[4,64,576]{2,1,0:T(8,128)(2,1)} fusion(bf16[1,64,576]{2,1,0:T(8,128)(2,1)} %constant_dynamic-slice_fusion, bf16[1,64,576]{2,1,0:T(8,128)(2,1)} %constant_dynamic-slice_fusion.1, bf16[1,64,576]{2,1,0:T(8,128)(2,1)} %constant_dynamic-slice_fusion.2, bf16[1,64,576]{2,1,0:T(8,128)(2,1)} %dynamic-slice_bitcast_fusion.4), kind=kLoop, calls=%fused_computation.6 | loop fusion | flops 442368 | bytes 589824 | tf_op jit(solution)/shard_map/stack | solution.py:311
  64.0 0.8 collective-permute-start.8
  64.9 0.7 shard_map.125
  65.5 8.1 %collective-permute-done.8.refs_4_ = bf16[4,64,576]{2,1,0:T(8,128)(2,1)} collective-permute-done((bf16[4,64,576]{2,1,0:T(8,128)(2,1)}, bf16[4,64,576]{2,1,0:T(8,128)(2,1)}, u32[]{:S(2)}, u32[]{:S(2)}) %collective-permute-start.8) | collective-permute-done | bytes 294944 | tf_op jit(solution)/shard_map/ppermute | solution.py:312
  73.7 4.4 %all-to-all-start.2 = ((bf16[8,576,128]{2,1,0:T(8,128)(2,1)}), bf16[8,576,128]{2,1,0:T(8,128)(2,1)}, u32[]{:S(2)}, u32[]{:S(2)}) async-start(bf16[8,576,128]{2,1,0:T(8,128)(2,1)} %shard_map.125), calls=%async_computation.2 | async-start | bytes 2359296 | tf_op jit(solution)/shard_map/all_to_all | solution.py:374
  78.1 0.6 slice_bitcast_fusion.refs_7_
  78.7 5.2 %shard_map.126 = (bf16[256,512]{1,0:T(8,128)(2,1)S(1)}, f32[16,256]{1,0:T(8,128)S(1)}, bf16[272,512]{1,0:T(8,128)(2,1)S(1)}) custom-call(s32[3]{0:T(128)S(1)} %pad_add_fusion.info, bf16[256,640]{1,0:T(8,128)(2,1)S(1)} %reshape.54.near, bf16[256,640]{1,0:T(8,128)(2,1)S(1)} %collective-permute-done.7.far, bf16[32,80,128]{2,1,0:T(8,128)(2,1)S(1)} %get-tuple-element.33.r0, ...), custom_call_target="tpu_custom_call" | custom-call | tf_op jit(solution)/shard_map/pallas_call | solution.py:263
  84.0 0.7 copy-done.3
  84.6 0.6 copy-done.5
  85.2 0.7 copy-done.9
  86.0 7.4 %all-to-all-done.2.refs_5_ = bf16[8,576,128]{2,1,0:T(8,128)(2,1)} async-done(((bf16[8,576,128]{2,1,0:T(8,128)(2,1)}), bf16[8,576,128]{2,1,0:T(8,128)(2,1)}, u32[]{:S(2)}, u32[]{:S(2)}) %all-to-all-start.2) | async-done | bytes 1179680 | tf_op jit(solution)/shard_map/all_to_all | solution.py:374
  93.4 4.8 %shard_map.127 = bf16[8,64,512]{2,1,0:T(8,128)(2,1)} custom-call(s32[3]{0:T(128)} %copy-done.7, bf16[2,64,576]{2,1,0:T(8,128)(2,1)} %get-tuple-element.26.refs_0_, bf16[2,64,576]{2,1,0:T(8,128)(2,1)} %copy-done.14, bf16[2,64,576]{2,1,0:T(8,128)(2,1)} %copy-done.13, bf16[2,64,576]{2,1,0:T(8,128)(2,1)} %copy-done.12, ...), custom_call_target="tpu_custom_call" | custom-call | tf_op jit(solution)/shard_map/pallas_call | solution.py:192
  98.2 3.6 %all-to-all-start.3 = ((bf16[8,64,512]{2,1,0:T(8,128)(2,1)}), bf16[8,64,512]{2,1,0:T(8,128)(2,1)S(1)}, u32[]{:S(2)}, u32[]{:S(2)}) async-start(bf16[8,64,512]{2,1,0:T(8,128)(2,1)} %shard_map.127), calls=%async_computation.3 | async-start | bytes 1048576 | tf_op jit(solution)/shard_map/all_to_all | solution.py:380
  101.9 2.0 %collective-permute-start.9 = (bf16[272,512]{1,0:T(8,128)(2,1)S(1)}, bf16[272,512]{1,0:T(8,128)(2,1)S(1)}, u32[]{:S(2)}, u32[]{:S(2)}) collective-permute-start(bf16[272,512]{1,0:T(8,128)(2,1)S(1)} %copy-done.10), channel_id=1, source_target_pairs={{0,4},{1,5},{2,6},{3,7},{4,0},{5,1},{6,2},{7,3},{8,12},{9,13},{10,... | collective-permute-start | bytes 835592 | tf_op jit(solution)/shard_map/ppermute | solution.py:377
  103.9 12.1 %collective-permute-done.9.far = bf16[272,512]{1,0:T(8,128)(2,1)S(1)} collective-permute-done((bf16[272,512]{1,0:T(8,128)(2,1)S(1)}, bf16[272,512]{1,0:T(8,128)(2,1)S(1)}, u32[]{:S(2)}, u32[]{:S(2)}) %collective-permute-start.9) | collective-permute-done | bytes 278560 | tf_op jit(solution)/shard_map/ppermute | solution.py:377
  116.0 0.5 shard_map.128
  116.5 0.7 reshape.58
  117.2 0.5 fusion.5
  117.8 0.7 copy.27
  (47 shorter events, 0.5 us)
Async XLA Ops:
  0.6 21.9 %copy-start = (bf16[4,8,576]{2,1,0:T(8,128)(2,1)S(1)}, bf16[4,8,576]{2,1,0:T(8,128)(2,1)}, u32[]{:S(2)}) copy-start(bf16[4,8,576]{2,1,0:T(8,128)(2,1)} %param.15) | copy-start | bytes 110596
  0.6 14.3 %copy-start.11 = (bf16[4,8,16,576]{3,2,1,0:T(8,128)(2,1)S(1)}, bf16[4,8,16,576]{3,2,1,0:T(8,128)(2,1)}, u32[]{:S(2)}) copy-start(bf16[4,8,16,576]{3,2,1,0:T(8,128)(2,1)} %param.14) | copy-start | bytes 1769476
  3.3 34.4 %all-to-all-start = ((bf16[32,104,128]{2,1,0:T(8,128)(2,1)}), bf16[32,104,128]{2,1,0:T(8,128)(2,1)S(1)}, u32[]{:S(2)}, u32[]{:S(2)}) async-start(bf16[32,104,128]{2,1,0:T(8,128)(2,1)} %shard_map.122), calls=%async_computation | async-start | bytes 1703936 | tf_op jit(solution)/shard_map/all_to_all | solution.py:350
  14.9 8.3 %copy-start.15 = (s32[8]{0:T(128)S(1)}, s32[8]{0:T(128)}, u32[]{:S(2)}) copy-start(s32[8]{0:T(128)} %lens.1) | copy-start | bytes 100
  14.9 8.8 %copy-start.2 = (bf16[8,128,576]{1,2,0:T(8,128)(2,1)S(1)}, bf16[8,128,576]{1,2,0:T(8,128)(2,1)}, u32[]{:S(2)}) copy-start(bf16[8,128,576]{1,2,0:T(8,128)(2,1)} %param.11) | copy-start | bytes 3538948
  16.0 13.6 %collective-permute-start.2 = (bf16[2,64,576]{2,1,0:T(8,128)(2,1)}, bf16[2,64,576]{2,1,0:T(8,128)(2,1)S(1)}, u32[]{:S(2)}, u32[]{:S(2)}) collective-permute-start(bf16[2,64,576]{2,1,0:T(8,128)(2,1)} %get-tuple-element.48), channel_id=1, source_target_pairs={{0,3},{1,2},{2,1},{3,0},{4,7},{5,6},{6,5},{7,4},{8,11},{9,10},{10,... | collective-permute-start | bytes 442376 | tf_op jit(solution)/shard_map/ppermute | solution.py:310
  19.0 10.6 %collective-permute-start.1 = (bf16[2,64,576]{2,1,0:T(8,128)(2,1)}, bf16[2,64,576]{2,1,0:T(8,128)(2,1)S(1)}, u32[]{:S(2)}, u32[]{:S(2)}) collective-permute-start(bf16[2,64,576]{2,1,0:T(8,128)(2,1)} %get-tuple-element.49), channel_id=1, source_target_pairs={{0,2},{1,3},{2,0},{3,1},{4,6},{5,7},{6,4},{7,5},{8,10},{9,11},{10,... | collective-permute-start | bytes 442376 | tf_op jit(solution)/shard_map/ppermute | solution.py:310
  19.6 9.9 %collective-permute-start = (bf16[2,64,576]{2,1,0:T(8,128)(2,1)}, bf16[2,64,576]{2,1,0:T(8,128)(2,1)S(1)}, u32[]{:S(2)}, u32[]{:S(2)}) collective-permute-start(bf16[2,64,576]{2,1,0:T(8,128)(2,1)} %get-tuple-element.50), channel_id=1, source_target_pairs={{0,1},{1,0},{2,3},{3,2},{4,5},{5,4},{6,7},{7,6},{8,9},{9,8},{10,11... | collective-permute-start | bytes 442376 | tf_op jit(solution)/shard_map/ppermute | solution.py:310
  22.6 15.1 %copy-start.8 = (s32[32]{0:T(128)S(1)}, s32[32]{0:T(128)}, u32[]{:S(2)}) copy-start(s32[32]{0:T(128)} %partner.1) | copy-start | bytes 388
  29.5 49.2 %copy-start.7 = (s32[3]{0:T(128)}, s32[3]{0:T(128)S(1)}, u32[]{:S(2)}) copy-start(s32[3]{0:T(128)S(1)} %pad_add_fusion.info) | copy-start | bytes 40
  29.5 36.0 %copy-start.12 = (bf16[2,64,576]{2,1,0:T(8,128)(2,1)}, bf16[2,64,576]{2,1,0:T(8,128)(2,1)S(1)}, u32[]{:S(2)}) copy-start(bf16[2,64,576]{2,1,0:T(8,128)(2,1)S(1)} %collective-permute-done.2.refs_3_) | copy-start | bytes 442372
  29.5 9.4 %copy-start.13 = (bf16[2,64,576]{2,1,0:T(8,128)(2,1)}, bf16[2,64,576]{2,1,0:T(8,128)(2,1)S(1)}, u32[]{:S(2)}) copy-start(bf16[2,64,576]{2,1,0:T(8,128)(2,1)S(1)} %collective-permute-done.1.refs_2_) | copy-start | bytes 442372
  29.6 9.4 %copy-start.14 = (bf16[2,64,576]{2,1,0:T(8,128)(2,1)}, bf16[2,64,576]{2,1,0:T(8,128)(2,1)S(1)}, u32[]{:S(2)}) copy-start(bf16[2,64,576]{2,1,0:T(8,128)(2,1)S(1)} %collective-permute-done.refs_1_) | copy-start | bytes 442372
  39.0 18.8 %collective-permute-start.4 = (bf16[32,80,128]{2,1,0:T(8,128)(2,1)S(1)}, bf16[32,80,128]{2,1,0:T(8,128)(2,1)S(1)}, u32[]{:S(2)}, u32[]{:S(2)}) collective-permute-start(bf16[32,80,128]{2,1,0:T(8,128)(2,1)S(1)} %get-tuple-element.33.r0), channel_id=1, source_target_pairs={{0,3},{1,2},{2,1},{3,0},{4,7},{5,6},{6,5},{7,4},{8,11},{9,10},{10,... | collective-permute-start | bytes 1966088 | tf_op jit(solution)/shard_map/ppermute | solution.py:367
  42.0 17.2 %collective-permute-start.3 = (bf16[32,80,128]{2,1,0:T(8,128)(2,1)S(1)}, bf16[32,80,128]{2,1,0:T(8,128)(2,1)S(1)}, u32[]{:S(2)}, u32[]{:S(2)}) collective-permute-start(bf16[32,80,128]{2,1,0:T(8,128)(2,1)S(1)} %get-tuple-element.33.r0), channel_id=1, source_target_pairs={{0,1},{1,0},{2,3},{3,2},{4,5},{5,4},{6,7},{7,6},{8,9},{9,8},{10,11... | collective-permute-start | bytes 1966088 | tf_op jit(solution)/shard_map/ppermute | solution.py:367
  46.5 27.2 %collective-permute-start.7 = (bf16[256,640]{1,0:T(8,128)(2,1)S(1)}, bf16[256,640]{1,0:T(8,128)(2,1)S(1)}, u32[]{:S(2)}, u32[]{:S(2)}) collective-permute-start(bf16[256,640]{1,0:T(8,128)(2,1)S(1)} %reshape.54.near), channel_id=1, source_target_pairs={{0,4},{1,5},{2,6},{3,7},{4,0},{5,1},{6,2},{7,3},{8,12},{9,13},{10,... | collective-permute-start | bytes 983048 | tf_op jit(solution)/shard_map/ppermute | solution.py:365
  47.8 17.0 %all-to-all-start.1 = ((bf16[32,24,128]{2,1,0:T(8,128)(2,1)}), bf16[32,24,128]{2,1,0:T(8,128)(2,1)S(1)}, u32[]{:S(2)}, u32[]{:S(2)}) async-start(bf16[32,24,128]{2,1,0:T(8,128)(2,1)} %get-tuple-element.31), calls=%async_computation.1 | async-start | bytes 393216 | tf_op jit(solution)/shard_map/all_to_all | solution.py:368
  60.7 12.9 %collective-permute-start.6 = (bf16[16,80,128]{2,1,0:T(8,128)(2,1)}, bf16[16,80,128]{2,1,0:T(8,128)(2,1)S(1)}, u32[]{:S(2)}, u32[]{:S(2)}) collective-permute-start(bf16[16,80,128]{2,1,0:T(8,128)(2,1)} %slice.10), channel_id=1, source_target_pairs={{0,3},{1,2},{2,1},{3,0},{4,7},{5,6},{6,5},{7,4},{8,11},{9,10},{10,... | collective-permute-start | bytes 983048 | tf_op jit(solution)/shard_map/ppermute | solution.py:372
  62.2 11.4 %collective-permute-start.5 = (bf16[16,80,128]{2,1,0:T(8,128)(2,1)}, bf16[16,80,128]{2,1,0:T(8,128)(2,1)}, u32[]{:S(2)}, u32[]{:S(2)}) collective-permute-start(bf16[16,80,128]{2,1,0:T(8,128)(2,1)} %slice.9), channel_id=1, source_target_pairs={{0,1},{1,0},{2,3},{3,2},{4,5},{5,4},{6,7},{7,6},{8,9},{9,8},{10,11... | collective-permute-start | bytes 983048 | tf_op jit(solution)/shard_map/ppermute | solution.py:371
  64.0 9.6 %collective-permute-start.8 = (bf16[4,64,576]{2,1,0:T(8,128)(2,1)}, bf16[4,64,576]{2,1,0:T(8,128)(2,1)}, u32[]{:S(2)}, u32[]{:S(2)}) collective-permute-start(bf16[4,64,576]{2,1,0:T(8,128)(2,1)} %pad_maximum_fusion), channel_id=1, source_target_pairs={{0,4},{1,5},{2,6},{3,7},{4,0},{5,1},{6,2},{7,3},{8,12},{9,13},{10,... | collective-permute-start | bytes 884744 | tf_op jit(solution)/shard_map/ppermute | solution.py:312
  73.7 19.7 %all-to-all-start.2 = ((bf16[8,576,128]{2,1,0:T(8,128)(2,1)}), bf16[8,576,128]{2,1,0:T(8,128)(2,1)}, u32[]{:S(2)}, u32[]{:S(2)}) async-start(bf16[8,576,128]{2,1,0:T(8,128)(2,1)} %shard_map.125), calls=%async_computation.2 | async-start | bytes 2359296 | tf_op jit(solution)/shard_map/all_to_all | solution.py:374
  83.9 0.7 copy-start.3
  84.6 0.6 copy-start.5
  85.2 0.7 copy-start.9
  86.0 30.0 %copy-start.1 = (bf16[16,512,128]{2,1,0:T(8,128)(2,1)S(1)}, bf16[16,512,128]{2,1,0:T(8,128)(2,1)}, u32[]{:S(2)}) copy-start(bf16[16,512,128]{2,1,0:T(8,128)(2,1)} %value_up.1) | copy-start | bytes 6291460
  93.4 8.5 %copy-start.10 = (bf16[272,512]{1,0:T(8,128)(2,1)S(1)}, bf16[272,512]{1,0:T(8,128)(2,1)}, u32[]{:S(2)}) copy-start(bf16[272,512]{1,0:T(8,128)(2,1)} %copy-done.9) | copy-start | bytes 835588
  93.4 22.6 %copy-start.4 = (bf16[256,512]{1,0:T(8,128)(2,1)S(1)}, bf16[256,512]{1,0:T(8,128)(2,1)}, u32[]{:S(2)}) copy-start(bf16[256,512]{1,0:T(8,128)(2,1)} %copy-done.3) | copy-start | bytes 786436
  93.4 22.6 %copy-start.6 = (f32[16,256]{1,0:T(8,128)S(1)}, f32[16,256]{1,0:T(8,128)}, u32[]{:S(2)}) copy-start(f32[16,256]{1,0:T(8,128)} %copy-done.5) | copy-start | bytes 49156
  98.2 19.0 %all-to-all-start.3 = ((bf16[8,64,512]{2,1,0:T(8,128)(2,1)}), bf16[8,64,512]{2,1,0:T(8,128)(2,1)S(1)}, u32[]{:S(2)}, u32[]{:S(2)}) async-start(bf16[8,64,512]{2,1,0:T(8,128)(2,1)} %shard_map.127), calls=%async_computation.3 | async-start | bytes 1048576 | tf_op jit(solution)/shard_map/all_to_all | solution.py:380
  101.9 14.1 %collective-permute-start.9 = (bf16[272,512]{1,0:T(8,128)(2,1)S(1)}, bf16[272,512]{1,0:T(8,128)(2,1)S(1)}, u32[]{:S(2)}, u32[]{:S(2)}) collective-permute-start(bf16[272,512]{1,0:T(8,128)(2,1)S(1)} %copy-done.10), channel_id=1, source_target_pairs={{0,4},{1,5},{2,6},{3,7},{4,0},{5,1},{6,2},{7,3},{8,12},{9,13},{10,... | collective-permute-start | bytes 835592 | tf_op jit(solution)/shard_map/ppermute | solution.py:377

commit v3 on v2

--- a/solution.py
+++ b/solution.py
@@ -120,22 +120,24 @@
     )(moved, cache)
 
 
-def forward_kernel(partner, landed, out, rows):
+def forward_kernel(partner, landed, out, low, high):
     for d in range(N_INST):
         out[d] = landed[partner[d], ROWS_SENT:, :]
-    rows[...] = landed[:, :ROWS_SENT, :]
+    low[...] = landed[: N_INST // 2, :ROWS_SENT, :]
+    high[...] = landed[N_INST // 2 :, :ROWS_SENT, :]
 
 
 def forward(partner, landed):
     shapes = (
         jax.ShapeDtypeStruct((N_INST, PIECE, LANES), BF),
-        jax.ShapeDtypeStruct((N_INST, ROWS_SENT, LANES), BF),
+        jax.ShapeDtypeStruct((N_INST // 2, ROWS_SENT, LANES), BF),
+        jax.ShapeDtypeStruct((N_INST // 2, ROWS_SENT, LANES), BF),
     )
     return pl.pallas_call(
         forward_kernel,
         out_shape=shapes,
         in_specs=[smem(), vmem()],
-        out_specs=(vmem(),) * 2,
+        out_specs=(vmem(),) * 3,
         compiler_params=params(),
     )(partner, landed)
 
@@ -205,9 +207,10 @@
     )(info, *inputs)
 
 
-def arrival_kernel(info, near, far, r0, r1, r2, r3, r4, tail, out_near, stat_near, out_far, keys):
+def arrival_kernel(info, near, far, tail, *refs):
+    row_blocks, (out_near, stat_near, out_far, keys) = refs[:-4], refs[-4:]
     start = 0
-    for r in (r0, r1, r2, r3, r4):
+    for r in row_blocks:
         count = r.shape[0] * CAP
         for t in range(KX // LANES):
             keys[start : start + count, t * LANES : (t + 1) * LANES] = r[
@@ -259,7 +262,7 @@
         jax.ShapeDtypeStruct((CAP, n), F32),
         jax.ShapeDtypeStruct((n + CAP, LATENT), BF),
     )
-    inputs = (near, far, *rows, tail)
+    inputs = (near, far, tail, *rows)
     return pl.pallas_call(
         arrival_kernel,
         out_shape=shapes,
@@ -308,8 +311,7 @@
     for d in range(N_Y):
         block = lax.dynamic_index_in_dim(paired, y ^ d, 1, keepdims=False)
         across.append(block if d == 0 else lax.ppermute(block, "head", xor_pairs(d)))
-    beyond = jnp.stack([lax.dynamic_index_in_dim(b, 1 - side, 0, keepdims=False) for b in across])
-    return across, lax.ppermute(beyond, "head", xor_pairs(N_Y))
+    return across, jnp.stack([lax.dynamic_index_in_dim(b, 1 - side, 0, keepdims=False) for b in across])
 
 
 def local(
@@ -358,24 +360,26 @@
     new_tail = jnp.concatenate([new_step_rows, mark], -1).reshape(steps * new_count, KX)
     blank = jnp.full((LANES - steps * new_count, KX), 0.0, BF)
     new_tail = jnp.concatenate([new_tail, blank], 0)
-    landed, full, info, tail, new_tail, near, *across = lax.optimization_barrier(
-        (landed, full, info, tail, new_tail, near, *across)
-    )
-    pieces, rows = forward(partner, landed)
+    landed, full, info, tail, new_tail, near, beyond, *across = lax.optimization_barrier(
+        (landed, full, info, tail, new_tail, near, beyond, *across)
+    )
+    beyond = lax.ppermute(beyond, "head", xor_pairs(N_Y))
+    pieces, low, high = forward(partner, landed)
     far = lax.ppermute(near, "head", xor_pairs(N_Y))
-    half = N_INST // 2
-    r1, r3 = (lax.ppermute(rows, "head", xor_pairs(d)) for d in (1, 3))
+    low3 = lax.ppermute(low, "head", xor_pairs(3))
+    high1 = lax.ppermute(high, "head", xor_pairs(1))
     moved = lax.all_to_all(pieces, "inst", split_axis=0, concat_axis=0, tiled=True)
     full = settle(moved.reshape(-1, LANES), full)
-    r1, r3 = lax.optimization_barrier((r1, r3))
-    f1 = lax.ppermute(r3[:half], "head", xor_pairs(1))
-    f3 = lax.ppermute(r1[half:], "head", xor_pairs(3))
-    full, f1, f3, far, beyond = lax.optimization_barrier((full, f1, f3, far, beyond))
+    f1 = lax.ppermute(low3, "head", xor_pairs(1))
+    f3 = lax.ppermute(high1, "head", xor_pairs(3))
+    low1 = lax.ppermute(low, "head", xor_pairs(1))
+    high3 = lax.ppermute(high, "head", xor_pairs(3))
+    full, f1, f3, low1, high3, far, beyond = lax.optimization_barrier((full, f1, f3, low1, high3, far, beyond))
     keys = lax.all_to_all(full, "head", split_axis=0, concat_axis=0, tiled=True)
-    row_blocks = (rows, r1, r3, f1, f3)
+    row_blocks = (low, high, low1, high1, low3, high3, f1, f3)
     out_near, stat_near, out_far = arrival(info, near, far, row_blocks, new_tail)
     got = lax.ppermute(out_far, "head", xor_pairs(N_Y))
-    keys, out_far = lax.optimization_barrier((keys, out_far))
+    keys, got = lax.optimization_barrier((keys, got))
     lat = resident(info, across, beyond, keys, tail, moved[PIECES])
     lat = lax.all_to_all(lat, "head", split_axis=0, concat_axis=0, tiled=True)
     lat = lat.reshape(count, steps, heads, LATENT)

time: 120 us -> 115 us (0.958)
  local copies, waits for them, and re-layouts: 14.3 us -> 5.3 us
  starting transfers between devices: 39.1 us -> 42.3 us
  waiting for transfers between devices: 40.8 us -> 43.4 us
  other arithmetic: 4.9 us -> 2.71 us
    all_to_all x1, waiting for transfers between devices: 7.44 us -> 0.01 us  [local(): keys = lax.all_to_all(full, 'head', split_axis=0, concat_axis=0, tiled=True)]
    all_to_all x1, waiting for transfers between devices: 0.01 us -> 7.15 us  [local(): lat = lax.all_to_all(lat, 'head', split_axis=0, concat_axis=0, tiled=True)]
    ppermute x5 -> x7, waiting for transfers between devices: 13.1 us -> 6.96 us  [the longest x1 3.35 us: local(): f1 = lax.ppermute(low3, 'head', xor_pairs(1))]
    dynamic_slice x4, local copies, waits for them, and re-layouts: 4.31 us -> 0.03 us  [spread(): lax.dynamic_index_in_dim(b, 1 - side, 0, keepdims=False)]
    ppermute x1, waiting for transfers between devices: 0.01 us -> 3.79 us  [local(): far = lax.ppermute(near, 'head', xor_pairs(N_Y))]
    ppermute x5 -> x7, starting transfers between devices: 5.48 us -> 9.2 us  [the longest x1 3.01 us: local(): low3 = lax.ppermute(low, 'head', xor_pairs(3))]
    all_to_all x1, waiting for transfers between devices: 0.01 us -> 3.27 us  [local(): lax.all_to_all(pieces, 'inst', split_axis=0, concat_axis=0, tiled=True)]
    unnamed x34 -> x28, local copies, waits for them, and re-layouts: 2.83 us -> 0.82 us
  transfers between devices with their start and end apart: 14 -> 16, of which waited for: 6 -> 11; matrix products, arithmetic and copies ran while one was open for 14% -> 6% of each run, Pallas kernels for 8% -> 8%
where the time goes in v3:
time: 115 us; the launch traced here: 114 us
  waiting for transfers between devices  43.4 us (38%)
  starting transfers between devices  42.3 us (37%)
  Pallas kernels  18 us (16%)
  local copies, waits for them, and re-layouts  5.3 us (5%)
  other arithmetic  2.71 us (2%)
  matrix products  1.62 us (1%)
    ppermute x1, waiting for transfers between devices, local(): got = lax.ppermute(out_far, 'head', xor_pairs(N_Y))  11.8 us
    all_to_all x1, starting transfers between devices, local(): lax.all_to_all(sent, 'inst', split_axis=0, concat_axis=0, tiled=True)  11.7 us
    all_to_all x1, waiting for transfers between devices, local(): lax.all_to_all(sent, 'inst', split_axis=0, concat_axis=0, tiled=True)  9.06 us
    all_to_all x1, waiting for transfers between devices, local(): lat = lax.all_to_all(lat, 'head', split_axis=0, concat_axis=0, tiled=True)  7.15 us
    all_to_all x1, starting transfers between devices, local(): lax.all_to_all(pieces, 'inst', split_axis=0, concat_axis=0, tiled=True)  6.4 us
    pallas_call x1, Pallas kernels, arrival(): pl.pallas_call(arrival_kernel, out_shape=shapes, in_specs=[smem()] + [vme...  5.35 us
    pallas_call x1, Pallas kernels, resident(): pl.pallas_call(resident_kernel, out_shape=shape, in_specs=[smem()] + [who...  4.78 us
    all_to_all x1, starting transfers between devices, local(): keys = lax.all_to_all(full, 'head', split_axis=0, concat_axis=0, tiled=True)  4.44 us
  transfers between devices with their start and end apart: 16, of which 11 were waited for; matrix products, arithmetic and copies ran while one was open for 6% of the time, Pallas kernels for 8%

profile of v3, /device:TPU:6, one launch (start us, length us, event | category | flops | bytes accessed | tf_op | source)
XLA Modules:
  0.0 114.2 jit_solution(3838381563303447046)
XLA Ops:
  0.7 2.7 %shard_map.122 = bf16[32,104,128]{2,1,0:T(8,128)(2,1)} custom-call(s32[8]{0:T(128)} %lens.1, s32[1,256]{1,0:T(1,128)} %bitcast.51, s32[1,256]{1,0:T(1,128)} %bitcast.52, bf16[576,256]{1,0:T(8,128)(2,1)} %bitcast.48, bf16[8,576,128]{2,1,0:T(8,128)(2,1)} %bitcast.43), custom_call_target="tpu_custom_call" | custom-call | tf_op jit(solution)/shard_map/pallas_call | solution.py:81
  3.3 11.7 %all-to-all-start = ((bf16[32,104,128]{2,1,0:T(8,128)(2,1)}), bf16[32,104,128]{2,1,0:T(8,128)(2,1)S(1)}, u32[]{:S(2)}, u32[]{:S(2)}) async-start(bf16[32,104,128]{2,1,0:T(8,128)(2,1)} %shard_map.122), calls=%async_computation | async-start | bytes 1703936 | tf_op jit(solution)/shard_map/all_to_all | solution.py:352
  15.2 0.9 dynamic-slice_bitcast_fusion
  16.1 3.0 %collective-permute-start.2 = (bf16[2,64,576]{2,1,0:T(8,128)(2,1)}, bf16[2,64,576]{2,1,0:T(8,128)(2,1)S(1)}, u32[]{:S(2)}, u32[]{:S(2)}) collective-permute-start(bf16[2,64,576]{2,1,0:T(8,128)(2,1)} %get-tuple-element.55), channel_id=1, source_target_pairs={{0,3},{1,2},{2,1},{3,0},{4,7},{5,6},{6,5},{7,4},{8,11},{9,10},{10,... | collective-permute-start | bytes 442376 | tf_op jit(solution)/shard_map/ppermute | solution.py:313
  19.1 0.6 collective-permute-start.1
  19.7 0.5 collective-permute-start
  20.2 0.1 pad_maximum_fusion.1
  20.3 1.1 maximum_bitcast_fusion
  21.5 0.7 dynamic_slice.36
  22.1 0.8 pad_add_fusion.info
  22.9 2.7 %shard_map.123._ = bf16[8,576,128]{2,1,0:T(8,128)(2,1)} custom-call(bf16[8,576,128]{2,1,0:T(8,128)(2,1)S(1)} %bitcast.44), custom_call_target="tpu_custom_call" | custom-call | tf_op jit(solution)/shard_map/pallas_call | solution.py:97
  25.7 0.7 pad.5.refs_6_
  26.3 0.1 copy.16
  26.5 0.1 reshape.54.near
  26.6 0.2 collective-permute-done.2.refs_3_
  26.8 1.1 collective-permute-done.1.refs_2_
  28.0 0.8 pad_maximum_fusion
  28.8 9.1 %all-to-all-done.landed = bf16[32,104,128]{2,1,0:T(8,128)(2,1)S(1)} async-done(((bf16[32,104,128]{2,1,0:T(8,128)(2,1)}), bf16[32,104,128]{2,1,0:T(8,128)(2,1)S(1)}, u32[]{:S(2)}, u32[]{:S(2)}) %all-to-all-start) | async-done | bytes 852000 | tf_op jit(solution)/shard_map/all_to_all | solution.py:352
  37.8 1.3 %shard_map.124 = (bf16[32,24,128]{2,1,0:T(8,128)(2,1)}, bf16[16,80,128]{2,1,0:T(8,128)(2,1)S(1)}, bf16[16,80,128]{2,1,0:T(8,128)(2,1)S(1)}) custom-call(s32[32]{0:T(128)S(1)} %copy-done.6, bf16[32,104,128]{2,1,0:T(8,128)(2,1)S(1)} %all-to-all-done.landed), custom_call_target="tpu_custom_call" | custom-call | tf_op jit(solution)/shard_map/pallas_call | solution.py:136
  39.1 3.0 %collective-permute-start.3 = (bf16[16,80,128]{2,1,0:T(8,128)(2,1)S(1)}, bf16[16,80,128]{2,1,0:T(8,128)(2,1)S(1)}, u32[]{:S(2)}, u32[]{:S(2)}) collective-permute-start(bf16[16,80,128]{2,1,0:T(8,128)(2,1)S(1)} %get-tuple-element.36.refs_0_), channel_id=1, source_target_pairs={{0,3},{1,2},{2,1},{3,0},{4,7},{5,6},{6,5},{7,4},{8,11},{9,10},{10,... | collective-permute-start | bytes 983048 | tf_op jit(solution)/shard_map/ppermute | solution.py:369
  42.1 0.1 collective-permute-start.5
  42.3 1.4 %collective-permute-start.10 = (bf16[4,64,576]{2,1,0:T(8,128)(2,1)}, bf16[4,64,576]{2,1,0:T(8,128)(2,1)}, u32[]{:S(2)}, u32[]{:S(2)}) collective-permute-start(bf16[4,64,576]{2,1,0:T(8,128)(2,1)} %pad_maximum_fusion), channel_id=1, source_target_pairs={{0,4},{1,5},{2,6},{3,7},{4,0},{5,1},{6,2},{7,3},{8,12},{9,13},{10,... | collective-permute-start | bytes 884744 | tf_op jit(solution)/shard_map/ppermute | solution.py:366
  43.6 6.4 %all-to-all-start.1 = ((bf16[32,24,128]{2,1,0:T(8,128)(2,1)}), bf16[32,24,128]{2,1,0:T(8,128)(2,1)S(1)}, u32[]{:S(2)}, u32[]{:S(2)}) async-start(bf16[32,24,128]{2,1,0:T(8,128)(2,1)} %get-tuple-element.34), calls=%async_computation.1 | async-start | bytes 393216 | tf_op jit(solution)/shard_map/all_to_all | solution.py:371
  50.1 2.0 %collective-permute-start.7 = (bf16[16,80,128]{2,1,0:T(8,128)(2,1)S(1)}, bf16[16,80,128]{2,1,0:T(8,128)(2,1)S(1)}, u32[]{:S(2)}, u32[]{:S(2)}) collective-permute-start(bf16[16,80,128]{2,1,0:T(8,128)(2,1)S(1)} %get-tuple-element.36.refs_0_), channel_id=1, source_target_pairs={{0,1},{1,0},{2,3},{3,2},{4,5},{5,4},{6,7},{7,6},{8,9},{9,8},{10,11... | collective-permute-start | bytes 983048 | tf_op jit(solution)/shard_map/ppermute | solution.py:375
  52.0 0.2 collective-permute-start.8
  52.2 0.8 collective-permute-done.10.refs_4_
  53.1 0.5 collective-permute-start.9
  53.6 1.6 %collective-permute-start.4 = (bf16[16,80,128]{2,1,0:T(8,128)(2,1)S(1)}, bf16[16,80,128]{2,1,0:T(8,128)(2,1)}, u32[]{:S(2)}, u32[]{:S(2)}) collective-permute-start(bf16[16,80,128]{2,1,0:T(8,128)(2,1)S(1)} %collective-permute-done.3.refs_4_), channel_id=1, source_target_pairs={{0,1},{1,0},{2,3},{3,2},{4,5},{5,4},{6,7},{7,6},{8,9},{9,8},{10,11... | collective-permute-start | bytes 983048 | tf_op jit(solution)/shard_map/ppermute | solution.py:373
  55.2 0.8 collective-permute-start.6
  56.0 3.3 %all-to-all-done.1 = bf16[32,24,128]{2,1,0:T(8,128)(2,1)S(1)} async-done(((bf16[32,24,128]{2,1,0:T(8,128)(2,1)}), bf16[32,24,128]{2,1,0:T(8,128)(2,1)S(1)}, u32[]{:S(2)}, u32[]{:S(2)}) %all-to-all-start.1) | async-done | bytes 196640 | tf_op jit(solution)/shard_map/all_to_all | solution.py:371
  59.3 0.7 shard_map.125
  60.0 3.8 %collective-permute-done.9.far = bf16[256,640]{1,0:T(8,128)(2,1)S(1)} collective-permute-done((bf16[256,640]{1,0:T(8,128)(2,1)S(1)}, bf16[256,640]{1,0:T(8,128)(2,1)S(1)}, u32[]{:S(2)}, u32[]{:S(2)}) %collective-permute-start.9) | collective-permute-done | bytes 327712 | tf_op jit(solution)/shard_map/ppermute | solution.py:368
  63.8 0.1 collective-permute-done.8.refs_5_
  63.8 3.3 %collective-permute-done.4.refs_6_ = bf16[16,80,128]{2,1,0:T(8,128)(2,1)} collective-permute-done((bf16[16,80,128]{2,1,0:T(8,128)(2,1)S(1)}, bf16[16,80,128]{2,1,0:T(8,128)(2,1)}, u32[]{:S(2)}, u32[]{:S(2)}) %collective-permute-start.4) | collective-permute-done | bytes 327712 | tf_op jit(solution)/shard_map/ppermute | solution.py:373
  67.2 2.7 %collective-permute-done.6.refs_7_ = bf16[16,80,128]{2,1,0:T(8,128)(2,1)} collective-permute-done((bf16[16,80,128]{2,1,0:T(8,128)(2,1)S(1)}, bf16[16,80,128]{2,1,0:T(8,128)(2,1)}, u32[]{:S(2)}, u32[]{:S(2)}) %collective-permute-start.6) | collective-permute-done | bytes 327712 | tf_op jit(solution)/shard_map/ppermute | solution.py:374
  69.9 4.4 %all-to-all-start.2 = ((bf16[8,576,128]{2,1,0:T(8,128)(2,1)}), bf16[8,576,128]{2,1,0:T(8,128)(2,1)}, u32[]{:S(2)}, u32[]{:S(2)}) async-start(bf16[8,576,128]{2,1,0:T(8,128)(2,1)} %shard_map.125), calls=%async_computation.2 | async-start | bytes 2359296 | tf_op jit(solution)/shard_map/all_to_all | solution.py:378
  74.3 5.3 %shard_map.126 = (bf16[256,512]{1,0:T(8,128)(2,1)S(1)}, f32[16,256]{1,0:T(8,128)S(1)}, bf16[272,512]{1,0:T(8,128)(2,1)S(1)}) custom-call(s32[3]{0:T(128)S(1)} %pad_add_fusion.info, bf16[256,640]{1,0:T(8,128)(2,1)S(1)} %reshape.54.near, bf16[256,640]{1,0:T(8,128)(2,1)S(1)} %collective-permute-done.9.far, bf16[128,640]{1,0:T(8,128)(2,1)S(1)} %concatenate.10.tail, ...), custom_call_target="tpu_custom_call" | custom-call | tf_op jit(solution)/shard_map/pallas_call | solution.py:266
  79.7 0.7 copy-done.3
  80.4 1.7 %collective-permute-start.11 = (bf16[272,512]{1,0:T(8,128)(2,1)S(1)}, bf16[272,512]{1,0:T(8,128)(2,1)S(1)}, u32[]{:S(2)}, u32[]{:S(2)}) collective-permute-start(bf16[272,512]{1,0:T(8,128)(2,1)S(1)} %get-tuple-element.48), channel_id=1, source_target_pairs={{0,4},{1,5},{2,6},{3,7},{4,0},{5,1},{6,2},{7,3},{8,12},{9,13},{10,... | collective-permute-start | bytes 835592 | tf_op jit(solution)/shard_map/ppermute | solution.py:381
  82.1 0.6 slice_bitcast_fusion.refs_7_
  82.7 11.8 %collective-permute-done.11.far = bf16[272,512]{1,0:T(8,128)(2,1)S(1)} collective-permute-done((bf16[272,512]{1,0:T(8,128)(2,1)S(1)}, bf16[272,512]{1,0:T(8,128)(2,1)S(1)}, u32[]{:S(2)}, u32[]{:S(2)}) %collective-permute-start.11) | collective-permute-done | bytes 278560 | tf_op jit(solution)/shard_map/ppermute | solution.py:381
  94.5 4.8 %shard_map.127 = bf16[8,64,512]{2,1,0:T(8,128)(2,1)} custom-call(s32[3]{0:T(128)} %copy-done.5, bf16[2,64,576]{2,1,0:T(8,128)(2,1)} %get-tuple-element.29.refs_0_, bf16[2,64,576]{2,1,0:T(8,128)(2,1)} %copy-done.10, bf16[2,64,576]{2,1,0:T(8,128)(2,1)} %copy-done.9, bf16[2,64,576]{2,1,0:T(8,128)(2,1)} %copy-done.8, ...), custom_call_target="tpu_custom_call" | custom-call | tf_op jit(solution)/shard_map/pallas_call | solution.py:194
  99.3 4.3 %all-to-all-start.3 = ((bf16[8,64,512]{2,1,0:T(8,128)(2,1)}), bf16[8,64,512]{2,1,0:T(8,128)(2,1)}, u32[]{:S(2)}, u32[]{:S(2)}) async-start(bf16[8,64,512]{2,1,0:T(8,128)(2,1)} %shard_map.127), calls=%async_computation.3 | async-start | bytes 1048576 | tf_op jit(solution)/shard_map/all_to_all | solution.py:384
  103.5 0.5 shard_map.128
  104.1 0.7 reshape.58
  104.8 7.2 %all-to-all-done.3 = bf16[8,64,512]{2,1,0:T(8,128)(2,1)} async-done(((bf16[8,64,512]{2,1,0:T(8,128)(2,1)}), bf16[8,64,512]{2,1,0:T(8,128)(2,1)}, u32[]{:S(2)}, u32[]{:S(2)}) %all-to-all-start.3) | async-done | bytes 524320 | tf_op jit(solution)/shard_map/all_to_all | solution.py:384
  111.9 1.6 %fusion.5 = bf16[16,4,1,8,128]{4,3,2,1,0:T(8,128)(2,1)S(1)} fusion(bf16[16,512,128]{2,1,0:T(8,128)(2,1)S(1)} %copy-done.1, bf16[8,4,16,512]{3,2,1,0:T(8,128)(2,1)} %bitcast.17), kind=kOutput, calls=%fused_computation.3 | convolution fusion | flops 67174400 | bytes 2752512 | tf_op jit(solution)/shard_map/rshc,hcv->srhv/dot_general | solution.py:386
  113.5 0.7 copy.27
  (43 shorter events, 0.3 us)
Async XLA Ops:
  0.6 20.8 %copy-start = (bf16[4,8,576]{2,1,0:T(8,128)(2,1)S(1)}, bf16[4,8,576]{2,1,0:T(8,128)(2,1)}, u32[]{:S(2)}) copy-start(bf16[4,8,576]{2,1,0:T(8,128)(2,1)} %param.15) | copy-start | bytes 110596
  0.6 14.5 %copy-start.7 = (bf16[4,8,16,576]{3,2,1,0:T(8,128)(2,1)S(1)}, bf16[4,8,16,576]{3,2,1,0:T(8,128)(2,1)}, u32[]{:S(2)}) copy-start(bf16[4,8,16,576]{3,2,1,0:T(8,128)(2,1)} %param.14) | copy-start | bytes 1769476
  3.3 16.9 %copy-start.11 = (bf16[4,4,576]{2,1,0:T(4,128)(2,1)S(1)}, bf16[4,4,576]{2,1,0:T(4,128)(2,1)}, u32[]{:S(2)}) copy-start(bf16[4,4,576]{2,1,0:T(4,128)(2,1)} %param.20) | copy-start | bytes 55300
  3.3 34.5 %all-to-all-start = ((bf16[32,104,128]{2,1,0:T(8,128)(2,1)}), bf16[32,104,128]{2,1,0:T(8,128)(2,1)S(1)}, u32[]{:S(2)}, u32[]{:S(2)}) async-start(bf16[32,104,128]{2,1,0:T(8,128)(2,1)} %shard_map.122), calls=%async_computation | async-start | bytes 1703936 | tf_op jit(solution)/shard_map/all_to_all | solution.py:352
  15.1 6.4 %copy-start.12 = (s32[8]{0:T(128)S(1)}, s32[8]{0:T(128)}, u32[]{:S(2)}) copy-start(s32[8]{0:T(128)} %lens.1) | copy-start | bytes 100
  15.1 7.8 %copy-start.2 = (bf16[8,128,576]{1,2,0:T(8,128)(2,1)S(1)}, bf16[8,128,576]{1,2,0:T(8,128)(2,1)}, u32[]{:S(2)}) copy-start(bf16[8,128,576]{1,2,0:T(8,128)(2,1)} %param.11) | copy-start | bytes 3538948
  16.1 10.7 %collective-permute-start.2 = (bf16[2,64,576]{2,1,0:T(8,128)(2,1)}, bf16[2,64,576]{2,1,0:T(8,128)(2,1)S(1)}, u32[]{:S(2)}, u32[]{:S(2)}) collective-permute-start(bf16[2,64,576]{2,1,0:T(8,128)(2,1)} %get-tuple-element.55), channel_id=1, source_target_pairs={{0,3},{1,2},{2,1},{3,0},{4,7},{5,6},{6,5},{7,4},{8,11},{9,10},{10,... | collective-permute-start | bytes 442376 | tf_op jit(solution)/shard_map/ppermute | solution.py:313
  19.1 8.8 %collective-permute-start.1 = (bf16[2,64,576]{2,1,0:T(8,128)(2,1)}, bf16[2,64,576]{2,1,0:T(8,128)(2,1)S(1)}, u32[]{:S(2)}, u32[]{:S(2)}) collective-permute-start(bf16[2,64,576]{2,1,0:T(8,128)(2,1)} %get-tuple-element.56), channel_id=1, source_target_pairs={{0,2},{1,3},{2,0},{3,1},{4,6},{5,7},{6,4},{7,5},{8,10},{9,11},{10,... | collective-permute-start | bytes 442376 | tf_op jit(solution)/shard_map/ppermute | solution.py:313
  19.7 8.2 %collective-permute-start = (bf16[2,64,576]{2,1,0:T(8,128)(2,1)}, bf16[2,64,576]{2,1,0:T(8,128)(2,1)S(1)}, u32[]{:S(2)}, u32[]{:S(2)}) collective-permute-start(bf16[2,64,576]{2,1,0:T(8,128)(2,1)} %get-tuple-element.57), channel_id=1, source_target_pairs={{0,1},{1,0},{2,3},{3,2},{4,5},{5,4},{6,7},{7,6},{8,9},{9,8},{10,11... | collective-permute-start | bytes 442376 | tf_op jit(solution)/shard_map/ppermute | solution.py:313
  22.9 51.4 %copy-start.5 = (s32[3]{0:T(128)}, s32[3]{0:T(128)S(1)}, u32[]{:S(2)}) copy-start(s32[3]{0:T(128)S(1)} %pad_add_fusion.info) | copy-start | bytes 40
  22.9 14.9 %copy-start.6 = (s32[32]{0:T(128)S(1)}, s32[32]{0:T(128)}, u32[]{:S(2)}) copy-start(s32[32]{0:T(128)} %partner.1) | copy-start | bytes 388
  26.8 33.2 %copy-start.8 = (bf16[2,64,576]{2,1,0:T(8,128)(2,1)}, bf16[2,64,576]{2,1,0:T(8,128)(2,1)S(1)}, u32[]{:S(2)}) copy-start(bf16[2,64,576]{2,1,0:T(8,128)(2,1)S(1)} %collective-permute-done.2.refs_3_) | copy-start | bytes 442372
  27.9 32.1 %copy-start.9 = (bf16[2,64,576]{2,1,0:T(8,128)(2,1)}, bf16[2,64,576]{2,1,0:T(8,128)(2,1)S(1)}, u32[]{:S(2)}) copy-start(bf16[2,64,576]{2,1,0:T(8,128)(2,1)S(1)} %collective-permute-done.1.refs_2_) | copy-start | bytes 442372
  28.0 22.1 %copy-start.10 = (bf16[2,64,576]{2,1,0:T(8,128)(2,1)}, bf16[2,64,576]{2,1,0:T(8,128)(2,1)S(1)}, u32[]{:S(2)}) copy-start(bf16[2,64,576]{2,1,0:T(8,128)(2,1)S(1)} %collective-permute-done.refs_1_) | copy-start | bytes 442372
  39.1 14.4 %collective-permute-start.3 = (bf16[16,80,128]{2,1,0:T(8,128)(2,1)S(1)}, bf16[16,80,128]{2,1,0:T(8,128)(2,1)S(1)}, u32[]{:S(2)}, u32[]{:S(2)}) collective-permute-start(bf16[16,80,128]{2,1,0:T(8,128)(2,1)S(1)} %get-tuple-element.36.refs_0_), channel_id=1, source_target_pairs={{0,3},{1,2},{2,1},{3,0},{4,7},{5,6},{6,5},{7,4},{8,11},{9,10},{10,... | collective-permute-start | bytes 983048 | tf_op jit(solution)/shard_map/ppermute | solution.py:369
  42.1 13.1 %collective-permute-start.5 = (bf16[16,80,128]{2,1,0:T(8,128)(2,1)S(1)}, bf16[16,80,128]{2,1,0:T(8,128)(2,1)S(1)}, u32[]{:S(2)}, u32[]{:S(2)}) collective-permute-start(bf16[16,80,128]{2,1,0:T(8,128)(2,1)S(1)} %get-tuple-element.37.refs_1_), channel_id=1, source_target_pairs={{0,1},{1,0},{2,3},{3,2},{4,5},{5,4},{6,7},{7,6},{8,9},{9,8},{10,11... | collective-permute-start | bytes 983048 | tf_op jit(solution)/shard_map/ppermute | solution.py:370
  42.3 10.8 %collective-permute-start.10 = (bf16[4,64,576]{2,1,0:T(8,128)(2,1)}, bf16[4,64,576]{2,1,0:T(8,128)(2,1)}, u32[]{:S(2)}, u32[]{:S(2)}) collective-permute-start(bf16[4,64,576]{2,1,0:T(8,128)(2,1)} %pad_maximum_fusion), channel_id=1, source_target_pairs={{0,4},{1,5},{2,6},{3,7},{4,0},{5,1},{6,2},{7,3},{8,12},{9,13},{10,... | collective-permute-start | bytes 884744 | tf_op jit(solution)/shard_map/ppermute | solution.py:366
  43.6 15.7 %all-to-all-start.1 = ((bf16[32,24,128]{2,1,0:T(8,128)(2,1)}), bf16[32,24,128]{2,1,0:T(8,128)(2,1)S(1)}, u32[]{:S(2)}, u32[]{:S(2)}) async-start(bf16[32,24,128]{2,1,0:T(8,128)(2,1)} %get-tuple-element.34), calls=%async_computation.1 | async-start | bytes 393216 | tf_op jit(solution)/shard_map/all_to_all | solution.py:371
  50.1 13.7 %collective-permute-start.7 = (bf16[16,80,128]{2,1,0:T(8,128)(2,1)S(1)}, bf16[16,80,128]{2,1,0:T(8,128)(2,1)S(1)}, u32[]{:S(2)}, u32[]{:S(2)}) collective-permute-start(bf16[16,80,128]{2,1,0:T(8,128)(2,1)S(1)} %get-tuple-element.36.refs_0_), channel_id=1, source_target_pairs={{0,1},{1,0},{2,3},{3,2},{4,5},{5,4},{6,7},{7,6},{8,9},{9,8},{10,11... | collective-permute-start | bytes 983048 | tf_op jit(solution)/shard_map/ppermute | solution.py:375
  52.0 11.8 %collective-permute-start.8 = (bf16[16,80,128]{2,1,0:T(8,128)(2,1)S(1)}, bf16[16,80,128]{2,1,0:T(8,128)(2,1)S(1)}, u32[]{:S(2)}, u32[]{:S(2)}) collective-permute-start(bf16[16,80,128]{2,1,0:T(8,128)(2,1)S(1)} %get-tuple-element.37.refs_1_), channel_id=1, source_target_pairs={{0,3},{1,2},{2,1},{3,0},{4,7},{5,6},{6,5},{7,4},{8,11},{9,10},{10,... | collective-permute-start | bytes 983048 | tf_op jit(solution)/shard_map/ppermute | solution.py:376
  53.1 10.7 %collective-permute-start.9 = (bf16[256,640]{1,0:T(8,128)(2,1)S(1)}, bf16[256,640]{1,0:T(8,128)(2,1)S(1)}, u32[]{:S(2)}, u32[]{:S(2)}) collective-permute-start(bf16[256,640]{1,0:T(8,128)(2,1)S(1)} %reshape.54.near), channel_id=1, source_target_pairs={{0,4},{1,5},{2,6},{3,7},{4,0},{5,1},{6,2},{7,3},{8,12},{9,13},{10,... | collective-permute-start | bytes 983048 | tf_op jit(solution)/shard_map/ppermute | solution.py:368
  53.6 13.6 %collective-permute-start.4 = (bf16[16,80,128]{2,1,0:T(8,128)(2,1)S(1)}, bf16[16,80,128]{2,1,0:T(8,128)(2,1)}, u32[]{:S(2)}, u32[]{:S(2)}) collective-permute-start(bf16[16,80,128]{2,1,0:T(8,128)(2,1)S(1)} %collective-permute-done.3.refs_4_), channel_id=1, source_target_pairs={{0,1},{1,0},{2,3},{3,2},{4,5},{5,4},{6,7},{7,6},{8,9},{9,8},{10,11... | collective-permute-start | bytes 983048 | tf_op jit(solution)/shard_map/ppermute | solution.py:373
  55.2 14.7 %collective-permute-start.6 = (bf16[16,80,128]{2,1,0:T(8,128)(2,1)S(1)}, bf16[16,80,128]{2,1,0:T(8,128)(2,1)}, u32[]{:S(2)}, u32[]{:S(2)}) collective-permute-start(bf16[16,80,128]{2,1,0:T(8,128)(2,1)S(1)} %collective-permute-done.5.refs_3_), channel_id=1, source_target_pairs={{0,3},{1,2},{2,1},{3,0},{4,7},{5,6},{6,5},{7,4},{8,11},{9,10},{10,... | collective-permute-start | bytes 983048 | tf_op jit(solution)/shard_map/ppermute | solution.py:374
  69.9 24.6 %all-to-all-start.2 = ((bf16[8,576,128]{2,1,0:T(8,128)(2,1)}), bf16[8,576,128]{2,1,0:T(8,128)(2,1)}, u32[]{:S(2)}, u32[]{:S(2)}) async-start(bf16[8,576,128]{2,1,0:T(8,128)(2,1)} %shard_map.125), calls=%async_computation.2 | async-start | bytes 2359296 | tf_op jit(solution)/shard_map/all_to_all | solution.py:378
  79.7 0.7 copy-start.3
  80.4 23.1 %copy-start.1 = (bf16[16,512,128]{2,1,0:T(8,128)(2,1)S(1)}, bf16[16,512,128]{2,1,0:T(8,128)(2,1)}, u32[]{:S(2)}) copy-start(bf16[16,512,128]{2,1,0:T(8,128)(2,1)} %value_up.1) | copy-start | bytes 6291460
  80.4 23.1 %copy-start.4 = (bf16[256,512]{1,0:T(8,128)(2,1)S(1)}, bf16[256,512]{1,0:T(8,128)(2,1)}, u32[]{:S(2)}) copy-start(bf16[256,512]{1,0:T(8,128)(2,1)} %copy-done.3) | copy-start | bytes 786436
  80.4 14.1 %collective-permute-start.11 = (bf16[272,512]{1,0:T(8,128)(2,1)S(1)}, bf16[272,512]{1,0:T(8,128)(2,1)S(1)}, u32[]{:S(2)}, u32[]{:S(2)}) collective-permute-start(bf16[272,512]{1,0:T(8,128)(2,1)S(1)} %get-tuple-element.48), channel_id=1, source_target_pairs={{0,4},{1,5},{2,6},{3,7},{4,0},{5,1},{6,2},{7,3},{8,12},{9,13},{10,... | collective-permute-start | bytes 835592 | tf_op jit(solution)/shard_map/ppermute | solution.py:381
  99.3 12.6 %all-to-all-start.3 = ((bf16[8,64,512]{2,1,0:T(8,128)(2,1)}), bf16[8,64,512]{2,1,0:T(8,128)(2,1)}, u32[]{:S(2)}, u32[]{:S(2)}) async-start(bf16[8,64,512]{2,1,0:T(8,128)(2,1)} %shard_map.127), calls=%async_computation.3 | async-start | bytes 1048576 | tf_op jit(solution)/shard_map/all_to_all | solution.py:384

commit v4 on v3

--- a/solution.py
+++ b/solution.py
@@ -1,3 +1,5 @@
+import functools
+
 import jax
 import jax.numpy as jnp
 from jax import lax
@@ -142,18 +144,21 @@
     )(partner, landed)
 
 
-def resident_kernel(info, *refs):
-    across = refs[:N_Y]
-    beyond, chunked, tail, tag, out, query, keys, weights, totals = refs[N_Y:]
+def resident_kernel(flip, info, *refs):
+    n = 1 if flip else N_Y
+    blocks, (chunked, tail, tag), rest = refs[:n], refs[n : n + 3], refs[n + 3 :]
+    if flip:
+        done, rest = rest[0], rest[1:]
+    out, query, keys, weights, totals = rest
     me, length = info[0], info[1]
-    side = me // N_Y
     chunks = chunked.shape[0]
-    rows = beyond.shape[1]
+    rows = out.shape[1]
     heads = rows // 4
     width = chunks * LANES
+    if flip:
+        out[...] = done[...]
     for d in range(N_Y):
-        query[d * rows : (d + 1) * rows, :] = across[d][side]
-        query[(N_Y + d) * rows : (N_Y + d + 1) * rows, :] = beyond[d]
+        query[d * rows : (d + 1) * rows, :] = blocks[0][d] if flip else blocks[d][me // N_Y]
     for c in range(chunks):
         keys[:, c * LANES : (c + 1) * LANES] = chunked[c]
     moved = tag[...].astype(F32)
@@ -161,7 +166,7 @@
     length = jnp.where(me == 0, moved, length)
     valid = lax.broadcasted_iota(jnp.int32, (1, width), 1) < length
     tile = 128
-    for part in range(N_HEAD * rows // tile):
+    for part in range(N_Y * rows // tile):
         span = slice(part * tile, (part + 1) * tile)
         q = query[span, :]
         main = jnp.dot(q, keys[...], preferred_element_type=F32)
@@ -180,19 +185,19 @@
         weights[span, width:] = last.astype(BF)
     acc = lax.dot_general(weights[:, :width], keys[:LATENT, :], NT, preferred_element_type=F32)
     acc = acc + jnp.dot(weights[:, width:], tail[:, :LATENT], preferred_element_type=F32)
-    for b in range(N_HEAD):
-        span = slice(b * rows, (b + 1) * rows)
-        out[me ^ b] = (acc[span] / totals[span, :1]).astype(BF)
-
-
-def resident(info, across, beyond, keys, tail, tag):
-    rows = beyond.shape[1]
-    count = N_HEAD * rows
+    for d in range(N_Y):
+        span = slice(d * rows, (d + 1) * rows)
+        out[me ^ (flip * N_Y + d)] = (acc[span] / totals[span, :1]).astype(BF)
+
+
+def resident(flip, info, blocks, keys, tail, tag, done=()):
+    rows = blocks[0].shape[1]
+    count = N_Y * rows
     width = keys.shape[0] * LANES
     shape = jax.ShapeDtypeStruct((N_HEAD, rows, LATENT), BF)
-    inputs = (*across, beyond, keys, tail, tag)
-    return pl.pallas_call(
-        resident_kernel,
+    inputs = (*blocks, keys, tail, tag, *done)
+    return pl.pallas_call(
+        functools.partial(resident_kernel, flip),
         out_shape=shape,
         in_specs=[smem()] + [whole(x) for x in inputs],
         out_specs=whole(shape),
@@ -207,8 +212,11 @@
     )(info, *inputs)
 
 
-def arrival_kernel(info, near, far, tail, *refs):
-    row_blocks, (out_near, stat_near, out_far, keys) = refs[:-4], refs[-4:]
+def arrival_kernel(send, info, query, tail, *refs):
+    if send:
+        row_blocks, (out, keys) = refs[:-2], refs[-2:]
+    else:
+        row_blocks, (out, stat_out, keys) = refs[:-3], refs[-3:]
     start = 0
     for r in row_blocks:
         count = r.shape[0] * CAP
@@ -218,56 +226,45 @@
             ].reshape(count, LANES)
         start = start + count
     use_tail = info[2]
-    rows = near.shape[0]
-    tile = 256
-    for source in range(2):
-        stats = []
-        for part in range(rows // tile):
-            q = (near, far)[source][part * tile : (part + 1) * tile, :]
-            main = lax.dot_general(q, keys[...], NT, preferred_element_type=F32) * SCALE
-            last = lax.dot_general(q, tail[...], NT, preferred_element_type=F32) * SCALE
-            tstep = lax.broadcasted_iota(jnp.int32, last.shape, 1) // 4
-            step = (lax.broadcasted_iota(jnp.int32, last.shape, 0) % 16) // 4
-            last = jnp.where(jnp.logical_and(tstep <= step, use_tail > 0), last, -BIG)
-            peak = jnp.maximum(jnp.max(main, -1, keepdims=True), jnp.max(last, -1, keepdims=True))
-            main = jnp.exp(main - peak)
-            last = jnp.exp(last - peak)
-            total = jnp.sum(main, -1, keepdims=True) + jnp.sum(last, -1, keepdims=True)
-            acc = jnp.dot(main.astype(BF), keys[:, :LATENT], preferred_element_type=F32)
-            acc = acc + jnp.dot(last.astype(BF), tail[:, :LATENT], preferred_element_type=F32)
-            value = (acc / total).astype(BF)
-            lse = peak + jnp.log(total)
-            stats.append(jnp.transpose(jnp.broadcast_to(lse, (tile, LANES))))
-            if source == 0:
-                out_near[part * tile : (part + 1) * tile, :] = value
-            else:
-                out_far[part * tile : (part + 1) * tile, :] = value
-        stat = jnp.concatenate(stats, 1)[:CAP]
-        if source == 0:
-            stat_near[...] = stat
-        else:
-            high = stat.astype(BF).astype(F32)
-            middle = (stat - high).astype(BF).astype(F32)
-            low = stat - high - middle
-            row = lax.broadcasted_iota(jnp.int32, stat.shape, 0)
-            split = jnp.where(row == 0, high, jnp.where(row == 1, middle, jnp.where(row == 2, low, 0.0)))
-            out_far[rows:, :rows] = split.astype(BF)
-            out_far[rows:, rows:] = jnp.zeros((CAP, LATENT - rows), BF)
-
-
-def arrival(info, near, far, rows, tail):
-    n = near.shape[0]
-    shapes = (
-        jax.ShapeDtypeStruct((n, LATENT), BF),
-        jax.ShapeDtypeStruct((CAP, n), F32),
-        jax.ShapeDtypeStruct((n + CAP, LATENT), BF),
-    )
-    inputs = (near, far, tail, *rows)
-    return pl.pallas_call(
-        arrival_kernel,
+    rows = query.shape[0]
+    q = query[...]
+    main = lax.dot_general(q, keys[...], NT, preferred_element_type=F32) * SCALE
+    last = lax.dot_general(q, tail[...], NT, preferred_element_type=F32) * SCALE
+    tstep = lax.broadcasted_iota(jnp.int32, last.shape, 1) // 4
+    step = (lax.broadcasted_iota(jnp.int32, last.shape, 0) % 16) // 4
+    last = jnp.where(jnp.logical_and(tstep <= step, use_tail > 0), last, -BIG)
+    peak = jnp.maximum(jnp.max(main, -1, keepdims=True), jnp.max(last, -1, keepdims=True))
+    main = jnp.exp(main - peak)
+    last = jnp.exp(last - peak)
+    total = jnp.sum(main, -1, keepdims=True) + jnp.sum(last, -1, keepdims=True)
+    acc = jnp.dot(main.astype(BF), keys[:, :LATENT], preferred_element_type=F32)
+    acc = acc + jnp.dot(last.astype(BF), tail[:, :LATENT], preferred_element_type=F32)
+    out[:rows, :] = (acc / total).astype(BF)
+    stat = jnp.transpose(jnp.broadcast_to(peak + jnp.log(total), (rows, LANES)))[:CAP]
+    if send:
+        high = stat.astype(BF).astype(F32)
+        middle = (stat - high).astype(BF).astype(F32)
+        low = stat - high - middle
+        row = lax.broadcasted_iota(jnp.int32, stat.shape, 0)
+        split = jnp.where(row == 0, high, jnp.where(row == 1, middle, jnp.where(row == 2, low, 0.0)))
+        out[rows:, :rows] = split.astype(BF)
+        out[rows:, rows:] = jnp.zeros((CAP, LATENT - rows), BF)
+    else:
+        stat_out[...] = stat
+
+
+def arrival(send, info, query, rows, tail):
+    n = query.shape[0]
+    if send:
+        shapes = jax.ShapeDtypeStruct((n + CAP, LATENT), BF)
+    else:
+        shapes = (jax.ShapeDtypeStruct((n, LATENT), BF), jax.ShapeDtypeStruct((CAP, n), F32))
+    inputs = (query, tail, *rows)
+    return pl.pallas_call(
+        functools.partial(arrival_kernel, send),
         out_shape=shapes,
         in_specs=[smem()] + [vmem()] * len(inputs),
-        out_specs=(vmem(),) * 3,
+        out_specs=vmem() if send else (vmem(),) * 2,
         scratch_shapes=[pltpu.VMEM((4 * N_INST * CAP, KX), BF)],
         compiler_params=params(),
     )(info, *inputs)
@@ -377,10 +374,13 @@
     full, f1, f3, low1, high3, far, beyond = lax.optimization_barrier((full, f1, f3, low1, high3, far, beyond))
     keys = lax.all_to_all(full, "head", split_axis=0, concat_axis=0, tiled=True)
     row_blocks = (low, high, low1, high1, low3, high3, f1, f3)
-    out_near, stat_near, out_far = arrival(info, near, far, row_blocks, new_tail)
+    out_far = arrival(True, info, far, row_blocks, new_tail)
     got = lax.ppermute(out_far, "head", xor_pairs(N_Y))
-    keys, got = lax.optimization_barrier((keys, got))
-    lat = resident(info, across, beyond, keys, tail, moved[PIECES])
+    out_near, stat_near = arrival(False, info, near, row_blocks, new_tail)
+    keys, out_near = lax.optimization_barrier((keys, out_near))
+    first = resident(0, info, across, keys, tail, moved[PIECES])
+    first, got = lax.optimization_barrier((first, got))
+    lat = resident(1, info, (beyond,), keys, tail, moved[PIECES], (first,))
     lat = lax.all_to_all(lat, "head", split_axis=0, concat_axis=0, tiled=True)
     lat = lat.reshape(count, steps, heads, LATENT)
     local_out = jnp.einsum("rshc,hcv->srhv", lat, value_up, preferred_element_type=F32)

time: 115 us -> 113 us (0.983)
  Pallas kernels: 18 us -> 25.7 us
  waiting for transfers between devices: 43.4 us -> 35.7 us
    ppermute x1, waiting for transfers between devices: 11.8 us -> 0.12 us  [local(): got = lax.ppermute(out_far, 'head', xor_pairs(N_Y))]
    pallas_call x2 -> x4, Pallas kernels: 10.1 us -> 16.8 us  [the longest x2 9.08 us: arrival(): pl.pallas_call(functools.partial(arrival_kernel, send), out_shape=shapes,...]
    all_to_all x1, waiting for transfers between devices: 0.01 us -> 4.87 us  [local(): keys = lax.all_to_all(full, 'head', split_axis=0, concat_axis=0, tiled=True)]
    ppermute x1, waiting for transfers between devices: 3.79 us -> 0.02 us  [local(): far = lax.ppermute(near, 'head', xor_pairs(N_Y))]
    ppermute x1, waiting for transfers between devices: 0.08 us -> 3.16 us  [local(): high3 = lax.ppermute(high, 'head', xor_pairs(3))]
  transfers between devices with their start and end apart: 16 -> 16, of which waited for: 11 -> 12; matrix products, arithmetic and copies ran while one was open for 6% -> 6% of each run, Pallas kernels for 8% -> 16%
where the time goes in v4:
time: 113 us; the launch traced here: 112 us
  starting transfers between devices  42.3 us (37%)
  waiting for transfers between devices  35.7 us (32%)
  Pallas kernels  25.7 us (23%)
  local copies, waits for them, and re-layouts  4.5 us (4%)
  other arithmetic  2.6 us (2%)
    all_to_all x1, starting transfers between devices, local(): lax.all_to_all(sent, 'inst', split_axis=0, concat_axis=0, tiled=True)  11.7 us
    pallas_call x2, Pallas kernels, arrival(): pl.pallas_call(functools.partial(arrival_kernel, send), out_shape=shapes,...  9.08 us
    all_to_all x1, waiting for transfers between devices, local(): lax.all_to_all(sent, 'inst', split_axis=0, concat_axis=0, tiled=True)  9.07 us
    pallas_call x2, Pallas kernels, resident(): pl.pallas_call(functools.partial(resident_kernel, flip), out_shape=shape,...  7.76 us
    all_to_all x1, starting transfers between devices, local(): lax.all_to_all(pieces, 'inst', split_axis=0, concat_axis=0, tiled=True)  6.41 us
    all_to_all x1, waiting for transfers between devices, local(): lat = lax.all_to_all(lat, 'head', split_axis=0, concat_axis=0, tiled=True)  6.13 us
    all_to_all x1, waiting for transfers between devices, local(): keys = lax.all_to_all(full, 'head', split_axis=0, concat_axis=0, tiled=True)  4.87 us
    all_to_all x1, starting transfers between devices, local(): keys = lax.all_to_all(full, 'head', split_axis=0, concat_axis=0, tiled=True)  4.25 us
  transfers between devices with their start and end apart: 16, of which 12 were waited for; matrix products, arithmetic and copies ran while one was open for 6% of the time, Pallas kernels for 16%

profile of v4, /device:TPU:6, one launch (start us, length us, event | category | flops | bytes accessed | tf_op | source)
XLA Modules:
  0.0 112.2 jit_solution(11791545195838666248)
XLA Ops:
  0.7 2.6 %shard_map.122 = bf16[32,104,128]{2,1,0:T(8,128)(2,1)} custom-call(s32[8]{0:T(128)} %lens.1, s32[1,256]{1,0:T(1,128)} %bitcast.52, s32[1,256]{1,0:T(1,128)} %bitcast.53, bf16[576,256]{1,0:T(8,128)(2,1)} %bitcast.49, bf16[8,576,128]{2,1,0:T(8,128)(2,1)} %bitcast.43), custom_call_target="tpu_custom_call" | custom-call | tf_op jit(solution)/shard_map/pallas_call | solution.py:83
  3.3 11.7 %all-to-all-start = ((bf16[32,104,128]{2,1,0:T(8,128)(2,1)}), bf16[32,104,128]{2,1,0:T(8,128)(2,1)S(1)}, u32[]{:S(2)}, u32[]{:S(2)}) async-start(bf16[32,104,128]{2,1,0:T(8,128)(2,1)} %shard_map.122), calls=%async_computation | async-start | bytes 1703936 | tf_op jit(solution)/shard_map/all_to_all | solution.py:349
  15.2 0.9 dynamic-slice_bitcast_fusion
  16.1 3.0 %collective-permute-start.2 = (bf16[2,64,576]{2,1,0:T(8,128)(2,1)}, bf16[2,64,576]{2,1,0:T(8,128)(2,1)S(1)}, u32[]{:S(2)}, u32[]{:S(2)}) collective-permute-start(bf16[2,64,576]{2,1,0:T(8,128)(2,1)} %get-tuple-element.57), channel_id=1, source_target_pairs={{0,3},{1,2},{2,1},{3,0},{4,7},{5,6},{6,5},{7,4},{8,11},{9,10},{10,... | collective-permute-start | bytes 442376 | tf_op jit(solution)/shard_map/ppermute | solution.py:310
  19.1 0.6 collective-permute-start.1
  19.7 0.5 collective-permute-start
  20.3 1.1 maximum_bitcast_fusion
  21.4 0.6 dynamic_slice.36
  22.0 0.6 pad_add_fusion.info
  22.7 2.7 %shard_map.123._ = bf16[8,576,128]{2,1,0:T(8,128)(2,1)} custom-call(bf16[8,576,128]{2,1,0:T(8,128)(2,1)S(1)} %bitcast.44), custom_call_target="tpu_custom_call" | custom-call | tf_op jit(solution)/shard_map/pallas_call | solution.py:99
  25.4 0.7 pad.5.refs_5_.refs_2_
  26.1 0.1 copy.16
  26.3 0.4 collective-permute-done.2.refs_3_
  26.8 1.1 collective-permute-done.1.refs_2_
  27.9 0.8 pad_maximum_fusion
  28.7 9.1 %all-to-all-done.landed = bf16[32,104,128]{2,1,0:T(8,128)(2,1)S(1)} async-done(((bf16[32,104,128]{2,1,0:T(8,128)(2,1)}), bf16[32,104,128]{2,1,0:T(8,128)(2,1)S(1)}, u32[]{:S(2)}, u32[]{:S(2)}) %all-to-all-start) | async-done | bytes 852000 | tf_op jit(solution)/shard_map/all_to_all | solution.py:349
  37.8 1.3 %shard_map.124 = (bf16[32,24,128]{2,1,0:T(8,128)(2,1)}, bf16[16,80,128]{2,1,0:T(8,128)(2,1)S(1)}, bf16[16,80,128]{2,1,0:T(8,128)(2,1)S(1)}) custom-call(s32[32]{0:T(128)S(1)} %copy-done.4, bf16[32,104,128]{2,1,0:T(8,128)(2,1)S(1)} %all-to-all-done.landed), custom_call_target="tpu_custom_call" | custom-call | tf_op jit(solution)/shard_map/pallas_call | solution.py:138
  39.1 3.0 %collective-permute-start.3 = (bf16[16,80,128]{2,1,0:T(8,128)(2,1)S(1)}, bf16[16,80,128]{2,1,0:T(8,128)(2,1)S(1)}, u32[]{:S(2)}, u32[]{:S(2)}) collective-permute-start(bf16[16,80,128]{2,1,0:T(8,128)(2,1)S(1)} %get-tuple-element.33.refs_0_), channel_id=1, source_target_pairs={{0,3},{1,2},{2,1},{3,0},{4,7},{5,6},{6,5},{7,4},{8,11},{9,10},{10,... | collective-permute-start | bytes 983048 | tf_op jit(solution)/shard_map/ppermute | solution.py:366
  42.1 0.1 collective-permute-start.5
  42.3 1.4 %collective-permute-start.10 = (bf16[4,64,576]{2,1,0:T(8,128)(2,1)}, bf16[4,64,576]{2,1,0:T(8,128)(2,1)}, u32[]{:S(2)}, u32[]{:S(2)}) collective-permute-start(bf16[4,64,576]{2,1,0:T(8,128)(2,1)} %pad_maximum_fusion), channel_id=1, source_target_pairs={{0,4},{1,5},{2,6},{3,7},{4,0},{5,1},{6,2},{7,3},{8,12},{9,13},{10,... | collective-permute-start | bytes 884744 | tf_op jit(solution)/shard_map/ppermute | solution.py:363
  43.7 6.4 %all-to-all-start.1 = ((bf16[32,24,128]{2,1,0:T(8,128)(2,1)}), bf16[32,24,128]{2,1,0:T(8,128)(2,1)S(1)}, u32[]{:S(2)}, u32[]{:S(2)}) async-start(bf16[32,24,128]{2,1,0:T(8,128)(2,1)} %get-tuple-element.31), calls=%async_computation.1 | async-start | bytes 393216 | tf_op jit(solution)/shard_map/all_to_all | solution.py:368
  50.1 2.0 %collective-permute-start.7 = (bf16[16,80,128]{2,1,0:T(8,128)(2,1)S(1)}, bf16[16,80,128]{2,1,0:T(8,128)(2,1)S(1)}, u32[]{:S(2)}, u32[]{:S(2)}) collective-permute-start(bf16[16,80,128]{2,1,0:T(8,128)(2,1)S(1)} %get-tuple-element.33.refs_0_), channel_id=1, source_target_pairs={{0,1},{1,0},{2,3},{3,2},{4,5},{5,4},{6,7},{7,6},{8,9},{9,8},{10,11... | collective-permute-start | bytes 983048 | tf_op jit(solution)/shard_map/ppermute | solution.py:372
  52.0 0.2 collective-permute-start.8
  52.2 0.9 collective-permute-done.10.refs_0_
  53.1 0.5 collective-permute-start.9
  53.6 1.7 %collective-permute-start.4 = (bf16[16,80,128]{2,1,0:T(8,128)(2,1)S(1)}, bf16[16,80,128]{2,1,0:T(8,128)(2,1)S(1)}, u32[]{:S(2)}, u32[]{:S(2)}) collective-permute-start(bf16[16,80,128]{2,1,0:T(8,128)(2,1)S(1)} %collective-permute-done.3.refs_4_), channel_id=1, source_target_pairs={{0,1},{1,0},{2,3},{3,2},{4,5},{5,4},{6,7},{7,6},{8,9},{9,8},{10,11... | collective-permute-start | bytes 983048 | tf_op jit(solution)/shard_map/ppermute | solution.py:370
  55.2 0.8 collective-permute-start.6
  56.1 3.3 %all-to-all-done.1 = bf16[32,24,128]{2,1,0:T(8,128)(2,1)S(1)} async-done(((bf16[32,24,128]{2,1,0:T(8,128)(2,1)}), bf16[32,24,128]{2,1,0:T(8,128)(2,1)S(1)}, u32[]{:S(2)}, u32[]{:S(2)}) %all-to-all-start.1) | async-done | bytes 196640 | tf_op jit(solution)/shard_map/all_to_all | solution.py:368
  59.3 0.7 shard_map.125
  60.0 0.7 collective-permute-done.7.refs_2_
  60.7 3.2 %collective-permute-done.8.refs_5_ = bf16[16,80,128]{2,1,0:T(8,128)(2,1)S(1)} collective-permute-done((bf16[16,80,128]{2,1,0:T(8,128)(2,1)S(1)}, bf16[16,80,128]{2,1,0:T(8,128)(2,1)S(1)}, u32[]{:S(2)}, u32[]{:S(2)}) %collective-permute-start.8) | collective-permute-done | bytes 327712 | tf_op jit(solution)/shard_map/ppermute | solution.py:373
  63.9 3.2 %collective-permute-done.4.refs_6_ = bf16[16,80,128]{2,1,0:T(8,128)(2,1)S(1)} collective-permute-done((bf16[16,80,128]{2,1,0:T(8,128)(2,1)S(1)}, bf16[16,80,128]{2,1,0:T(8,128)(2,1)S(1)}, u32[]{:S(2)}, u32[]{:S(2)}) %collective-permute-start.4) | collective-permute-done | bytes 327712 | tf_op jit(solution)/shard_map/ppermute | solution.py:370
  67.1 2.7 %collective-permute-done.6.refs_7_ = bf16[16,80,128]{2,1,0:T(8,128)(2,1)S(1)} collective-permute-done((bf16[16,80,128]{2,1,0:T(8,128)(2,1)S(1)}, bf16[16,80,128]{2,1,0:T(8,128)(2,1)S(1)}, u32[]{:S(2)}, u32[]{:S(2)}) %collective-permute-start.6) | collective-permute-done | bytes 327712 | tf_op jit(solution)/shard_map/ppermute | solution.py:371
  69.8 4.3 %all-to-all-start.2 = ((bf16[8,576,128]{2,1,0:T(8,128)(2,1)}), bf16[8,576,128]{2,1,0:T(8,128)(2,1)}, u32[]{:S(2)}, u32[]{:S(2)}) async-start(bf16[8,576,128]{2,1,0:T(8,128)(2,1)} %shard_map.125), calls=%async_computation.2 | async-start | bytes 2359296 | tf_op jit(solution)/shard_map/all_to_all | solution.py:375
  74.0 5.1 %shard_map.128 = bf16[272,512]{1,0:T(8,128)(2,1)} custom-call(s32[3]{0:T(128)S(1)} %pad_add_fusion.info, bf16[256,640]{1,0:T(8,128)(2,1)} %collective-permute-done.9.query, bf16[128,640]{1,0:T(8,128)(2,1)S(1)} %concatenate.10.tail, bf16[16,80,128]{2,1,0:T(8,128)(2,1)S(1)} %get-tuple-element.33.refs_0_, bf16[16,80,128]{2,1,0:T(8,128)(2,1)S(1)} %get-tuple-element.34.refs_1_, ...), custom_call_target="tpu_custom_call" | custom-call | tf_op jit(solution)/shard_map/pallas_call | solution.py:263
  79.1 1.9 %collective-permute-start.11 = (bf16[272,512]{1,0:T(8,128)(2,1)}, bf16[272,512]{1,0:T(8,128)(2,1)}, u32[]{:S(2)}, u32[]{:S(2)}) collective-permute-start(bf16[272,512]{1,0:T(8,128)(2,1)} %shard_map.128), channel_id=1, source_target_pairs={{0,4},{1,5},{2,6},{3,7},{4,0},{5,1},{6,2},{7,3},{8,12},{9,13},{10,... | collective-permute-start | bytes 835592 | tf_op jit(solution)/shard_map/ppermute | solution.py:378
  81.1 0.6 slice_bitcast_fusion.refs_6_.refs_3_
  81.7 4.0 %shard_map.126 = (bf16[256,512]{1,0:T(8,128)(2,1)S(1)}, f32[16,256]{1,0:T(8,128)S(1)}) custom-call(s32[3]{0:T(128)S(1)} %pad_add_fusion.info, bf16[256,640]{1,0:T(8,128)(2,1)S(1)} %reshape.54.query, bf16[128,640]{1,0:T(8,128)(2,1)S(1)} %concatenate.10.tail, bf16[16,80,128]{2,1,0:T(8,128)(2,1)S(1)} %get-tuple-element.33.refs_0_, ...), custom_call_target="tpu_custom_call" | custom-call | tf_op jit(solution)/shard_map/pallas_call | solution.py:263
  85.6 4.9 %all-to-all-done.2.refs_4_.refs_1_ = bf16[8,576,128]{2,1,0:T(8,128)(2,1)} async-done(((bf16[8,576,128]{2,1,0:T(8,128)(2,1)}), bf16[8,576,128]{2,1,0:T(8,128)(2,1)}, u32[]{:S(2)}, u32[]{:S(2)}) %all-to-all-start.2) | async-done | bytes 1179680 | tf_op jit(solution)/shard_map/all_to_all | solution.py:375
  90.5 3.9 %shard_map.127.refs_4_ = bf16[8,64,512]{2,1,0:T(8,128)(2,1)} custom-call(s32[3]{0:T(128)} %copy-done.3, bf16[2,64,576]{2,1,0:T(8,128)(2,1)} %get-tuple-element.47.refs_0_, bf16[2,64,576]{2,1,0:T(8,128)(2,1)} %copy-done.8, bf16[2,64,576]{2,1,0:T(8,128)(2,1)} %copy-done.7, bf16[2,64,576]{2,1,0:T(8,128)(2,1)} %copy-done.6, ...), custom_call_target="tpu_custom_call" | custom-call | tf_op jit(solution)/shard_map/pallas_call | solution.py:199
  94.4 0.1 collective-permute-done.11.far
  94.5 3.9 %shard_map.129 = bf16[8,64,512]{2,1,0:T(8,128)(2,1)} custom-call(s32[3]{0:T(128)} %copy-done.3, bf16[4,64,576]{2,1,0:T(8,128)(2,1)} %collective-permute-done.10.refs_0_, bf16[8,576,128]{2,1,0:T(8,128)(2,1)} %all-to-all-done.2.refs_4_.refs_1_, bf16[128,576]{1,0:T(8,128)(2,1)} %pad.5.refs_5_.refs_2_, bf16[24,128]{1,0:T(8,128)(2,1)} %slice_bitcast_fusion.refs_6_.refs_3_, ...), custom_call_target="tpu_custom_call" | custom-call | tf_op jit(solution)/shard_map/pallas_call | solution.py:199
  98.4 4.2 %all-to-all-start.3 = ((bf16[8,64,512]{2,1,0:T(8,128)(2,1)}), bf16[8,64,512]{2,1,0:T(8,128)(2,1)S(1)}, u32[]{:S(2)}, u32[]{:S(2)}) async-start(bf16[8,64,512]{2,1,0:T(8,128)(2,1)} %shard_map.129), calls=%async_computation.3 | async-start | bytes 1048576 | tf_op jit(solution)/shard_map/all_to_all | solution.py:384
  102.6 1.5 %shard_map.130 = bf16[16,2048]{1,0:T(8,128)(2,1)S(1)} custom-call(bf16[256,512]{1,0:T(8,128)(2,1)S(1)} %get-tuple-element.53.near, f32[16,256]{1,0:T(8,128)S(1)} %get-tuple-element.54.stat_near, bf16[272,512]{1,0:T(8,128)(2,1)} %collective-permute-done.11.far, bf16[16,512,128]{2,1,0:T(8,128)(2,1)S(1)} %copy-done.1), custom_call_target="tpu_custom_call" | custom-call | tf_op jit(solution)/shard_map/pallas_call | solution.py:292
  104.1 0.7 reshape.58
  104.8 6.1 %all-to-all-done.3 = bf16[8,64,512]{2,1,0:T(8,128)(2,1)S(1)} async-done(((bf16[8,64,512]{2,1,0:T(8,128)(2,1)}), bf16[8,64,512]{2,1,0:T(8,128)(2,1)S(1)}, u32[]{:S(2)}, u32[]{:S(2)}) %all-to-all-start.3) | async-done | bytes 524320 | tf_op jit(solution)/shard_map/all_to_all | solution.py:384
  110.9 0.5 fusion.5
  111.5 0.7 copy.27
  (41 shorter events, 0.5 us)
Async XLA Ops:
  0.6 20.7 %copy-start = (bf16[4,8,576]{2,1,0:T(8,128)(2,1)S(1)}, bf16[4,8,576]{2,1,0:T(8,128)(2,1)}, u32[]{:S(2)}) copy-start(bf16[4,8,576]{2,1,0:T(8,128)(2,1)} %param.15) | copy-start | bytes 110596
  0.6 14.5 %copy-start.5 = (bf16[4,8,16,576]{3,2,1,0:T(8,128)(2,1)S(1)}, bf16[4,8,16,576]{3,2,1,0:T(8,128)(2,1)}, u32[]{:S(2)}) copy-start(bf16[4,8,16,576]{3,2,1,0:T(8,128)(2,1)} %param.14) | copy-start | bytes 1769476
  3.3 16.9 %copy-start.9 = (bf16[4,4,576]{2,1,0:T(4,128)(2,1)S(1)}, bf16[4,4,576]{2,1,0:T(4,128)(2,1)}, u32[]{:S(2)}) copy-start(bf16[4,4,576]{2,1,0:T(4,128)(2,1)} %param.20) | copy-start | bytes 55300
  3.3 34.5 %all-to-all-start = ((bf16[32,104,128]{2,1,0:T(8,128)(2,1)}), bf16[32,104,128]{2,1,0:T(8,128)(2,1)S(1)}, u32[]{:S(2)}, u32[]{:S(2)}) async-start(bf16[32,104,128]{2,1,0:T(8,128)(2,1)} %shard_map.122), calls=%async_computation | async-start | bytes 1703936 | tf_op jit(solution)/shard_map/all_to_all | solution.py:349
  15.0 6.4 %copy-start.10 = (s32[8]{0:T(128)S(1)}, s32[8]{0:T(128)}, u32[]{:S(2)}) copy-start(s32[8]{0:T(128)} %lens.1) | copy-start | bytes 100
  15.1 7.6 %copy-start.2 = (bf16[8,128,576]{1,2,0:T(8,128)(2,1)S(1)}, bf16[8,128,576]{1,2,0:T(8,128)(2,1)}, u32[]{:S(2)}) copy-start(bf16[8,128,576]{1,2,0:T(8,128)(2,1)} %param.11) | copy-start | bytes 3538948
  16.1 10.7 %collective-permute-start.2 = (bf16[2,64,576]{2,1,0:T(8,128)(2,1)}, bf16[2,64,576]{2,1,0:T(8,128)(2,1)S(1)}, u32[]{:S(2)}, u32[]{:S(2)}) collective-permute-start(bf16[2,64,576]{2,1,0:T(8,128)(2,1)} %get-tuple-element.57), channel_id=1, source_target_pairs={{0,3},{1,2},{2,1},{3,0},{4,7},{5,6},{6,5},{7,4},{8,11},{9,10},{10,... | collective-permute-start | bytes 442376 | tf_op jit(solution)/shard_map/ppermute | solution.py:310
  19.1 8.8 %collective-permute-start.1 = (bf16[2,64,576]{2,1,0:T(8,128)(2,1)}, bf16[2,64,576]{2,1,0:T(8,128)(2,1)S(1)}, u32[]{:S(2)}, u32[]{:S(2)}) collective-permute-start(bf16[2,64,576]{2,1,0:T(8,128)(2,1)} %get-tuple-element.58), channel_id=1, source_target_pairs={{0,2},{1,3},{2,0},{3,1},{4,6},{5,7},{6,4},{7,5},{8,10},{9,11},{10,... | collective-permute-start | bytes 442376 | tf_op jit(solution)/shard_map/ppermute | solution.py:310
  19.7 8.2 %collective-permute-start = (bf16[2,64,576]{2,1,0:T(8,128)(2,1)}, bf16[2,64,576]{2,1,0:T(8,128)(2,1)S(1)}, u32[]{:S(2)}, u32[]{:S(2)}) collective-permute-start(bf16[2,64,576]{2,1,0:T(8,128)(2,1)} %get-tuple-element.59), channel_id=1, source_target_pairs={{0,1},{1,0},{2,3},{3,2},{4,5},{5,4},{6,7},{7,6},{8,9},{9,8},{10,11... | collective-permute-start | bytes 442376 | tf_op jit(solution)/shard_map/ppermute | solution.py:310
  22.7 59.0 %copy-start.3 = (s32[3]{0:T(128)}, s32[3]{0:T(128)S(1)}, u32[]{:S(2)}) copy-start(s32[3]{0:T(128)S(1)} %pad_add_fusion.info) | copy-start | bytes 40
  22.7 15.2 %copy-start.4 = (s32[32]{0:T(128)S(1)}, s32[32]{0:T(128)}, u32[]{:S(2)}) copy-start(s32[32]{0:T(128)} %partner.1) | copy-start | bytes 388
  26.7 26.8 %copy-start.6 = (bf16[2,64,576]{2,1,0:T(8,128)(2,1)}, bf16[2,64,576]{2,1,0:T(8,128)(2,1)S(1)}, u32[]{:S(2)}) copy-start(bf16[2,64,576]{2,1,0:T(8,128)(2,1)S(1)} %collective-permute-done.2.refs_3_) | copy-start | bytes 442372
  27.9 27.3 %copy-start.7 = (bf16[2,64,576]{2,1,0:T(8,128)(2,1)}, bf16[2,64,576]{2,1,0:T(8,128)(2,1)S(1)}, u32[]{:S(2)}) copy-start(bf16[2,64,576]{2,1,0:T(8,128)(2,1)S(1)} %collective-permute-done.1.refs_2_) | copy-start | bytes 442372
  27.9 15.7 %copy-start.8 = (bf16[2,64,576]{2,1,0:T(8,128)(2,1)}, bf16[2,64,576]{2,1,0:T(8,128)(2,1)S(1)}, u32[]{:S(2)}) copy-start(bf16[2,64,576]{2,1,0:T(8,128)(2,1)S(1)} %collective-permute-done.refs_1_) | copy-start | bytes 442372
  39.1 14.4 %collective-permute-start.3 = (bf16[16,80,128]{2,1,0:T(8,128)(2,1)S(1)}, bf16[16,80,128]{2,1,0:T(8,128)(2,1)S(1)}, u32[]{:S(2)}, u32[]{:S(2)}) collective-permute-start(bf16[16,80,128]{2,1,0:T(8,128)(2,1)S(1)} %get-tuple-element.33.refs_0_), channel_id=1, source_target_pairs={{0,3},{1,2},{2,1},{3,0},{4,7},{5,6},{6,5},{7,4},{8,11},{9,10},{10,... | collective-permute-start | bytes 983048 | tf_op jit(solution)/shard_map/ppermute | solution.py:366
  42.1 13.1 %collective-permute-start.5 = (bf16[16,80,128]{2,1,0:T(8,128)(2,1)S(1)}, bf16[16,80,128]{2,1,0:T(8,128)(2,1)S(1)}, u32[]{:S(2)}, u32[]{:S(2)}) collective-permute-start(bf16[16,80,128]{2,1,0:T(8,128)(2,1)S(1)} %get-tuple-element.34.refs_1_), channel_id=1, source_target_pairs={{0,1},{1,0},{2,3},{3,2},{4,5},{5,4},{6,7},{7,6},{8,9},{9,8},{10,11... | collective-permute-start | bytes 983048 | tf_op jit(solution)/shard_map/ppermute | solution.py:367
  42.3 10.8 %collective-permute-start.10 = (bf16[4,64,576]{2,1,0:T(8,128)(2,1)}, bf16[4,64,576]{2,1,0:T(8,128)(2,1)}, u32[]{:S(2)}, u32[]{:S(2)}) collective-permute-start(bf16[4,64,576]{2,1,0:T(8,128)(2,1)} %pad_maximum_fusion), channel_id=1, source_target_pairs={{0,4},{1,5},{2,6},{3,7},{4,0},{5,1},{6,2},{7,3},{8,12},{9,13},{10,... | collective-permute-start | bytes 884744 | tf_op jit(solution)/shard_map/ppermute | solution.py:363
  43.7 15.7 %all-to-all-start.1 = ((bf16[32,24,128]{2,1,0:T(8,128)(2,1)}), bf16[32,24,128]{2,1,0:T(8,128)(2,1)S(1)}, u32[]{:S(2)}, u32[]{:S(2)}) async-start(bf16[32,24,128]{2,1,0:T(8,128)(2,1)} %get-tuple-element.31), calls=%async_computation.1 | async-start | bytes 393216 | tf_op jit(solution)/shard_map/all_to_all | solution.py:368
  50.1 10.6 %collective-permute-start.7 = (bf16[16,80,128]{2,1,0:T(8,128)(2,1)S(1)}, bf16[16,80,128]{2,1,0:T(8,128)(2,1)S(1)}, u32[]{:S(2)}, u32[]{:S(2)}) collective-permute-start(bf16[16,80,128]{2,1,0:T(8,128)(2,1)S(1)} %get-tuple-element.33.refs_0_), channel_id=1, source_target_pairs={{0,1},{1,0},{2,3},{3,2},{4,5},{5,4},{6,7},{7,6},{8,9},{9,8},{10,11... | collective-permute-start | bytes 983048 | tf_op jit(solution)/shard_map/ppermute | solution.py:372
  52.0 11.8 %collective-permute-start.8 = (bf16[16,80,128]{2,1,0:T(8,128)(2,1)S(1)}, bf16[16,80,128]{2,1,0:T(8,128)(2,1)S(1)}, u32[]{:S(2)}, u32[]{:S(2)}) collective-permute-start(bf16[16,80,128]{2,1,0:T(8,128)(2,1)S(1)} %get-tuple-element.34.refs_1_), channel_id=1, source_target_pairs={{0,3},{1,2},{2,1},{3,0},{4,7},{5,6},{6,5},{7,4},{8,11},{9,10},{10,... | collective-permute-start | bytes 983048 | tf_op jit(solution)/shard_map/ppermute | solution.py:373
  53.1 10.8 %collective-permute-start.9 = (bf16[256,640]{1,0:T(8,128)(2,1)S(1)}, bf16[256,640]{1,0:T(8,128)(2,1)}, u32[]{:S(2)}, u32[]{:S(2)}) collective-permute-start(bf16[256,640]{1,0:T(8,128)(2,1)S(1)} %reshape.54.query), channel_id=1, source_target_pairs={{0,4},{1,5},{2,6},{3,7},{4,0},{5,1},{6,2},{7,3},{8,12},{9,13},{10,... | collective-permute-start | bytes 983048 | tf_op jit(solution)/shard_map/ppermute | solution.py:365
  53.6 13.5 %collective-permute-start.4 = (bf16[16,80,128]{2,1,0:T(8,128)(2,1)S(1)}, bf16[16,80,128]{2,1,0:T(8,128)(2,1)S(1)}, u32[]{:S(2)}, u32[]{:S(2)}) collective-permute-start(bf16[16,80,128]{2,1,0:T(8,128)(2,1)S(1)} %collective-permute-done.3.refs_4_), channel_id=1, source_target_pairs={{0,1},{1,0},{2,3},{3,2},{4,5},{5,4},{6,7},{7,6},{8,9},{9,8},{10,11... | collective-permute-start | bytes 983048 | tf_op jit(solution)/shard_map/ppermute | solution.py:370
  55.2 14.6 %collective-permute-start.6 = (bf16[16,80,128]{2,1,0:T(8,128)(2,1)S(1)}, bf16[16,80,128]{2,1,0:T(8,128)(2,1)S(1)}, u32[]{:S(2)}, u32[]{:S(2)}) collective-permute-start(bf16[16,80,128]{2,1,0:T(8,128)(2,1)S(1)} %collective-permute-done.5.refs_3_), channel_id=1, source_target_pairs={{0,3},{1,2},{2,1},{3,0},{4,7},{5,6},{6,5},{7,4},{8,11},{9,10},{10,... | collective-permute-start | bytes 983048 | tf_op jit(solution)/shard_map/ppermute | solution.py:371
  69.8 20.7 %all-to-all-start.2 = ((bf16[8,576,128]{2,1,0:T(8,128)(2,1)}), bf16[8,576,128]{2,1,0:T(8,128)(2,1)}, u32[]{:S(2)}, u32[]{:S(2)}) async-start(bf16[8,576,128]{2,1,0:T(8,128)(2,1)} %shard_map.125), calls=%async_computation.2 | async-start | bytes 2359296 | tf_op jit(solution)/shard_map/all_to_all | solution.py:375
  79.1 15.3 %collective-permute-start.11 = (bf16[272,512]{1,0:T(8,128)(2,1)}, bf16[272,512]{1,0:T(8,128)(2,1)}, u32[]{:S(2)}, u32[]{:S(2)}) collective-permute-start(bf16[272,512]{1,0:T(8,128)(2,1)} %shard_map.128), channel_id=1, source_target_pairs={{0,4},{1,5},{2,6},{3,7},{4,0},{5,1},{6,2},{7,3},{8,12},{9,13},{10,... | collective-permute-start | bytes 835592 | tf_op jit(solution)/shard_map/ppermute | solution.py:378
  94.4 8.3 %copy-start.1 = (bf16[16,512,128]{2,1,0:T(8,128)(2,1)S(1)}, bf16[16,512,128]{2,1,0:T(8,128)(2,1)}, u32[]{:S(2)}) copy-start(bf16[16,512,128]{2,1,0:T(8,128)(2,1)} %value_up.1) | copy-start | bytes 6291460
  98.4 12.6 %all-to-all-start.3 = ((bf16[8,64,512]{2,1,0:T(8,128)(2,1)}), bf16[8,64,512]{2,1,0:T(8,128)(2,1)S(1)}, u32[]{:S(2)}, u32[]{:S(2)}) async-start(bf16[8,64,512]{2,1,0:T(8,128)(2,1)} %shard_map.129), calls=%async_computation.3 | async-start | bytes 1048576 | tf_op jit(solution)/shard_map/all_to_all | solution.py:384

commit v5 on v4

--- a/solution.py
+++ b/solution.py
@@ -227,20 +227,25 @@
         start = start + count
     use_tail = info[2]
     rows = query.shape[0]
-    q = query[...]
-    main = lax.dot_general(q, keys[...], NT, preferred_element_type=F32) * SCALE
-    last = lax.dot_general(q, tail[...], NT, preferred_element_type=F32) * SCALE
-    tstep = lax.broadcasted_iota(jnp.int32, last.shape, 1) // 4
-    step = (lax.broadcasted_iota(jnp.int32, last.shape, 0) % 16) // 4
-    last = jnp.where(jnp.logical_and(tstep <= step, use_tail > 0), last, -BIG)
-    peak = jnp.maximum(jnp.max(main, -1, keepdims=True), jnp.max(last, -1, keepdims=True))
-    main = jnp.exp(main - peak)
-    last = jnp.exp(last - peak)
-    total = jnp.sum(main, -1, keepdims=True) + jnp.sum(last, -1, keepdims=True)
-    acc = jnp.dot(main.astype(BF), keys[:, :LATENT], preferred_element_type=F32)
-    acc = acc + jnp.dot(last.astype(BF), tail[:, :LATENT], preferred_element_type=F32)
-    out[:rows, :] = (acc / total).astype(BF)
-    stat = jnp.transpose(jnp.broadcast_to(peak + jnp.log(total), (rows, LANES)))[:CAP]
+    tile = 128
+    stats = []
+    for part in range(rows // tile):
+        span = slice(part * tile, (part + 1) * tile)
+        q = query[span, :]
+        main = lax.dot_general(q, keys[...], NT, preferred_element_type=F32) * SCALE
+        last = lax.dot_general(q, tail[...], NT, preferred_element_type=F32) * SCALE
+        tstep = lax.broadcasted_iota(jnp.int32, last.shape, 1) // 4
+        step = (lax.broadcasted_iota(jnp.int32, last.shape, 0) % 16) // 4
+        last = jnp.where(jnp.logical_and(tstep <= step, use_tail > 0), last, -BIG)
+        peak = jnp.maximum(jnp.max(main, -1, keepdims=True), jnp.max(last, -1, keepdims=True))
+        main = jnp.exp(main - peak)
+        last = jnp.exp(last - peak)
+        total = jnp.sum(main, -1, keepdims=True) + jnp.sum(last, -1, keepdims=True)
+        acc = jnp.dot(main.astype(BF), keys[:, :LATENT], preferred_element_type=F32)
+        acc = acc + jnp.dot(last.astype(BF), tail[:, :LATENT], preferred_element_type=F32)
+        out[span, :] = (acc / total).astype(BF)
+        stats.append(jnp.transpose(jnp.broadcast_to(peak + jnp.log(total), (tile, LANES)))[:CAP])
+    stat = jnp.concatenate(stats, 1)
     if send:
         high = stat.astype(BF).astype(F32)
         middle = (stat - high).astype(BF).astype(F32)

time: 113 us -> 113 us (level)
  no operation moved by 1% of the time
where the time goes in v5:
time: 113 us; the launch traced here: 112 us
  starting transfers between devices  42.3 us (37%)
  waiting for transfers between devices  36.1 us (32%)
  Pallas kernels  25.3 us (22%)
  local copies, waits for them, and re-layouts  4.5 us (4%)
  other arithmetic  2.6 us (2%)
    all_to_all x1, starting transfers between devices, local(): lax.all_to_all(sent, 'inst', split_axis=0, concat_axis=0, tiled=True)  11.7 us
    all_to_all x1, waiting for transfers between devices, local(): lax.all_to_all(sent, 'inst', split_axis=0, concat_axis=0, tiled=True)  9.07 us
    pallas_call x2, Pallas kernels, arrival(): pl.pallas_call(functools.partial(arrival_kernel, send), out_shape=shapes,...  8.68 us
    pallas_call x2, Pallas kernels, resident(): pl.pallas_call(functools.partial(resident_kernel, flip), out_shape=shape,...  7.76 us
    all_to_all x1, starting transfers between devices, local(): lax.all_to_all(pieces, 'inst', split_axis=0, concat_axis=0, tiled=True)  6.41 us
    all_to_all x1, waiting for transfers between devices, local(): lat = lax.all_to_all(lat, 'head', split_axis=0, concat_axis=0, tiled=True)  6.12 us
    all_to_all x1, waiting for transfers between devices, local(): keys = lax.all_to_all(full, 'head', split_axis=0, concat_axis=0, tiled=True)  5.28 us
    all_to_all x1, starting transfers between devices, local(): keys = lax.all_to_all(full, 'head', split_axis=0, concat_axis=0, tiled=True)  4.25 us
  transfers between devices with their start and end apart: 16, of which 12 were waited for; matrix products, arithmetic and copies ran while one was open for 6% of the time, Pallas kernels for 16%

profile of v5, /device:TPU:6, one launch (start us, length us, event | category | flops | bytes accessed | tf_op | source)
XLA Modules:
  0.0 112.2 jit_solution(9993480424347488806)
XLA Ops:
  0.7 2.6 %shard_map.122 = bf16[32,104,128]{2,1,0:T(8,128)(2,1)} custom-call(s32[8]{0:T(128)} %lens.1, s32[1,256]{1,0:T(1,128)} %bitcast.52, s32[1,256]{1,0:T(1,128)} %bitcast.53, bf16[576,256]{1,0:T(8,128)(2,1)} %bitcast.49, bf16[8,576,128]{2,1,0:T(8,128)(2,1)} %bitcast.43), custom_call_target="tpu_custom_call" | custom-call | tf_op jit(solution)/shard_map/pallas_call | solution.py:83
  3.3 11.7 %all-to-all-start = ((bf16[32,104,128]{2,1,0:T(8,128)(2,1)}), bf16[32,104,128]{2,1,0:T(8,128)(2,1)S(1)}, u32[]{:S(2)}, u32[]{:S(2)}) async-start(bf16[32,104,128]{2,1,0:T(8,128)(2,1)} %shard_map.122), calls=%async_computation | async-start | bytes 1703936 | tf_op jit(solution)/shard_map/all_to_all | solution.py:354
  15.2 0.9 dynamic-slice_bitcast_fusion
  16.1 3.0 %collective-permute-start.2 = (bf16[2,64,576]{2,1,0:T(8,128)(2,1)}, bf16[2,64,576]{2,1,0:T(8,128)(2,1)S(1)}, u32[]{:S(2)}, u32[]{:S(2)}) collective-permute-start(bf16[2,64,576]{2,1,0:T(8,128)(2,1)} %get-tuple-element.57), channel_id=1, source_target_pairs={{0,3},{1,2},{2,1},{3,0},{4,7},{5,6},{6,5},{7,4},{8,11},{9,10},{10,... | collective-permute-start | bytes 442376 | tf_op jit(solution)/shard_map/ppermute | solution.py:315
  19.1 0.6 collective-permute-start.1
  19.7 0.5 collective-permute-start
  20.3 1.1 maximum_bitcast_fusion
  21.4 0.6 dynamic_slice.36
  22.0 0.6 pad_add_fusion.info
  22.7 2.7 %shard_map.123._ = bf16[8,576,128]{2,1,0:T(8,128)(2,1)} custom-call(bf16[8,576,128]{2,1,0:T(8,128)(2,1)S(1)} %bitcast.44), custom_call_target="tpu_custom_call" | custom-call | tf_op jit(solution)/shard_map/pallas_call | solution.py:99
  25.4 0.7 pad.5.refs_5_.refs_2_
  26.1 0.1 copy.16
  26.3 0.4 collective-permute-done.2.refs_3_
  26.8 1.1 collective-permute-done.1.refs_2_
  27.9 0.8 pad_maximum_fusion
  28.7 9.1 %all-to-all-done.landed = bf16[32,104,128]{2,1,0:T(8,128)(2,1)S(1)} async-done(((bf16[32,104,128]{2,1,0:T(8,128)(2,1)}), bf16[32,104,128]{2,1,0:T(8,128)(2,1)S(1)}, u32[]{:S(2)}, u32[]{:S(2)}) %all-to-all-start) | async-done | bytes 852000 | tf_op jit(solution)/shard_map/all_to_all | solution.py:354
  37.8 1.3 %shard_map.124 = (bf16[32,24,128]{2,1,0:T(8,128)(2,1)}, bf16[16,80,128]{2,1,0:T(8,128)(2,1)S(1)}, bf16[16,80,128]{2,1,0:T(8,128)(2,1)S(1)}) custom-call(s32[32]{0:T(128)S(1)} %copy-done.4, bf16[32,104,128]{2,1,0:T(8,128)(2,1)S(1)} %all-to-all-done.landed), custom_call_target="tpu_custom_call" | custom-call | tf_op jit(solution)/shard_map/pallas_call | solution.py:138
  39.1 3.0 %collective-permute-start.3 = (bf16[16,80,128]{2,1,0:T(8,128)(2,1)S(1)}, bf16[16,80,128]{2,1,0:T(8,128)(2,1)S(1)}, u32[]{:S(2)}, u32[]{:S(2)}) collective-permute-start(bf16[16,80,128]{2,1,0:T(8,128)(2,1)S(1)} %get-tuple-element.33.refs_0_), channel_id=1, source_target_pairs={{0,3},{1,2},{2,1},{3,0},{4,7},{5,6},{6,5},{7,4},{8,11},{9,10},{10,... | collective-permute-start | bytes 983048 | tf_op jit(solution)/shard_map/ppermute | solution.py:371
  42.1 0.1 collective-permute-start.5
  42.3 1.4 %collective-permute-start.10 = (bf16[4,64,576]{2,1,0:T(8,128)(2,1)}, bf16[4,64,576]{2,1,0:T(8,128)(2,1)}, u32[]{:S(2)}, u32[]{:S(2)}) collective-permute-start(bf16[4,64,576]{2,1,0:T(8,128)(2,1)} %pad_maximum_fusion), channel_id=1, source_target_pairs={{0,4},{1,5},{2,6},{3,7},{4,0},{5,1},{6,2},{7,3},{8,12},{9,13},{10,... | collective-permute-start | bytes 884744 | tf_op jit(solution)/shard_map/ppermute | solution.py:368
  43.6 6.4 %all-to-all-start.1 = ((bf16[32,24,128]{2,1,0:T(8,128)(2,1)}), bf16[32,24,128]{2,1,0:T(8,128)(2,1)S(1)}, u32[]{:S(2)}, u32[]{:S(2)}) async-start(bf16[32,24,128]{2,1,0:T(8,128)(2,1)} %get-tuple-element.31), calls=%async_computation.1 | async-start | bytes 393216 | tf_op jit(solution)/shard_map/all_to_all | solution.py:373
  50.1 2.0 %collective-permute-start.7 = (bf16[16,80,128]{2,1,0:T(8,128)(2,1)S(1)}, bf16[16,80,128]{2,1,0:T(8,128)(2,1)S(1)}, u32[]{:S(2)}, u32[]{:S(2)}) collective-permute-start(bf16[16,80,128]{2,1,0:T(8,128)(2,1)S(1)} %get-tuple-element.33.refs_0_), channel_id=1, source_target_pairs={{0,1},{1,0},{2,3},{3,2},{4,5},{5,4},{6,7},{7,6},{8,9},{9,8},{10,11... | collective-permute-start | bytes 983048 | tf_op jit(solution)/shard_map/ppermute | solution.py:377
  52.0 0.2 collective-permute-start.8
  52.2 0.9 collective-permute-done.10.refs_0_
  53.1 0.5 collective-permute-start.9
  53.5 1.7 %collective-permute-start.4 = (bf16[16,80,128]{2,1,0:T(8,128)(2,1)S(1)}, bf16[16,80,128]{2,1,0:T(8,128)(2,1)S(1)}, u32[]{:S(2)}, u32[]{:S(2)}) collective-permute-start(bf16[16,80,128]{2,1,0:T(8,128)(2,1)S(1)} %collective-permute-done.3.refs_4_), channel_id=1, source_target_pairs={{0,1},{1,0},{2,3},{3,2},{4,5},{5,4},{6,7},{7,6},{8,9},{9,8},{10,11... | collective-permute-start | bytes 983048 | tf_op jit(solution)/shard_map/ppermute | solution.py:375
  55.2 0.8 collective-permute-start.6
  56.1 3.3 %all-to-all-done.1 = bf16[32,24,128]{2,1,0:T(8,128)(2,1)S(1)} async-done(((bf16[32,24,128]{2,1,0:T(8,128)(2,1)}), bf16[32,24,128]{2,1,0:T(8,128)(2,1)S(1)}, u32[]{:S(2)}, u32[]{:S(2)}) %all-to-all-start.1) | async-done | bytes 196640 | tf_op jit(solution)/shard_map/all_to_all | solution.py:373
  59.3 0.7 shard_map.125
  60.0 0.7 collective-permute-done.7.refs_2_
  60.7 3.2 %collective-permute-done.8.refs_5_ = bf16[16,80,128]{2,1,0:T(8,128)(2,1)S(1)} collective-permute-done((bf16[16,80,128]{2,1,0:T(8,128)(2,1)S(1)}, bf16[16,80,128]{2,1,0:T(8,128)(2,1)S(1)}, u32[]{:S(2)}, u32[]{:S(2)}) %collective-permute-start.8) | collective-permute-done | bytes 327712 | tf_op jit(solution)/shard_map/ppermute | solution.py:378
  63.9 3.2 %collective-permute-done.4.refs_6_ = bf16[16,80,128]{2,1,0:T(8,128)(2,1)S(1)} collective-permute-done((bf16[16,80,128]{2,1,0:T(8,128)(2,1)S(1)}, bf16[16,80,128]{2,1,0:T(8,128)(2,1)S(1)}, u32[]{:S(2)}, u32[]{:S(2)}) %collective-permute-start.4) | collective-permute-done | bytes 327712 | tf_op jit(solution)/shard_map/ppermute | solution.py:375
  67.1 2.7 %collective-permute-done.6.refs_7_ = bf16[16,80,128]{2,1,0:T(8,128)(2,1)S(1)} collective-permute-done((bf16[16,80,128]{2,1,0:T(8,128)(2,1)S(1)}, bf16[16,80,128]{2,1,0:T(8,128)(2,1)S(1)}, u32[]{:S(2)}, u32[]{:S(2)}) %collective-permute-start.6) | collective-permute-done | bytes 327712 | tf_op jit(solution)/shard_map/ppermute | solution.py:376
  69.8 4.3 %all-to-all-start.2 = ((bf16[8,576,128]{2,1,0:T(8,128)(2,1)}), bf16[8,576,128]{2,1,0:T(8,128)(2,1)}, u32[]{:S(2)}, u32[]{:S(2)}) async-start(bf16[8,576,128]{2,1,0:T(8,128)(2,1)} %shard_map.125), calls=%async_computation.2 | async-start | bytes 2359296 | tf_op jit(solution)/shard_map/all_to_all | solution.py:380
  74.0 4.9 %shard_map.128 = bf16[272,512]{1,0:T(8,128)(2,1)} custom-call(s32[3]{0:T(128)S(1)} %pad_add_fusion.info, bf16[256,640]{1,0:T(8,128)(2,1)} %collective-permute-done.9.query, bf16[128,640]{1,0:T(8,128)(2,1)S(1)} %concatenate.10.tail, bf16[16,80,128]{2,1,0:T(8,128)(2,1)S(1)} %get-tuple-element.33.refs_0_, bf16[16,80,128]{2,1,0:T(8,128)(2,1)S(1)} %get-tuple-element.34.refs_1_, ...), custom_call_target="tpu_custom_call" | custom-call | tf_op jit(solution)/shard_map/pallas_call | solution.py:268
  78.9 1.9 %collective-permute-start.11 = (bf16[272,512]{1,0:T(8,128)(2,1)}, bf16[272,512]{1,0:T(8,128)(2,1)}, u32[]{:S(2)}, u32[]{:S(2)}) collective-permute-start(bf16[272,512]{1,0:T(8,128)(2,1)} %shard_map.128), channel_id=1, source_target_pairs={{0,4},{1,5},{2,6},{3,7},{4,0},{5,1},{6,2},{7,3},{8,12},{9,13},{10,... | collective-permute-start | bytes 835592 | tf_op jit(solution)/shard_map/ppermute | solution.py:383
  80.8 0.6 slice_bitcast_fusion.refs_6_.refs_3_
  81.4 3.8 %shard_map.126 = (bf16[256,512]{1,0:T(8,128)(2,1)S(1)}, f32[16,256]{1,0:T(8,128)S(1)}) custom-call(s32[3]{0:T(128)S(1)} %pad_add_fusion.info, bf16[256,640]{1,0:T(8,128)(2,1)S(1)} %reshape.54.query, bf16[128,640]{1,0:T(8,128)(2,1)S(1)} %concatenate.10.tail, bf16[16,80,128]{2,1,0:T(8,128)(2,1)S(1)} %get-tuple-element.33.refs_0_, ...), custom_call_target="tpu_custom_call" | custom-call | tf_op jit(solution)/shard_map/pallas_call | solution.py:268
  85.2 5.3 %all-to-all-done.2.refs_4_.refs_1_ = bf16[8,576,128]{2,1,0:T(8,128)(2,1)} async-done(((bf16[8,576,128]{2,1,0:T(8,128)(2,1)}), bf16[8,576,128]{2,1,0:T(8,128)(2,1)}, u32[]{:S(2)}, u32[]{:S(2)}) %all-to-all-start.2) | async-done | bytes 1179680 | tf_op jit(solution)/shard_map/all_to_all | solution.py:380
  90.5 3.9 %shard_map.127.refs_4_ = bf16[8,64,512]{2,1,0:T(8,128)(2,1)} custom-call(s32[3]{0:T(128)} %copy-done.3, bf16[2,64,576]{2,1,0:T(8,128)(2,1)} %get-tuple-element.47.refs_0_, bf16[2,64,576]{2,1,0:T(8,128)(2,1)} %copy-done.8, bf16[2,64,576]{2,1,0:T(8,128)(2,1)} %copy-done.7, bf16[2,64,576]{2,1,0:T(8,128)(2,1)} %copy-done.6, ...), custom_call_target="tpu_custom_call" | custom-call | tf_op jit(solution)/shard_map/pallas_call | solution.py:199
  94.3 0.1 collective-permute-done.11.far
  94.5 3.9 %shard_map.129 = bf16[8,64,512]{2,1,0:T(8,128)(2,1)} custom-call(s32[3]{0:T(128)} %copy-done.3, bf16[4,64,576]{2,1,0:T(8,128)(2,1)} %collective-permute-done.10.refs_0_, bf16[8,576,128]{2,1,0:T(8,128)(2,1)} %all-to-all-done.2.refs_4_.refs_1_, bf16[128,576]{1,0:T(8,128)(2,1)} %pad.5.refs_5_.refs_2_, bf16[24,128]{1,0:T(8,128)(2,1)} %slice_bitcast_fusion.refs_6_.refs_3_, ...), custom_call_target="tpu_custom_call" | custom-call | tf_op jit(solution)/shard_map/pallas_call | solution.py:199
  98.4 4.2 %all-to-all-start.3 = ((bf16[8,64,512]{2,1,0:T(8,128)(2,1)}), bf16[8,64,512]{2,1,0:T(8,128)(2,1)S(1)}, u32[]{:S(2)}, u32[]{:S(2)}) async-start(bf16[8,64,512]{2,1,0:T(8,128)(2,1)} %shard_map.129), calls=%async_computation.3 | async-start | bytes 1048576 | tf_op jit(solution)/shard_map/all_to_all | solution.py:389
  102.6 1.5 %shard_map.130 = bf16[16,2048]{1,0:T(8,128)(2,1)S(1)} custom-call(bf16[256,512]{1,0:T(8,128)(2,1)S(1)} %get-tuple-element.53.near, f32[16,256]{1,0:T(8,128)S(1)} %get-tuple-element.54.stat_near, bf16[272,512]{1,0:T(8,128)(2,1)} %collective-permute-done.11.far, bf16[16,512,128]{2,1,0:T(8,128)(2,1)S(1)} %copy-done.1), custom_call_target="tpu_custom_call" | custom-call | tf_op jit(solution)/shard_map/pallas_call | solution.py:297
  104.1 0.7 reshape.58
  104.8 6.1 %all-to-all-done.3 = bf16[8,64,512]{2,1,0:T(8,128)(2,1)S(1)} async-done(((bf16[8,64,512]{2,1,0:T(8,128)(2,1)}), bf16[8,64,512]{2,1,0:T(8,128)(2,1)S(1)}, u32[]{:S(2)}, u32[]{:S(2)}) %all-to-all-start.3) | async-done | bytes 524320 | tf_op jit(solution)/shard_map/all_to_all | solution.py:389
  110.9 0.5 fusion.5
  111.5 0.7 copy.27
  (41 shorter events, 0.5 us)
Async XLA Ops:
  0.6 20.7 %copy-start = (bf16[4,8,576]{2,1,0:T(8,128)(2,1)S(1)}, bf16[4,8,576]{2,1,0:T(8,128)(2,1)}, u32[]{:S(2)}) copy-start(bf16[4,8,576]{2,1,0:T(8,128)(2,1)} %param.15) | copy-start | bytes 110596
  0.6 14.5 %copy-start.5 = (bf16[4,8,16,576]{3,2,1,0:T(8,128)(2,1)S(1)}, bf16[4,8,16,576]{3,2,1,0:T(8,128)(2,1)}, u32[]{:S(2)}) copy-start(bf16[4,8,16,576]{3,2,1,0:T(8,128)(2,1)} %param.14) | copy-start | bytes 1769476
  3.3 16.9 %copy-start.9 = (bf16[4,4,576]{2,1,0:T(4,128)(2,1)S(1)}, bf16[4,4,576]{2,1,0:T(4,128)(2,1)}, u32[]{:S(2)}) copy-start(bf16[4,4,576]{2,1,0:T(4,128)(2,1)} %param.20) | copy-start | bytes 55300
  3.3 34.5 %all-to-all-start = ((bf16[32,104,128]{2,1,0:T(8,128)(2,1)}), bf16[32,104,128]{2,1,0:T(8,128)(2,1)S(1)}, u32[]{:S(2)}, u32[]{:S(2)}) async-start(bf16[32,104,128]{2,1,0:T(8,128)(2,1)} %shard_map.122), calls=%async_computation | async-start | bytes 1703936 | tf_op jit(solution)/shard_map/all_to_all | solution.py:354
  15.0 6.4 %copy-start.10 = (s32[8]{0:T(128)S(1)}, s32[8]{0:T(128)}, u32[]{:S(2)}) copy-start(s32[8]{0:T(128)} %lens.1) | copy-start | bytes 100
  15.1 7.6 %copy-start.2 = (bf16[8,128,576]{1,2,0:T(8,128)(2,1)S(1)}, bf16[8,128,576]{1,2,0:T(8,128)(2,1)}, u32[]{:S(2)}) copy-start(bf16[8,128,576]{1,2,0:T(8,128)(2,1)} %param.11) | copy-start | bytes 3538948
  16.1 10.7 %collective-permute-start.2 = (bf16[2,64,576]{2,1,0:T(8,128)(2,1)}, bf16[2,64,576]{2,1,0:T(8,128)(2,1)S(1)}, u32[]{:S(2)}, u32[]{:S(2)}) collective-permute-start(bf16[2,64,576]{2,1,0:T(8,128)(2,1)} %get-tuple-element.57), channel_id=1, source_target_pairs={{0,3},{1,2},{2,1},{3,0},{4,7},{5,6},{6,5},{7,4},{8,11},{9,10},{10,... | collective-permute-start | bytes 442376 | tf_op jit(solution)/shard_map/ppermute | solution.py:315
  19.1 8.8 %collective-permute-start.1 = (bf16[2,64,576]{2,1,0:T(8,128)(2,1)}, bf16[2,64,576]{2,1,0:T(8,128)(2,1)S(1)}, u32[]{:S(2)}, u32[]{:S(2)}) collective-permute-start(bf16[2,64,576]{2,1,0:T(8,128)(2,1)} %get-tuple-element.58), channel_id=1, source_target_pairs={{0,2},{1,3},{2,0},{3,1},{4,6},{5,7},{6,4},{7,5},{8,10},{9,11},{10,... | collective-permute-start | bytes 442376 | tf_op jit(solution)/shard_map/ppermute | solution.py:315
  19.7 8.2 %collective-permute-start = (bf16[2,64,576]{2,1,0:T(8,128)(2,1)}, bf16[2,64,576]{2,1,0:T(8,128)(2,1)S(1)}, u32[]{:S(2)}, u32[]{:S(2)}) collective-permute-start(bf16[2,64,576]{2,1,0:T(8,128)(2,1)} %get-tuple-element.59), channel_id=1, source_target_pairs={{0,1},{1,0},{2,3},{3,2},{4,5},{5,4},{6,7},{7,6},{8,9},{9,8},{10,11... | collective-permute-start | bytes 442376 | tf_op jit(solution)/shard_map/ppermute | solution.py:315
  22.7 58.8 %copy-start.3 = (s32[3]{0:T(128)}, s32[3]{0:T(128)S(1)}, u32[]{:S(2)}) copy-start(s32[3]{0:T(128)S(1)} %pad_add_fusion.info) | copy-start | bytes 40
  22.7 15.2 %copy-start.4 = (s32[32]{0:T(128)S(1)}, s32[32]{0:T(128)}, u32[]{:S(2)}) copy-start(s32[32]{0:T(128)} %partner.1) | copy-start | bytes 388
  26.7 26.8 %copy-start.6 = (bf16[2,64,576]{2,1,0:T(8,128)(2,1)}, bf16[2,64,576]{2,1,0:T(8,128)(2,1)S(1)}, u32[]{:S(2)}) copy-start(bf16[2,64,576]{2,1,0:T(8,128)(2,1)S(1)} %collective-permute-done.2.refs_3_) | copy-start | bytes 442372
  27.9 27.3 %copy-start.7 = (bf16[2,64,576]{2,1,0:T(8,128)(2,1)}, bf16[2,64,576]{2,1,0:T(8,128)(2,1)S(1)}, u32[]{:S(2)}) copy-start(bf16[2,64,576]{2,1,0:T(8,128)(2,1)S(1)} %collective-permute-done.1.refs_2_) | copy-start | bytes 442372
  27.9 15.7 %copy-start.8 = (bf16[2,64,576]{2,1,0:T(8,128)(2,1)}, bf16[2,64,576]{2,1,0:T(8,128)(2,1)S(1)}, u32[]{:S(2)}) copy-start(bf16[2,64,576]{2,1,0:T(8,128)(2,1)S(1)} %collective-permute-done.refs_1_) | copy-start | bytes 442372
  39.1 14.4 %collective-permute-start.3 = (bf16[16,80,128]{2,1,0:T(8,128)(2,1)S(1)}, bf16[16,80,128]{2,1,0:T(8,128)(2,1)S(1)}, u32[]{:S(2)}, u32[]{:S(2)}) collective-permute-start(bf16[16,80,128]{2,1,0:T(8,128)(2,1)S(1)} %get-tuple-element.33.refs_0_), channel_id=1, source_target_pairs={{0,3},{1,2},{2,1},{3,0},{4,7},{5,6},{6,5},{7,4},{8,11},{9,10},{10,... | collective-permute-start | bytes 983048 | tf_op jit(solution)/shard_map/ppermute | solution.py:371
  42.1 13.1 %collective-permute-start.5 = (bf16[16,80,128]{2,1,0:T(8,128)(2,1)S(1)}, bf16[16,80,128]{2,1,0:T(8,128)(2,1)S(1)}, u32[]{:S(2)}, u32[]{:S(2)}) collective-permute-start(bf16[16,80,128]{2,1,0:T(8,128)(2,1)S(1)} %get-tuple-element.34.refs_1_), channel_id=1, source_target_pairs={{0,1},{1,0},{2,3},{3,2},{4,5},{5,4},{6,7},{7,6},{8,9},{9,8},{10,11... | collective-permute-start | bytes 983048 | tf_op jit(solution)/shard_map/ppermute | solution.py:372
  42.3 10.8 %collective-permute-start.10 = (bf16[4,64,576]{2,1,0:T(8,128)(2,1)}, bf16[4,64,576]{2,1,0:T(8,128)(2,1)}, u32[]{:S(2)}, u32[]{:S(2)}) collective-permute-start(bf16[4,64,576]{2,1,0:T(8,128)(2,1)} %pad_maximum_fusion), channel_id=1, source_target_pairs={{0,4},{1,5},{2,6},{3,7},{4,0},{5,1},{6,2},{7,3},{8,12},{9,13},{10,... | collective-permute-start | bytes 884744 | tf_op jit(solution)/shard_map/ppermute | solution.py:368
  43.6 15.7 %all-to-all-start.1 = ((bf16[32,24,128]{2,1,0:T(8,128)(2,1)}), bf16[32,24,128]{2,1,0:T(8,128)(2,1)S(1)}, u32[]{:S(2)}, u32[]{:S(2)}) async-start(bf16[32,24,128]{2,1,0:T(8,128)(2,1)} %get-tuple-element.31), calls=%async_computation.1 | async-start | bytes 393216 | tf_op jit(solution)/shard_map/all_to_all | solution.py:373
  50.1 10.6 %collective-permute-start.7 = (bf16[16,80,128]{2,1,0:T(8,128)(2,1)S(1)}, bf16[16,80,128]{2,1,0:T(8,128)(2,1)S(1)}, u32[]{:S(2)}, u32[]{:S(2)}) collective-permute-start(bf16[16,80,128]{2,1,0:T(8,128)(2,1)S(1)} %get-tuple-element.33.refs_0_), channel_id=1, source_target_pairs={{0,1},{1,0},{2,3},{3,2},{4,5},{5,4},{6,7},{7,6},{8,9},{9,8},{10,11... | collective-permute-start | bytes 983048 | tf_op jit(solution)/shard_map/ppermute | solution.py:377
  52.0 11.8 %collective-permute-start.8 = (bf16[16,80,128]{2,1,0:T(8,128)(2,1)S(1)}, bf16[16,80,128]{2,1,0:T(8,128)(2,1)S(1)}, u32[]{:S(2)}, u32[]{:S(2)}) collective-permute-start(bf16[16,80,128]{2,1,0:T(8,128)(2,1)S(1)} %get-tuple-element.34.refs_1_), channel_id=1, source_target_pairs={{0,3},{1,2},{2,1},{3,0},{4,7},{5,6},{6,5},{7,4},{8,11},{9,10},{10,... | collective-permute-start | bytes 983048 | tf_op jit(solution)/shard_map/ppermute | solution.py:378
  53.1 10.8 %collective-permute-start.9 = (bf16[256,640]{1,0:T(8,128)(2,1)S(1)}, bf16[256,640]{1,0:T(8,128)(2,1)}, u32[]{:S(2)}, u32[]{:S(2)}) collective-permute-start(bf16[256,640]{1,0:T(8,128)(2,1)S(1)} %reshape.54.query), channel_id=1, source_target_pairs={{0,4},{1,5},{2,6},{3,7},{4,0},{5,1},{6,2},{7,3},{8,12},{9,13},{10,... | collective-permute-start | bytes 983048 | tf_op jit(solution)/shard_map/ppermute | solution.py:370
  53.5 13.5 %collective-permute-start.4 = (bf16[16,80,128]{2,1,0:T(8,128)(2,1)S(1)}, bf16[16,80,128]{2,1,0:T(8,128)(2,1)S(1)}, u32[]{:S(2)}, u32[]{:S(2)}) collective-permute-start(bf16[16,80,128]{2,1,0:T(8,128)(2,1)S(1)} %collective-permute-done.3.refs_4_), channel_id=1, source_target_pairs={{0,1},{1,0},{2,3},{3,2},{4,5},{5,4},{6,7},{7,6},{8,9},{9,8},{10,11... | collective-permute-start | bytes 983048 | tf_op jit(solution)/shard_map/ppermute | solution.py:375
  55.2 14.6 %collective-permute-start.6 = (bf16[16,80,128]{2,1,0:T(8,128)(2,1)S(1)}, bf16[16,80,128]{2,1,0:T(8,128)(2,1)S(1)}, u32[]{:S(2)}, u32[]{:S(2)}) collective-permute-start(bf16[16,80,128]{2,1,0:T(8,128)(2,1)S(1)} %collective-permute-done.5.refs_3_), channel_id=1, source_target_pairs={{0,3},{1,2},{2,1},{3,0},{4,7},{5,6},{6,5},{7,4},{8,11},{9,10},{10,... | collective-permute-start | bytes 983048 | tf_op jit(solution)/shard_map/ppermute | solution.py:376
  69.8 20.7 %all-to-all-start.2 = ((bf16[8,576,128]{2,1,0:T(8,128)(2,1)}), bf16[8,576,128]{2,1,0:T(8,128)(2,1)}, u32[]{:S(2)}, u32[]{:S(2)}) async-start(bf16[8,576,128]{2,1,0:T(8,128)(2,1)} %shard_map.125), calls=%async_computation.2 | async-start | bytes 2359296 | tf_op jit(solution)/shard_map/all_to_all | solution.py:380
  78.9 15.5 %collective-permute-start.11 = (bf16[272,512]{1,0:T(8,128)(2,1)}, bf16[272,512]{1,0:T(8,128)(2,1)}, u32[]{:S(2)}, u32[]{:S(2)}) collective-permute-start(bf16[272,512]{1,0:T(8,128)(2,1)} %shard_map.128), channel_id=1, source_target_pairs={{0,4},{1,5},{2,6},{3,7},{4,0},{5,1},{6,2},{7,3},{8,12},{9,13},{10,... | collective-permute-start | bytes 835592 | tf_op jit(solution)/shard_map/ppermute | solution.py:383
  94.3 8.3 %copy-start.1 = (bf16[16,512,128]{2,1,0:T(8,128)(2,1)S(1)}, bf16[16,512,128]{2,1,0:T(8,128)(2,1)}, u32[]{:S(2)}) copy-start(bf16[16,512,128]{2,1,0:T(8,128)(2,1)} %value_up.1) | copy-start | bytes 6291460
  98.4 12.6 %all-to-all-start.3 = ((bf16[8,64,512]{2,1,0:T(8,128)(2,1)}), bf16[8,64,512]{2,1,0:T(8,128)(2,1)S(1)}, u32[]{:S(2)}, u32[]{:S(2)}) async-start(bf16[8,64,512]{2,1,0:T(8,128)(2,1)} %shard_map.129), calls=%async_computation.3 | async-start | bytes 1048576 | tf_op jit(solution)/shard_map/all_to_all | solution.py:389
